TPU v7x, 128 devices: a whole 4x4x4 slice. The times are simulated.
128 devices in a mesh: tm: 16 (over x, z_hi, core), row: 8 (over y, z_lo).
Axes of the slice: x: 4, y: 4, z: 4 (z_hi: 2, z_lo: 2; z = z_hi * 2 + z_lo), core: 2. Of those that a mesh axis runs over, the one named last changes fastest.
Arguments:
- stream: float32 [64, 512, 3072], P('tm', 'row'), may hold values from -6 to 6
- clip_ids: int32 [64], replicated, may hold values from 0 to 7, never falling along the last dimension, each value on 1 to 16 neighbouring positions
- modulation: float32 [8, 3, 3072], replicated, may hold values from -2 to 3, as said below
- qkv_weight: bfloat16 [3072, 3, 2048], P(None, None, 'row'), may hold values from -3 to 3
- out_weight: bfloat16 [2048, 3072], replicated, may hold values from -0.125 to 0.125
Outputs:
- update: float32 [64, 512, 3072], P('tm', 'row')
Inputs may be any that keep to these rules, and one draw needn't show every extreme that they name: clip_ids never falls along the frames; each clip holds 1 to 16 consecutive frames. `modulation`: 1 + scale and the gate are positive.
All inputs are finite; a program needn't handle non-finite values.
Results may differ from a plain program's by a relative error of at most 0.0095.
Values may be sent and summed in bfloat16 or wider, within the bound.
A program may use at most 192 MiB of HBM per device.

v0:
```python
import math

import jax
import jax.numpy as jnp
from jax import lax
from jax.sharding import PartitionSpec as P

HD = 128
CLIP_MOST = 16


def shifted(array, axis, by):
    length = lax.axis_size(axis)
    pairs = [(i, i + by) for i in range(length) if 0 <= i + by < length]
    return lax.ppermute(array, axis, pairs)


def layer_norm(activation):
    average = jnp.mean(activation, axis=-1, keepdims=True)
    centred = activation - average
    variance = jnp.mean(centred * centred, axis=-1, keepdims=True)
    return centred * lax.rsqrt(variance + 1e-06)


def per_device(stream, clip_ids, modulation, qkv_weight, out_weight):
    frames, spat_dev, model_width = stream.shape
    heads_dev = qkv_weight.shape[2] // HD
    clips_total = modulation.shape[0]
    tm_index = lax.axis_index("tm")
    own_clip = lax.dynamic_slice_in_dim(clip_ids, tm_index * frames, frames)
    onehot = (own_clip[:, None] == jnp.arange(clips_total, dtype=jnp.int32)[None, :]).astype(
        jnp.float32
    )
    per_frame = jnp.dot(
        onehot, modulation.reshape(clips_total, 3 * model_width), precision=lax.Precision.HIGHEST
    )
    per_frame = per_frame.reshape(frames, 3, model_width)
    normed = layer_norm(stream) * (1.0 + per_frame[:, 1][:, None, :]) + per_frame[:, 0][:, None, :]
    normed = normed.astype(jnp.bfloat16)
    flat_weight = qkv_weight.reshape(model_width, -1)
    projected = jnp.dot(
        lax.all_gather(normed, "row", axis=1, tiled=True),
        flat_weight,
        preferred_element_type=jnp.float32,
    ).astype(jnp.bfloat16)
    spatial = projected.shape[1]
    projected = projected.reshape(frames, spatial, 3, heads_dev, HD)
    queries = projected[:, :, 0]
    key_block = projected[:, :, 1]
    values = projected[:, :, 2]
    scores = jnp.einsum(
        "fshd,fthd->fhst", queries, key_block, preferred_element_type=jnp.float32
    ) / math.sqrt(HD)
    row_max = jnp.max(scores, axis=-1, keepdims=True)
    weights = jnp.exp(scores - row_max)
    spatial_out = jnp.einsum(
        "fhst,fthd->fshd", weights.astype(jnp.bfloat16), values, preferred_element_type=jnp.float32
    )
    spatial_out = spatial_out / jnp.transpose(jnp.sum(weights, axis=-1), (0, 2, 1))[..., None]
    key_values = projected[:, :, 1:]
    reach = (CLIP_MOST + frames - 2) // frames
    earlier_pieces = []
    later_pieces = []
    for distance in range(1, reach + 1):
        earlier_pieces.append(shifted(key_values, "tm", distance))
        later_pieces.append(shifted(key_values, "tm", -distance))
    padded = jnp.concatenate(earlier_pieces[::-1] + [key_values] + later_pieces, axis=0)
    rim_rows = reach * frames
    padded_clip = jnp.pad(clip_ids, rim_rows, constant_values=-1)
    near_clip = lax.dynamic_slice_in_dim(padded_clip, tm_index * frames, frames * (2 * reach + 1))
    match = (own_clip[:, None] == near_clip[None, :])[None, None]
    scores = jnp.einsum(
        "fshd,gshd->shfg", queries, padded[:, :, 0], preferred_element_type=jnp.float32
    ) / math.sqrt(HD)
    scores = jnp.where(match, scores, -1e30)
    row_max = jnp.max(scores, axis=-1, keepdims=True)
    weights = jnp.where(match, jnp.exp(scores - row_max), 0.0)
    running = jnp.einsum(
        "shfg,gshd->shfd",
        weights.astype(jnp.bfloat16),
        padded[:, :, 1],
        preferred_element_type=jnp.float32,
    )
    temporal_out = jnp.transpose(running / jnp.sum(weights, axis=-1)[..., None], (2, 0, 1, 3))
    combined = (
        (spatial_out + temporal_out).astype(jnp.bfloat16).reshape(frames, spatial, heads_dev * HD)
    )
    gate_term = per_frame[:, 2][:, None, :]
    regrouped = lax.all_to_all(combined, "row", split_axis=1, concat_axis=2, tiled=True)
    update = jnp.dot(
        regrouped.reshape(frames * spat_dev, -1), out_weight, preferred_element_type=jnp.float32
    )
    update = update.reshape(frames, spat_dev, model_width)
    return update * gate_term


def solution(mesh):
    placed = (P("tm", "row", None), P(), P(), P(None, None, "row"), P())
    return jax.shard_map(
        per_device, mesh=mesh, in_specs=placed, out_specs=P("tm", "row", None), check_vma=False
    )
```

profile of v0, /device:TPU:32, one launch (start us, length us, event | category | flops | bytes accessed | tf_op | source)
XLA Modules:
  0.0 652.4 jit_solution(10306211373728055768)
XLA Ops:
  6.5 0.9 dynamic_slice.6
  7.4 0.1 copy-done
  7.5 0.3 fusion.24
  7.9 2.1 reduce_sum.36
  10.0 0.5 multiply_reduce_fusion.1
  10.5 1.8 add_convert_fusion
  12.3 0.0 all-gather.2.cloned.1.call-update
  12.3 6.6 %copy.25 = bf16[3072,3,256]{0,2,1:T(8,128)(2,1)} copy(bf16[3072,3,256]{2,0,1:T(8,128)(2,1)} %param.8) | data formatting | bytes 9437184 | tf_op args[3]
  19.0 241.3 %all-gather.2.cloned.1.call-done = bf16[4,512,3072]{2,1,0:T(8,128)(2,1)} async-done(((bf16[4,64,3072]{2,1,0:T(8,128)(2,1)}), bf16[4,512,3072]{2,1,0:T(8,128)(2,1)}) %all-gather.2.cloned.1.call-update) | async-done | bytes 12582928 | tf_op jit(solution)/shard_map/all_gather | solution.py:42
  260.3 15.5 %convolution_convert_fusion = bf16[4,512,768]{2,1,0:T(8,128)(2,1)} fusion(bf16[4,512,3072]{2,1,0:T(8,128)(2,1)} %all-gather.2.cloned.1.call-done, bf16[3072,768,1]{0,1,2:T(8,128)(2,1)} %bitcast.70), kind=kOutput, calls=%fused_computation.17 | convolution fusion | flops 9665249280 | bytes 20447232 | tf_op jit(solution)/shard_map/dot_general | solution.py:41
  275.8 5.7 reshape.63
  281.5 1.4 slice.41
  282.9 0.0 copy-start.8
  282.9 4.0 copy.44
  287.0 4.9 collective-permute-start
  291.8 5.0 collective-permute-start.1
  296.8 3.9 collective-permute-start.2
  300.6 0.1 pad_dynamic-slice_fusion
  300.7 2.6 collective-permute-start.3
  303.3 1.3 collective-permute-start.4
  304.6 32.2 %collective-permute-done = bf16[4,512,2,2,128]{4,0,3,1,2:T(4,128)(2,1)} collective-permute-done((bf16[4,512,2,2,128]{4,0,3,1,2:T(4,128)(2,1)}, bf16[4,512,2,2,128]{4,0,3,1,2:T(4,128)(2,1)}, u32[]{:S(2)}, u32[]{:S(2)}) %collective-permute-start) | collective-permute-done | bytes 2097184 | tf_op jit(solution)/shard_map/ppermute | solution.py:15
  336.9 1.3 collective-permute-start.5
  338.1 91.4 %collective-permute-done.1 = bf16[4,512,2,2,128]{4,0,3,1,2:T(4,128)(2,1)} collective-permute-done((bf16[4,512,2,2,128]{4,0,3,1,2:T(4,128)(2,1)}, bf16[4,512,2,2,128]{4,0,3,1,2:T(4,128)(2,1)}, u32[]{:S(2)}, u32[]{:S(2)}) %collective-permute-start.1) | collective-permute-done | bytes 2097184 | tf_op jit(solution)/shard_map/ppermute | solution.py:15
  429.5 1.5 collective-permute-start.6
  431.0 43.5 %collective-permute-done.2 = bf16[4,512,2,2,128]{4,0,3,1,2:T(4,128)(2,1)} collective-permute-done((bf16[4,512,2,2,128]{4,0,3,1,2:T(4,128)(2,1)}, bf16[4,512,2,2,128]{4,0,3,1,2:T(4,128)(2,1)}, u32[]{:S(2)}, u32[]{:S(2)}) %collective-permute-start.2) | collective-permute-done | bytes 2097184 | tf_op jit(solution)/shard_map/ppermute | solution.py:15
  474.5 1.3 collective-permute-start.7
  475.7 0.1 broadcast_compare_fusion
  475.8 3.1 fusion.33
  479.0 1.0 copy-done.3
  480.0 1.1 copy.60
  481.1 2.5 copy.41
  483.6 1.3 multiply_reduce_fusion
  484.9 1.4 fusion.5
  486.3 1.7 fusion.7
  488.1 0.0 collective-permute-done.3
  488.1 14.6 %collective-permute-done.7 = bf16[4,512,2,2,128]{4,0,3,1,2:T(4,128)(2,1)} collective-permute-done((bf16[4,512,2,2,128]{4,0,3,1,2:T(4,128)(2,1)}, bf16[4,512,2,2,128]{4,0,3,1,2:T(4,128)(2,1)}, u32[]{:S(2)}, u32[]{:S(2)}) %collective-permute-start.7) | collective-permute-done | bytes 2097184 | tf_op jit(solution)/shard_map/ppermute | solution.py:15
  502.7 91.1 %concatenate.3 = bf16[36,512,2,2,128]{4,0,3,1,2:T(8,128)(2,1)} concatenate(bf16[4,512,2,2,128]{4,0,3,1,2:T(4,128)(2,1)} %collective-permute-done, bf16[4,512,2,2,128]{4,0,3,1,2:T(4,128)(2,1)} %collective-permute-done.1, bf16[4,512,2,2,128]{4,0,3,1,2:T(4,128)(2,1)} %collective-permute-done.2, bf16[4,512,2,2,128]{4,0,3,1,2:T(4,128)(2,1)} %collective-permute-done.3, ...), dimensions={0} | concatenate | bytes 37748736 | tf_op jit(solution)/shard_map/concatenate | solution.py:67
  593.8 10.3 %fusion.34 = (f32[512,2,4]{2,1,0:T(2,128)}, bf16[512,2,4,36]{3,2,1,0:T(4,128)(2,1)}) fusion(pred[4,36]{1,0:T(4,128)(4,1)S(1)} %broadcast_compare_fusion, bf16[36,512,2,2,128]{4,0,3,1,2:T(8,128)(2,1)} %concatenate.3, bf16[4,512,2,128]{3,1,2,0:T(8,128)(2,1)S(1)} %bitcast.73), kind=kOutput, calls=%fused_computation.51 | convolution fusion | flops 38633508 | bytes 11846656 | tf_op jit(solution)/shard_map/sub | solution.py:77
  604.1 8.7 %fusion.3 = f32[512,2,4,128]{3,2,1,0:T(4,128)} fusion(bf16[36,512,2,2,128]{4,0,3,1,2:T(8,128)(2,1)} %concatenate.3, bf16[512,2,4,36]{3,2,1,0:T(4,128)(2,1)} %get-tuple-element.14), kind=kOutput, calls=%fused_computation.4 | convolution fusion | flops 37748736 | bytes 13631488 | tf_op jit(solution)/shard_map/shfg,gshd->shfd/dot_general | solution.py:78
  612.9 3.0 copy.33
  615.8 0.2 copy.34
  616.0 2.2 fusion.15
  618.2 0.7 copy.35
  618.9 16.7 %all_to_all.15 = bf16[4,512,256]{2,0,1:T(4,128)(2,1)S(1)} all-to-all(bf16[4,512,256]{2,0,1:T(4,128)(2,1)S(1)} %copy.35), channel_id=1, replica_groups=mesh['tm'=16,'row'=8] {'row'}, dimensions={1} | all-to-all | bytes 2097152 | tf_op jit(solution)/shard_map/all_to_all | solution.py:89
  635.6 0.1 copy.36
  635.7 0.1 copy.45
  635.8 0.0 copy-start.1
  635.8 9.7 %fusion.11 = f32[4,64,3072]{2,1,0:T(8,128)} fusion(bf16[4,64,2048]{2,1,0:T(8,128)(2,1)S(1)} %bitcast.74, bf16[2048,3072]{1,0:T(8,128)(2,1)} %param.9, f32[4,3072]{1,0:T(4,128)S(1)} %get-tuple-element.8), kind=kOutput, calls=%fused_computation.14 | convolution fusion | flops 3222011904 | bytes 16826368 | tf_op jit(solution)/shard_map/dot_general | solution.py:90
  (21 shorter events, 0.1 us)
Async XLA Ops:
  6.5 1.0 copy-start
  6.5 3.4 copy-start.2
  6.5 253.8 %all-gather.2.cloned.1.call-start = ((), (), s32[]{:S(2)}) async-start(), calls=%async_computation.1 | async-start | bytes 14155776 | tf_op jit(solution)/shard_map/all_gather | solution.py:42
  282.9 17.7 %copy-start.8 = (s32[64]{0:T(128)S(1)}, s32[64]{0:T(128)}, u32[]{:S(2)}) copy-start(s32[64]{0:T(128)} %param.6) | copy-start | bytes 772
  287.0 49.9 %collective-permute-start = (bf16[4,512,2,2,128]{4,0,3,1,2:T(4,128)(2,1)}, bf16[4,512,2,2,128]{4,0,3,1,2:T(4,128)(2,1)}, u32[]{:S(2)}, u32[]{:S(2)}) collective-permute-start(bf16[4,512,2,2,128]{4,0,3,1,2:T(4,128)(2,1)} %copy.44), channel_id=1, source_target_pairs={{0,32},{8,40},{16,48},{24,56},{32,64},{40,72},{48,80},{56,88},{64,... | collective-permute-start | bytes 6291464 | tf_op jit(solution)/shard_map/ppermute | solution.py:15
  291.8 137.7 %collective-permute-start.1 = (bf16[4,512,2,2,128]{4,0,3,1,2:T(4,128)(2,1)}, bf16[4,512,2,2,128]{4,0,3,1,2:T(4,128)(2,1)}, u32[]{:S(2)}, u32[]{:S(2)}) collective-permute-start(bf16[4,512,2,2,128]{4,0,3,1,2:T(4,128)(2,1)} %copy.44), channel_id=1, source_target_pairs={{0,24},{8,32},{16,40},{24,48},{32,56},{40,64},{48,72},{56,80},{64,... | collective-permute-start | bytes 6291464 | tf_op jit(solution)/shard_map/ppermute | solution.py:15
  296.8 177.7 %collective-permute-start.2 = (bf16[4,512,2,2,128]{4,0,3,1,2:T(4,128)(2,1)}, bf16[4,512,2,2,128]{4,0,3,1,2:T(4,128)(2,1)}, u32[]{:S(2)}, u32[]{:S(2)}) collective-permute-start(bf16[4,512,2,2,128]{4,0,3,1,2:T(4,128)(2,1)} %copy.44), channel_id=1, source_target_pairs={{0,16},{8,24},{16,32},{24,40},{32,48},{40,56},{48,64},{56,72},{64,... | collective-permute-start | bytes 6291464 | tf_op jit(solution)/shard_map/ppermute | solution.py:15
  300.7 187.4 %collective-permute-start.3 = (bf16[4,512,2,2,128]{4,0,3,1,2:T(4,128)(2,1)}, bf16[4,512,2,2,128]{4,0,3,1,2:T(4,128)(2,1)}, u32[]{:S(2)}, u32[]{:S(2)}) collective-permute-start(bf16[4,512,2,2,128]{4,0,3,1,2:T(4,128)(2,1)} %copy.44), channel_id=1, source_target_pairs={{0,8},{8,16},{16,24},{24,32},{32,40},{40,48},{48,56},{56,64},{64,7... | collective-permute-start | bytes 6291464 | tf_op jit(solution)/shard_map/ppermute | solution.py:15
  303.3 184.7 %collective-permute-start.4 = (bf16[4,512,2,2,128]{4,0,3,1,2:T(4,128)(2,1)}, bf16[4,512,2,2,128]{4,0,3,1,2:T(4,128)(2,1)}, u32[]{:S(2)}, u32[]{:S(2)}) collective-permute-start(bf16[4,512,2,2,128]{4,0,3,1,2:T(4,128)(2,1)} %copy.44), channel_id=1, source_target_pairs={{8,0},{16,8},{24,16},{32,24},{40,32},{48,40},{56,48},{64,56},{72,6... | collective-permute-start | bytes 6291464 | tf_op jit(solution)/shard_map/ppermute | solution.py:15
  336.9 151.2 %collective-permute-start.5 = (bf16[4,512,2,2,128]{4,0,3,1,2:T(4,128)(2,1)}, bf16[4,512,2,2,128]{4,0,3,1,2:T(4,128)(2,1)}, u32[]{:S(2)}, u32[]{:S(2)}) collective-permute-start(bf16[4,512,2,2,128]{4,0,3,1,2:T(4,128)(2,1)} %copy.44), channel_id=1, source_target_pairs={{16,0},{24,8},{32,16},{40,24},{48,32},{56,40},{64,48},{72,56},{80,... | collective-permute-start | bytes 6291464 | tf_op jit(solution)/shard_map/ppermute | solution.py:15
  429.5 58.6 %collective-permute-start.6 = (bf16[4,512,2,2,128]{4,0,3,1,2:T(4,128)(2,1)}, bf16[4,512,2,2,128]{4,0,3,1,2:T(4,128)(2,1)}, u32[]{:S(2)}, u32[]{:S(2)}) collective-permute-start(bf16[4,512,2,2,128]{4,0,3,1,2:T(4,128)(2,1)} %copy.44), channel_id=1, source_target_pairs={{24,0},{32,8},{40,16},{48,24},{56,32},{64,40},{72,48},{80,56},{88,... | collective-permute-start | bytes 6291464 | tf_op jit(solution)/shard_map/ppermute | solution.py:15
  474.5 28.2 %collective-permute-start.7 = (bf16[4,512,2,2,128]{4,0,3,1,2:T(4,128)(2,1)}, bf16[4,512,2,2,128]{4,0,3,1,2:T(4,128)(2,1)}, u32[]{:S(2)}, u32[]{:S(2)}) collective-permute-start(bf16[4,512,2,2,128]{4,0,3,1,2:T(4,128)(2,1)} %copy.44), channel_id=1, source_target_pairs={{32,0},{40,8},{48,16},{56,24},{64,32},{72,40},{80,48},{88,56},{96,... | collective-permute-start | bytes 6291464 | tf_op jit(solution)/shard_map/ppermute | solution.py:15
  479.0 1.0 copy-start.3
  479.0 4.7 copy-start.5
  481.1 2.6 copy-start.4
  488.1 105.7 %copy-start.6 = (bf16[4,512,1,2,128]{4,1,3,0,2:T(8,128)(2,1)S(1)}, bf16[4,512,1,2,128]{4,1,3,0,2:T(8,128)(2,1)}, u32[]{:S(2)}) copy-start(bf16[4,512,1,2,128]{4,1,3,0,2:T(8,128)(2,1)} %copy.60) | copy-start | bytes 3145732
  612.9 3.0 copy-start.7
  635.8 9.8 %copy-start.1 = (f32[8,3,3072]{2,0,1:T(8,128)S(1)}, f32[8,3,3072]{2,0,1:T(8,128)}, u32[]{:S(2)}) copy-start(f32[8,3,3072]{2,0,1:T(8,128)} %param.7) | copy-start | bytes 884740
Sparse Core Ops, SparseCore 0:
  12.4 247.8 all-gather.1
where the time goes:
time: 660 us; the launch traced here: 652 us
  waiting for transfers between devices  423 us (64%)
  local copies, waits for them, and re-layouts  122 us (18%)
  matrix products  47.6 us (7%)
  starting transfers between devices  21.6 us (3%)
  blocking collectives  16.7 us (3%)
  between operations  13.6 us (2%)
  other arithmetic  8.11 us (1%)
    all_gather x1, waiting for transfers between devices, per_device(): lax.all_gather(normed, 'row', axis=1, tiled=True)  241 us
    ppermute x8, waiting for transfers between devices, shifted(): return lax.ppermute(array, axis, pairs)  182 us
    concatenate x1, local copies, waits for them, and re-layouts, per_device(): jnp.concatenate(earlier_pieces[::-1] + [key_values] + later_pieces, axis=0)  91.1 us
    ppermute x8, starting transfers between devices, shifted(): return lax.ppermute(array, axis, pairs)  21.6 us
    all_to_all x1, blocking collectives, per_device(): lax.all_to_all(combined, 'row', split_axis=1, concat_axis=2, tiled=True)  16.7 us
    dot_general x1, matrix products, per_device(): jnp.dot(lax.all_gather(normed, 'row', axis=1, tiled=True), flat_weight, p...  15.5 us
    unnamed x22, local copies, waits for them, and re-layouts  15.4 us
  transfers between devices with their start and end apart: 9, of which 5 were waited for; matrix products, arithmetic and copies ran while one was open for 3% of the time, Pallas kernels for 0%

commit v1 on v0

v1 whole, which is shorter than its diff:
```python
import functools
import math

import jax
import jax.numpy as jnp
from jax import lax
from jax.experimental import pallas as pl
from jax.experimental.pallas import tpu as pltpu
from jax.sharding import PartitionSpec as P

HD = 128
MESH = pl.DeviceIdType.MESH
BF = jnp.bfloat16
F32 = jnp.float32
LOG2E = 1.4426950408889634


def dot(a, b):
    return jnp.dot(a, b, preferred_element_type=F32)


def dot_nt(a, b):
    return lax.dot_general(a, b, (((1,), (1,)), ((), ())), preferred_element_type=F32)


def attention_kernel(
    clip_ref, stream_hbm, mod_ref, w_hbm, comb_ref,
    stream_v, xg, wbuf, qkv, tsend, trecv, osend, orecv, csend, sp, perm, perm_t, mask,
    load_sem, y_send, y_recv, w_send, w_recv, z_send, z_recv, t_send, t_recv,
    o_send, o_recv, c_send, c_recv,
):
    tm = lax.axis_index("tm")
    row = lax.axis_index("row")
    zh = (tm // 2) % 2
    core = tm % 2
    y = row // 2
    zl = row % 2
    hz = (zl + zh) % 2
    partner_row = y * 2 + (1 - zl)
    outer_tm = tm + 2 - 4 * zh
    other_core = tm + 1 - 2 * core
    up_row = ((y + 1) % 4) * 2 + zl
    down_row = ((y + 3) % 4) * 2 + zl

    def rcopy(src, dst, send, recv, dev):
        return pltpu.make_async_remote_copy(
            src_ref=src, dst_ref=dst, send_sem=send, recv_sem=recv,
            device_id=dev, device_id_type=MESH,
        )

    def time_peer(t):
        return (t, y * 2 + (hz + (t // 2) % 2) % 2)

    load_stream = pltpu.make_async_copy(stream_hbm, stream_v, load_sem.at[0])
    load_stream.start()
    load_w = pltpu.make_async_copy(w_hbm, wbuf.at[zl], load_sem.at[1])
    load_w.start()

    barrier = pltpu.get_barrier_semaphore()

    @pl.loop(1, 16)
    def _(k):
        pl.semaphore_signal(barrier, inc=1, device_id=time_peer((tm + k) % 16), device_id_type=MESH)

    @pl.loop(1, 8)
    def _(k):
        pl.semaphore_signal(barrier, inc=1, device_id=(tm, (row + k) % 8), device_id_type=MESH)

    pl.semaphore_wait(barrier, 22)

    qa = core * 2
    w_out = [
        rcopy(w_hbm.at[:, qa], wbuf.at[zl, :, qa], w_send.at[0], w_recv.at[0], (tm, partner_row)),
        rcopy(w_hbm.at[:, qa + 1], wbuf.at[zl, :, qa + 1], w_send.at[1], w_recv.at[1],
              (outer_tm, partner_row)),
    ]
    for c in w_out:
        c.start()

    load_stream.wait()

    def norm_frame(f):
        clip = clip_ref[tm * 4 + f]
        shift = mod_ref[0, pl.ds(clip, 1), :]
        scale = 1.0 + mod_ref[1, pl.ds(clip, 1), :]
        for part in range(2):
            v = stream_v[f, pl.ds(part * 32, 32), :]
            centred = v - jnp.mean(v, axis=-1, keepdims=True)
            var = jnp.mean(centred * centred, axis=-1, keepdims=True)
            n = centred * lax.rsqrt(var + 1e-06) * scale + shift
            xg[y, pl.ds(f * 64 + part * 32, 32), :] = n.astype(BF)

    lo, hi = pl.ds(0, 128), pl.ds(128, 128)
    ym, yp, yq = (y + 3) % 4, (y + 1) % 4, (y + 2) % 4
    up, down = (tm, up_row), (tm, down_row)

    def ycopy(block, half, i, dev):
        return rcopy(xg.at[block, half], xg.at[block, half], y_send.at[i], y_recv.at[i], dev)

    @pl.loop(0, 2)
    def _(f):
        norm_frame(f)

    ycopy(y, lo, 0, up).start()

    @pl.loop(2, 4)
    def _(f):
        norm_frame(f)

    ycopy(y, hi, 2, down).start()
    ycopy(y, hi, 1, up).start()
    ycopy(y, lo, 3, down).start()

    def frame_row(j):
        return ((j // 4) % 4) * 64 + (j // 16) * 4 + j % 4

    r_i = lax.broadcasted_iota(jnp.int32, (256, 256), 0)
    c_i = lax.broadcasted_iota(jnp.int32, (256, 256), 1)
    perm[...] = (frame_row(r_i) == c_i).astype(BF)
    perm_t[...] = (frame_row(c_i) == r_i).astype(BF)
    fr = r_i // 4
    fc = c_i // 4

    def clip_of(f, carry):
        a, b = carry
        c = clip_ref[f]
        return jnp.where(fr == f, c, a), jnp.where(fc == f, c, b)

    zero = jnp.zeros((256, 256), jnp.int32)
    clip_r, clip_c = lax.fori_loop(0, 64, clip_of, (zero, zero))
    same = (clip_r == clip_c) & (r_i % 4 == c_i % 4)
    mask[...] = jnp.where(same, 0.0, -1e30).astype(F32)

    def project(yb, pz):
        kk = (pz + hz) % 2
        slot = kk * 2 + (1 - kk) * zl

        @pl.loop(0, 3)
        def _(part):
            acc = dot(xg[yb, :, 0:768], wbuf[pz, part, 0])
            for q in range(1, 4):
                acc = acc + dot(xg[yb, :, q * 768:(q + 1) * 768], wbuf[pz, part, q])
            qkv[yb, slot, part] = acc.astype(BF)

    def zcopy(yb, d):
        return rcopy(qkv.at[yb, 2], qkv.at[yb, zl], z_send.at[d], z_recv.at[d], (tm, partner_row))

    def tcopy(yb, d, t):
        return rcopy(tsend.at[yb, :, :, t], trecv.at[yb, :, :, tm], t_send.at[d, t], t_recv.at[d, tm],
                     time_peer(t))

    def stage_time(yb, d):
        rcopy(qkv.at[yb, 2], qkv.at[yb, 1 - zl], z_send.at[d], z_recv.at[d], (tm, partner_row)).wait_recv()

        @pl.loop(0, 6)
        def _(i):
            zz, part = i // 3, i % 3
            moved = dot(perm[...], qkv[yb, zz, part]).astype(BF)
            tsend[yb, zz, part] = moved.reshape(16, 16, 256)
            trecv[yb, zz, part, tm] = tsend[yb, zz, part, tm]

        @pl.loop(1, 16)
        def _(k):
            tcopy(yb, d, (tm + k) % 16).start()

    load_w.wait()
    project(y, zl)

    oz = 1 - zl
    for i in range(2):
        rcopy(w_hbm.at[:, qa + i], wbuf.at[oz, :, qa + i], w_send.at[i], w_recv.at[i],
              (tm, partner_row)).wait_recv()
        rcopy(wbuf.at[oz, :, qa + i], wbuf.at[oz, :, qa + i], w_send.at[2 + i], w_recv.at[2 + i],
              (other_core, row)).start()
    ycopy(ym, lo, 0, up).wait_recv()
    ycopy(ym, lo, 4, up).start()
    ycopy(yp, hi, 2, down).wait_recv()
    ycopy(yp, hi, 5, down).start()
    qb = (1 - core) * 2
    for i in range(2):
        rcopy(wbuf.at[oz, :, qb + i], wbuf.at[oz, :, qb + i], w_send.at[2 + i], w_recv.at[2 + i],
              (other_core, row)).wait_recv()

    project(y, oz)
    zcopy(y, 0).start()

    ycopy(ym, hi, 1, up).wait_recv()
    project(ym, 1 - hz)
    zcopy(ym, 1).start()
    project(ym, hz)
    stage_time(y, 0)

    ycopy(yp, lo, 3, down).wait_recv()
    project(yp, 1 - hz)
    zcopy(yp, 2).start()
    project(yp, hz)
    stage_time(ym, 1)

    ycopy(yq, lo, 4, up).wait_recv()
    ycopy(yq, hi, 5, down).wait_recv()
    project(yq, 1 - hz)
    zcopy(yq, 3).start()
    project(yq, hz)
    stage_time(yp, 2)
    stage_time(yq, 3)

    factor = LOG2E / math.sqrt(HD)

    def soften(s):
        p = jnp.exp2((s - jnp.max(s, axis=-1, keepdims=True)) * factor)
        return p, jnp.sum(p, axis=-1, keepdims=True)

    @pl.loop(0, 4)
    def _(f):
        rows = pl.ds(pl.multiple_of(f * 64, 64), 64)
        for h in range(2):
            cols = pl.ds(h * HD, HD)
            q, k, v = (qkv[:, 0:2, part, rows, cols].reshape(512, HD) for part in range(3))
            for half in range(2):
                p, total = soften(dot_nt(q[half * 256:(half + 1) * 256], k))
                o = dot(p.astype(BF), v) / total
                sp[pl.ds(half * 2, 2), :, rows, cols] = o.reshape(2, 2, 64, HD)

    for d, yb in enumerate((y, ym, yp, yq)):
        @pl.loop(1, 16)
        def _(k, d=d, yb=yb):
            t = (tm + k) % 16
            rcopy(tsend.at[yb, :, :, t], trecv.at[yb, :, :, t], t_send.at[d, t], t_recv.at[d, t],
                  time_peer(t)).wait_recv()

        @pl.loop(0, 2)
        def _(zz, yb=yb):
            for h in range(2):
                cols = pl.ds(h * HD, HD)
                q, k, v = (trecv[yb, zz, part, :, :, cols].reshape(256, HD) for part in range(3))
                p, total = soften(dot_nt(q, k) + mask[...])
                o = dot(p.astype(BF), v) / total
                osend[yb, zz, :, :, cols] = o.astype(BF).reshape(16, 16, HD)

    def ocopy(t, at):
        return rcopy(osend.at[:, :, t], orecv.at[:, :, at], o_send.at[t], o_recv.at[at], time_peer(t))

    @pl.loop(1, 16)
    def _(k):
        ocopy((tm + k) % 16, tm).start()

    orecv[:, :, tm] = osend[:, :, tm]

    @pl.loop(1, 16)
    def _(k):
        t = (tm + k) % 16
        ocopy(t, t).wait_recv()

    def cols_of(r):
        return pl.ds(pl.multiple_of((2 * (r // 2) + (r % 2 + zh) % 2) * 256, 256), 256)

    def ccopy(r, owner):
        return rcopy(csend.at[r], comb_ref.at[:, cols_of(owner)], c_send.at[r], c_recv.at[owner], (tm, r))

    def combine(r):
        back = dot(perm_t[...], orecv[r // 2, r % 2].reshape(256, 256))
        csend[r] = (sp[r // 2, r % 2] + back).astype(BF)

    @pl.loop(1, 8)
    def _(k):
        r = (row + k) % 8
        combine(r)
        ccopy(r, row).start()

    combine(row)
    comb_ref[:, cols_of(row)] = csend[row]

    @pl.loop(1, 8)
    def _(k):
        r = (row + k) % 8
        ccopy(r, r).wait_recv()

    for c in w_out:
        c.wait_send()
    for i in range(2):
        rcopy(wbuf.at[oz, :, qa + i], wbuf.at[oz, :, qa + i], w_send.at[2 + i], w_recv.at[2 + i],
              (other_core, row)).wait_send()
    for i, (block, half) in enumerate(((y, lo), (y, hi), (y, hi), (y, lo), (ym, lo), (yp, hi))):
        ycopy(block, half, i, up).wait_send()
    for d, yb in enumerate((y, ym, yp, yq)):
        zcopy(yb, d).wait_send()

        @pl.loop(1, 16)
        def _(k, d=d, yb=yb):
            tcopy(yb, d, (tm + k) % 16).wait_send()

    @pl.loop(1, 16)
    def _(k):
        ocopy((tm + k) % 16, tm).wait_send()

    @pl.loop(1, 8)
    def _(k):
        ccopy((row + k) % 8, row).wait_send()


def attention(clip_ids, stream, mod, weight):
    vmem = pl.BlockSpec(memory_space=pltpu.VMEM)
    hbm = pl.BlockSpec(memory_space=pl.ANY)
    dma = pltpu.SemaphoreType.DMA
    return pl.pallas_call(
        attention_kernel,
        out_shape=jax.ShapeDtypeStruct((256, 2048), BF),
        in_specs=[pl.BlockSpec(memory_space=pltpu.SMEM), hbm, vmem, hbm],
        out_specs=vmem,
        scratch_shapes=[
            pltpu.VMEM((4, 64, 3072), F32),
            pltpu.VMEM((4, 256, 3072), BF),
            pltpu.VMEM((2, 3, 4, 768, 256), BF),
            pltpu.VMEM((4, 3, 3, 256, 256), BF),
            pltpu.VMEM((4, 2, 3, 16, 16, 256), BF),
            pltpu.VMEM((4, 2, 3, 16, 16, 256), BF),
            pltpu.VMEM((4, 2, 16, 16, 256), BF),
            pltpu.VMEM((4, 2, 16, 16, 256), BF),
            pltpu.VMEM((8, 256, 256), BF),
            pltpu.VMEM((4, 2, 256, 256), F32),
            pltpu.VMEM((256, 256), BF),
            pltpu.VMEM((256, 256), BF),
            pltpu.VMEM((256, 256), F32),
            dma((2,)),
            dma((6,)), dma((6,)),
            dma((4,)), dma((4,)),
            dma((4,)), dma((4,)),
            dma((4, 16)), dma((4, 16)),
            dma((16,)), dma((16,)),
            dma((8,)), dma((8,)),
        ],
        compiler_params=pltpu.CompilerParams(
            collective_id=0, has_side_effects=True, vmem_limit_bytes=58 * 1024 * 1024
        ),
        name="attention",
    )(clip_ids, stream, mod, weight)


def out_kernel(clip_ref, comb_ref, weight_ref, gate_ref, out_ref):
    tm = lax.axis_index("tm")
    acc = dot(comb_ref[...], weight_ref[...])
    for f in range(4):
        clip = clip_ref[tm * 4 + f]
        out_ref[f] = acc[f * 64:(f + 1) * 64] * gate_ref[0, pl.ds(clip, 1), :]


def out_projection(clip_ids, comb, out_weight, mod):
    tile = 512
    return pl.pallas_call(
        out_kernel,
        grid=(3072 // tile,),
        out_shape=jax.ShapeDtypeStruct((4, 64, 3072), F32),
        in_specs=[
            pl.BlockSpec(memory_space=pltpu.SMEM),
            pl.BlockSpec((256, 2048), lambda i: (0, 0)),
            pl.BlockSpec((2048, tile), lambda i: (0, i)),
            pl.BlockSpec((1, 8, tile), lambda i: (2, 0, i)),
        ],
        out_specs=pl.BlockSpec((4, 64, tile), lambda i: (0, 0, i)),
        compiler_params=pltpu.CompilerParams(vmem_limit_bytes=32 * 1024 * 1024),
        name="out_projection",
    )(clip_ids, comb, out_weight, mod)


def per_device(stream, clip_ids, modulation, qkv_weight, out_weight):
    mod = jnp.transpose(modulation, (1, 0, 2))
    weight = jnp.transpose(qkv_weight, (1, 0, 2)).reshape(3, 4, 768, 256)
    comb = attention(clip_ids, stream, mod, weight)
    return out_projection(clip_ids, comb, out_weight, mod)


def solution(mesh):
    placed = (P("tm", "row", None), P(), P(), P(None, None, "row"), P())
    return jax.shard_map(
        per_device, mesh=mesh, in_specs=placed, out_specs=P("tm", "row", None), check_vma=False
    )
```

time: 660 us -> 141 us (0.21); the launches traced: 652 us -> 141 us
  waiting for transfers between devices: 423 us -> 0 us
  Pallas kernels: 0 us -> 135 us
  local copies, waits for them, and re-layouts: 122 us -> 5.8 us
  matrix products: 47.6 us -> 0 us
  starting transfers between devices: 21.6 us -> 0 us
  blocking collectives: 16.7 us -> 0 us
  between operations: 13.6 us -> 0.04 us
  other arithmetic: 8.11 us -> 0 us
    all_gather x1 -> x0, waiting for transfers between devices: 241 us -> none  [per_device(): lax.all_gather(normed, 'row', axis=1, tiled=True)]
    ppermute x8 -> x0, waiting for transfers between devices: 182 us -> none  [shifted(): return lax.ppermute(array, axis, pairs)]
    pallas_call x0 -> x2, Pallas kernels: none -> 135 us  [the longest x1 128 us: attention(): pl.pallas_call(attention_kernel, out_shape=jax.ShapeDtypeStruct((256, 204...]
    concatenate x1 -> x0, local copies, waits for them, and re-layouts: 91.1 us -> none  [per_device(): jnp.concatenate(earlier_pieces[::-1] + [key_values] + later_pieces, axis=0)]
    dot_general x6 -> x0, matrix products: 37.3 us -> none  [the longest x1 15.5 us: per_device(): jnp.dot(lax.all_gather(normed, 'row', axis=1, tiled=True), flat_weight, p...]
    ppermute x8 -> x0, starting transfers between devices: 21.6 us -> none  [shifted(): return lax.ppermute(array, axis, pairs)]
    all_to_all x1 -> x0, blocking collectives: 16.7 us -> none  [per_device(): lax.all_to_all(combined, 'row', split_axis=1, concat_axis=2, tiled=True)]
    sub x1 -> x0, matrix products: 10.3 us -> none  [per_device(): weights = jnp.where(match, jnp.exp(scores - row_max), 0.0)]
  transfers between devices with their start and end apart: 9 -> 0, of which waited for: 5 -> 0; matrix products, arithmetic and copies ran while one was open for 3% -> 0% of each run, Pallas kernels for 0% -> 0%
where the time goes in v1:
time: 141 us
  Pallas kernels  135 us (96%)
  local copies, waits for them, and re-layouts  5.8 us (4%)
    pallas_call x1, Pallas kernels, attention(): pl.pallas_call(attention_kernel, out_shape=jax.ShapeDtypeStruct((256, 204...  128 us
    pallas_call x1, Pallas kernels, out_projection(): pl.pallas_call(out_kernel, grid=(3072 // tile,), out_shape=jax.ShapeDtype...  6.49 us
    unnamed x8, local copies, waits for them, and re-layouts  5.8 us

profile of v1, /device:TPU:32, one launch (start us, length us, event | category | flops | bytes accessed | tf_op | source)
XLA Modules:
  0.0 140.6 jit_solution(9965706933956189786)
XLA Ops:
  0.0 0.0 copy-start.3
  0.0 0.0 copy-start.2
  0.0 128.3 %attention.1.comb_ref = bf16[256,2048]{1,0:T(8,128)(2,1)} custom-call(s32[64]{0:T(128)} %clip_ref.3, f32[4,64,3072]{2,1,0:T(8,128)} %stream_hbm.1, f32[3,8,3072]{2,1,0:T(8,128)} %bitcast.4, bf16[3,4,768,256]{3,2,1,0:T(8,128)(2,1)} %bitcast.6), custom_call_target="tpu_custom_call" | custom-call | tf_op jit(solution)/shard_map/attention/pallas_call | solution.py:305
  128.3 0.0 copy-done.3
  128.3 0.0 copy-done.2
  128.4 0.0 copy-start
  128.4 4.6 %copy-done = bf16[2048,3072]{1,0:T(8,128)(2,1)S(1)} copy-done((bf16[2048,3072]{1,0:T(8,128)(2,1)S(1)}, bf16[2048,3072]{1,0:T(8,128)(2,1)}, u32[]{:S(2)}) %copy-start) | copy-done | bytes 12582936
  132.9 0.0 copy-start.1
  132.9 1.2 copy-done.1
  134.2 6.5 %out_projection.1 = f32[4,64,3072]{2,1,0:T(8,128)} custom-call(s32[64]{0:T(128)S(1)} %copy-done.3, bf16[256,2048]{1,0:T(8,128)(2,1)S(1)} %copy-done.1, bf16[2048,3072]{1,0:T(8,128)(2,1)S(1)} %copy-done, f32[3,8,3072]{2,1,0:T(8,128)S(1)} %bitcast.5), custom_call_target="tpu_custom_call" | custom-call | tf_op jit(solution)/shard_map/out_projection/pallas_call | solution.py:349
Async XLA Ops:
  0.0 128.3 %copy-start.3 = (s32[64]{0:T(128)S(1)}, s32[64]{0:T(128)}, u32[]{:S(2)}) copy-start(s32[64]{0:T(128)} %clip_ref.3) | copy-start | bytes 772
  0.0 128.3 %copy-start.2 = (f32[8,3,3072]{2,0,1:T(8,128)S(1)}, f32[8,3,3072]{2,0,1:T(8,128)}, u32[]{:S(2)}) copy-start(f32[8,3,3072]{2,0,1:T(8,128)} %param.7) | copy-start | bytes 884740
  128.4 4.6 %copy-start = (bf16[2048,3072]{1,0:T(8,128)(2,1)S(1)}, bf16[2048,3072]{1,0:T(8,128)(2,1)}, u32[]{:S(2)}) copy-start(bf16[2048,3072]{1,0:T(8,128)(2,1)} %weight_ref.1) | copy-start | bytes 37748740
  132.9 1.2 copy-start.1

commit v2 on v1

v2 whole, which is shorter than its diff:
```python
import functools
import math

import jax
import jax.numpy as jnp
from jax import lax
from jax.experimental import pallas as pl
from jax.experimental.pallas import tpu as pltpu
from jax.sharding import PartitionSpec as P

HD = 128
MESH = pl.DeviceIdType.MESH
BF = jnp.bfloat16
F32 = jnp.float32
LOG2E = 1.4426950408889634


def dot(a, b):
    return jnp.dot(a, b, preferred_element_type=F32)


def dot_nt(a, b):
    return lax.dot_general(a, b, (((1,), (1,)), ((), ())), preferred_element_type=F32)


def attention_kernel(
    clip_ref, stream_hbm, mod_ref, w_hbm, wo_hbm, out_ref,
    stream_v, xg, wbuf, wo, qkv, tsend, trecv, osend, orecv, csend, comb, sp, perm, perm_t, mask,
    load_sem, y_send, y_recv, w_send, w_recv, z_send, z_recv, t_send, t_recv,
    o_send, o_recv, c_send, c_recv,
):
    tm = lax.axis_index("tm")
    row = lax.axis_index("row")
    zh = (tm // 2) % 2
    core = tm % 2
    y = row // 2
    zl = row % 2
    hz = (zl + zh) % 2
    partner_row = y * 2 + (1 - zl)
    outer_tm = tm + 2 - 4 * zh
    other_core = tm + 1 - 2 * core
    up_row = ((y + 1) % 4) * 2 + zl
    down_row = ((y + 3) % 4) * 2 + zl

    def rcopy(src, dst, send, recv, dev):
        return pltpu.make_async_remote_copy(
            src_ref=src, dst_ref=dst, send_sem=send, recv_sem=recv,
            device_id=dev, device_id_type=MESH,
        )

    def time_peer(t):
        return (t, y * 2 + (hz + (t // 2) % 2) % 2)

    load_stream = pltpu.make_async_copy(stream_hbm, stream_v, load_sem.at[0])
    load_stream.start()
    load_w = pltpu.make_async_copy(w_hbm, wbuf.at[zl], load_sem.at[1])
    load_w.start()
    load_wo = pltpu.make_async_copy(wo_hbm, wo, load_sem.at[2])
    load_wo.start()

    barrier = pltpu.get_barrier_semaphore()

    @pl.loop(1, 16)
    def _(k):
        pl.semaphore_signal(barrier, inc=1, device_id=time_peer((tm + k) % 16), device_id_type=MESH)

    @pl.loop(1, 8)
    def _(k):
        pl.semaphore_signal(barrier, inc=1, device_id=(tm, (row + k) % 8), device_id_type=MESH)

    pl.semaphore_wait(barrier, 22)

    qa = core * 2
    w_out = [
        rcopy(w_hbm.at[:, qa], wbuf.at[zl, :, qa], w_send.at[0], w_recv.at[0], (tm, partner_row)),
        rcopy(w_hbm.at[:, qa + 1], wbuf.at[zl, :, qa + 1], w_send.at[1], w_recv.at[1],
              (outer_tm, partner_row)),
    ]
    for c in w_out:
        c.start()

    load_stream.wait()

    def norm_frame(f):
        clip = clip_ref[tm * 4 + f]
        shift = mod_ref[0, pl.ds(clip, 1), :]
        scale = 1.0 + mod_ref[1, pl.ds(clip, 1), :]
        for part in range(2):
            v = stream_v[f, pl.ds(part * 32, 32), :]
            centred = v - jnp.mean(v, axis=-1, keepdims=True)
            var = jnp.mean(centred * centred, axis=-1, keepdims=True)
            n = centred * lax.rsqrt(var + 1e-06) * scale + shift
            xg[y, pl.ds(f * 64 + part * 32, 32), :] = n.astype(BF)

    lo, hi = pl.ds(0, 128), pl.ds(128, 128)
    ym, yp, yq = (y + 3) % 4, (y + 1) % 4, (y + 2) % 4
    up, down = (tm, up_row), (tm, down_row)

    def ycopy(block, half, i, dev):
        return rcopy(xg.at[block, half], xg.at[block, half], y_send.at[i], y_recv.at[i], dev)

    @pl.loop(0, 2)
    def _(f):
        norm_frame(f)

    ycopy(y, lo, 0, up).start()

    @pl.loop(2, 4)
    def _(f):
        norm_frame(f)

    ycopy(y, hi, 2, down).start()
    ycopy(y, hi, 1, up).start()
    ycopy(y, lo, 3, down).start()

    def frame_row(j):
        return ((j // 4) % 4) * 64 + (j // 16) * 4 + j % 4

    r_i = lax.broadcasted_iota(jnp.int32, (256, 256), 0)
    c_i = lax.broadcasted_iota(jnp.int32, (256, 256), 1)
    perm[...] = (frame_row(r_i) == c_i).astype(BF)
    perm_t[...] = (frame_row(c_i) == r_i).astype(BF)
    fr = r_i // 4
    fc = c_i // 4

    def clip_of(f, carry):
        a, b = carry
        c = clip_ref[f]
        return jnp.where(fr == f, c, a), jnp.where(fc == f, c, b)

    zero = jnp.zeros((256, 256), jnp.int32)
    clip_r, clip_c = lax.fori_loop(0, 64, clip_of, (zero, zero))
    same = (clip_r == clip_c) & (r_i % 4 == c_i % 4)
    mask[...] = jnp.where(same, 0.0, -1e30).astype(F32)

    def project(yb, pz):
        kk = (pz + hz) % 2
        slot = kk * 2 + (1 - kk) * zl

        @pl.loop(0, 3)
        def _(part):
            acc = dot(xg[yb, :, 0:768], wbuf[pz, part, 0])
            for q in range(1, 4):
                acc = acc + dot(xg[yb, :, q * 768:(q + 1) * 768], wbuf[pz, part, q])
            qkv[yb, slot, part] = acc.astype(BF)

    def zcopy(yb, d):
        return rcopy(qkv.at[yb, 2], qkv.at[yb, zl], z_send.at[d], z_recv.at[d], (tm, partner_row))

    def tcopy(yb, d, zz, t, at):
        return rcopy(tsend.at[yb, zz, :, t], trecv.at[yb, zz, :, at], t_send.at[d, zz, t],
                     t_recv.at[d, zz, at], time_peer(t))

    def stage_time(yb, d, zz):
        @pl.loop(0, 3)
        def _(part):
            moved = dot(perm[...], qkv[yb, zz, part]).astype(BF)
            tsend[yb, zz, part] = moved.reshape(16, 16, 256)
            trecv[yb, zz, part, tm] = tsend[yb, zz, part, tm]

        @pl.loop(1, 16)
        def _(k):
            tcopy(yb, d, zz, (tm + k) % 16, tm).start()

    def stage_partner(yb, d):
        rcopy(qkv.at[yb, 2], qkv.at[yb, 1 - zl], z_send.at[d], z_recv.at[d], (tm, partner_row)).wait_recv()
        stage_time(yb, d, 1 - zl)

    factor = LOG2E / math.sqrt(HD)

    def soften(s):
        p = jnp.exp2((s - jnp.max(s, axis=-1, keepdims=True)) * factor)
        return p, jnp.sum(p, axis=-1, keepdims=True)

    def ocopy(yb, d, t, at):
        return rcopy(osend.at[yb, :, t], orecv.at[yb, :, at], o_send.at[d, t], o_recv.at[d, at],
                     time_peer(t))

    def temporal(yb, d):
        @pl.loop(0, 30)
        def _(i):
            t = (tm + 1 + i % 15) % 16
            tcopy(yb, d, i // 15, t, t).wait_recv()

        @pl.loop(0, 2)
        def _(zz):
            for h in range(2):
                cols = pl.ds(h * HD, HD)
                q, k, v = (trecv[yb, zz, part, :, :, cols].reshape(256, HD) for part in range(3))
                p, total = soften(dot_nt(q, k) + mask[...])
                o = dot(p.astype(BF), v) / total
                osend[yb, zz, :, :, cols] = o.astype(BF).reshape(16, 16, HD)

        orecv[yb, :, tm] = osend[yb, :, tm]

        @pl.loop(1, 16)
        def _(k):
            ocopy(yb, d, (tm + k) % 16, tm).start()

    def spatial():
        @pl.loop(0, 4)
        def _(f):
            rows = pl.ds(pl.multiple_of(f * 64, 64), 64)
            for h in range(2):
                cols = pl.ds(h * HD, HD)
                q, k, v = (qkv[:, 0:2, part, rows, cols].reshape(512, HD) for part in range(3))
                for half in range(2):
                    p, total = soften(dot_nt(q[half * 256:(half + 1) * 256], k))
                    o = dot(p.astype(BF), v) / total
                    sp[pl.ds(half * 2, 2), :, rows, cols] = o.reshape(2, 2, 64, HD)

    def ccopy(r, at, kept):
        return rcopy(csend.at[r], comb.at[kept], c_send.at[r], c_recv.at[at], (tm, r))

    def combine(yb, zz):
        back = dot(perm_t[...], orecv[yb, zz].reshape(256, 256))
        return (sp[yb, zz] + back).astype(BF)

    def combine_send(yb, zz):
        r = yb * 2 + zz
        csend[r] = combine(yb, zz)
        ccopy(r, row, y * 2 + hz).start()

    def wait_back(yb, d):
        @pl.loop(1, 16)
        def _(k):
            t = (tm + k) % 16
            ocopy(yb, d, t, t).wait_recv()

    def combine_block(yb, d):
        wait_back(yb, d)
        for zz in range(2):
            combine_send(yb, zz)

    def project_out(ys, first=False, last=False):
        for i in range(2):
            r = ys * 2 + i
            if first:
                @pl.when(i != zl)
                def _(r=r):
                    ccopy(r, r, y * 2 + (r + zh) % 2).wait_recv()
            else:
                ccopy(r, r, ys * 2 + (r + zh) % 2).wait_recv()

        @pl.loop(0, 6)
        def _(n):
            cols = pl.ds(pl.multiple_of(n * 512, 512), 512)
            acc = dot(comb[2 * ys], wo[2 * ys, :, cols]) + dot(comb[2 * ys + 1], wo[2 * ys + 1, :, cols])
            acc = acc.reshape(4, 64, 512)
            if not first:
                acc = acc + out_ref[:, :, cols]
            if not last:
                out_ref[:, :, cols] = acc
            else:
                for f in range(4):
                    clip = clip_ref[tm * 4 + f]
                    out_ref[f, :, cols] = acc[f] * mod_ref[2, pl.ds(clip, 1), cols]

    load_w.wait()
    project(y, zl)

    oz = 1 - zl
    for i in range(2):
        rcopy(w_hbm.at[:, qa + i], wbuf.at[oz, :, qa + i], w_send.at[i], w_recv.at[i],
              (tm, partner_row)).wait_recv()
        rcopy(wbuf.at[oz, :, qa + i], wbuf.at[oz, :, qa + i], w_send.at[2 + i], w_recv.at[2 + i],
              (other_core, row)).start()
    ycopy(ym, lo, 0, up).wait_recv()
    ycopy(ym, lo, 4, up).start()
    ycopy(yp, hi, 2, down).wait_recv()
    ycopy(yp, hi, 5, down).start()
    qb = (1 - core) * 2
    for i in range(2):
        rcopy(wbuf.at[oz, :, qb + i], wbuf.at[oz, :, qb + i], w_send.at[2 + i], w_recv.at[2 + i],
              (other_core, row)).wait_recv()

    project(y, oz)
    zcopy(y, 0).start()
    stage_time(y, 0, zl)

    ycopy(ym, hi, 1, up).wait_recv()
    project(ym, 1 - hz)
    zcopy(ym, 1).start()
    project(ym, hz)
    stage_time(ym, 1, zl)
    stage_partner(y, 0)

    ycopy(yp, lo, 3, down).wait_recv()
    project(yp, 1 - hz)
    zcopy(yp, 2).start()
    project(yp, hz)
    stage_time(yp, 2, zl)
    stage_partner(ym, 1)
    temporal(y, 0)
    stage_partner(yp, 2)

    ycopy(yq, lo, 4, up).wait_recv()
    ycopy(yq, hi, 5, down).wait_recv()
    project(yq, 1 - hz)
    zcopy(yq, 3).start()
    project(yq, hz)
    stage_time(yq, 3, zl)
    temporal(ym, 1)
    stage_partner(yq, 3)
    temporal(yp, 2)
    spatial()

    wait_back(y, 0)
    combine_send(y, 1 - zl)
    comb[y * 2 + hz] = combine(y, zl)
    combine_block(ym, 1)
    temporal(yq, 3)
    combine_block(yp, 2)
    load_wo.wait()
    project_out(y, first=True)
    combine_block(yq, 3)
    project_out(yp)
    project_out(ym)
    project_out(yq, last=True)

    for c in w_out:
        c.wait_send()
    for i in range(2):
        rcopy(wbuf.at[oz, :, qa + i], wbuf.at[oz, :, qa + i], w_send.at[2 + i], w_recv.at[2 + i],
              (other_core, row)).wait_send()
    for i, (block, half) in enumerate(((y, lo), (y, hi), (y, hi), (y, lo), (ym, lo), (yp, hi))):
        ycopy(block, half, i, up).wait_send()
    for d, yb in enumerate((y, ym, yp, yq)):
        zcopy(yb, d).wait_send()

        @pl.loop(0, 30)
        def _(i, d=d, yb=yb):
            tcopy(yb, d, i // 15, (tm + 1 + i % 15) % 16, tm).wait_send()

        @pl.loop(1, 16)
        def _(k, d=d, yb=yb):
            ocopy(yb, d, (tm + k) % 16, tm).wait_send()

    @pl.loop(1, 8)
    def _(k):
        ccopy((row + k) % 8, row, y * 2 + hz).wait_send()


def attention(clip_ids, stream, mod, weight, out_weight):
    vmem = pl.BlockSpec(memory_space=pltpu.VMEM)
    hbm = pl.BlockSpec(memory_space=pl.ANY)
    dma = pltpu.SemaphoreType.DMA
    return pl.pallas_call(
        attention_kernel,
        out_shape=jax.ShapeDtypeStruct((4, 64, 3072), F32),
        in_specs=[pl.BlockSpec(memory_space=pltpu.SMEM), hbm, vmem, hbm, hbm],
        out_specs=vmem,
        scratch_shapes=[
            pltpu.VMEM((4, 64, 3072), F32),
            pltpu.VMEM((4, 256, 3072), BF),
            pltpu.VMEM((2, 3, 4, 768, 256), BF),
            pltpu.VMEM((8, 256, 3072), BF),
            pltpu.VMEM((4, 3, 3, 256, 256), BF),
            pltpu.VMEM((4, 2, 3, 16, 16, 256), BF),
            pltpu.VMEM((4, 2, 3, 16, 16, 256), BF),
            pltpu.VMEM((4, 2, 16, 16, 256), BF),
            pltpu.VMEM((4, 2, 16, 16, 256), BF),
            pltpu.VMEM((8, 256, 256), BF),
            pltpu.VMEM((8, 256, 256), BF),
            pltpu.VMEM((4, 2, 256, 256), F32),
            pltpu.VMEM((256, 256), BF),
            pltpu.VMEM((256, 256), BF),
            pltpu.VMEM((256, 256), F32),
            dma((3,)),
            dma((6,)), dma((6,)),
            dma((4,)), dma((4,)),
            dma((4,)), dma((4,)),
            dma((4, 2, 16)), dma((4, 2, 16)),
            dma((4, 16)), dma((4, 16)),
            dma((8,)), dma((8,)),
        ],
        compiler_params=pltpu.CompilerParams(
            collective_id=0, has_side_effects=True, vmem_limit_bytes=60 * 1024 * 1024
        ),
        name="attention",
    )(clip_ids, stream, mod, weight, out_weight)


def per_device(stream, clip_ids, modulation, qkv_weight, out_weight):
    mod = jnp.transpose(modulation, (1, 0, 2))
    weight = jnp.transpose(qkv_weight, (1, 0, 2)).reshape(3, 4, 768, 256)
    return attention(clip_ids, stream, mod, weight, out_weight.reshape(8, 256, 3072))


def solution(mesh):
    placed = (P("tm", "row", None), P(), P(), P(None, None, "row"), P())
    return jax.shard_map(
        per_device, mesh=mesh, in_specs=placed, out_specs=P("tm", "row", None), check_vma=False
    )
```

time: 141 us -> 128 us (0.908); the launches traced: 141 us -> 126 us
  Pallas kernels: 135 us -> 122 us
  local copies, waits for them, and re-layouts: 5.8 us -> 3.89 us
    pallas_call x2 -> x1, Pallas kernels: 135 us -> 122 us  [attention(): pl.pallas_call(attention_kernel, out_shape=jax.ShapeDtypeStruct((4, 64, 3...]
    unnamed x8 -> x1, local copies, waits for them, and re-layouts: 5.8 us -> 3.89 us
where the time goes in v2:
time: 128 us; the launch traced here: 126 us
  Pallas kernels  122 us (95%)
  local copies, waits for them, and re-layouts  3.89 us (3%)
    pallas_call x1, Pallas kernels, attention(): pl.pallas_call(attention_kernel, out_shape=jax.ShapeDtypeStruct((4, 64, 3...  122 us
    unnamed x1, local copies, waits for them, and re-layouts  3.89 us

profile of v2, /device:TPU:32, one launch (start us, length us, event | category | flops | bytes accessed | tf_op | source)
XLA Modules:
  0.0 126.2 jit_solution(17512455691740812494)
XLA Ops:
  0.0 122.3 %attention.1 = f32[4,64,3072]{2,1,0:T(8,128)} custom-call(s32[64]{0:T(128)} %clip_ref.1, f32[4,64,3072]{2,1,0:T(8,128)} %stream_hbm.1, f32[3,8,3072]{2,1,0:T(8,128)} %bitcast.7, bf16[3,4,768,256]{3,2,1,0:T(8,128)(2,1)} %bitcast.6, bf16[8,256,3072]{2,1,0:T(8,128)(2,1)} %bitcast.5), custom_call_target="tpu_custom_call" | custom-call | tf_op jit(solution)/shard_map/attention/pallas_call | solution.py:348
  122.3 3.9 %copy.7 = f32[4,64,3072]{2,1,0:T(8,128)} copy(f32[4,64,3072]{2,1,0:T(8,128)} %attention.1) | data formatting | bytes 6291456

commit v3 on v2

--- a/solution.py
+++ b/solution.py
@@ -26,7 +26,7 @@
 def attention_kernel(
     clip_ref, stream_hbm, mod_ref, w_hbm, wo_hbm, out_ref,
     stream_v, xg, wbuf, wo, qkv, tsend, trecv, osend, orecv, csend, comb, sp, perm, perm_t, mask,
-    load_sem, y_send, y_recv, w_send, w_recv, z_send, z_recv, t_send, t_recv,
+    load_sem, y_send, y_recv, wz_send, wz_recv, wx_send, wx_recv, wc_send, wc_recv, z_send, z_recv, t_send, t_recv,
     o_send, o_recv, c_send, c_recv,
 ):
     tm = lax.axis_index("tm")
@@ -70,14 +70,30 @@
 
     pl.semaphore_wait(barrier, 22)
 
-    qa = core * 2
-    w_out = [
-        rcopy(w_hbm.at[:, qa], wbuf.at[zl, :, qa], w_send.at[0], w_recv.at[0], (tm, partner_row)),
-        rcopy(w_hbm.at[:, qa + 1], wbuf.at[zl, :, qa + 1], w_send.at[1], w_recv.at[1],
-              (outer_tm, partner_row)),
-    ]
-    for c in w_out:
-        c.start()
+    x_par = (tm // 4) % 2
+    x_up, x_down = (tm + 4) % 16, (tm + 12) % 16
+    oz = 1 - zl
+    e_own = core * 4 + x_par * 2
+    e_x = core * 4 + (1 - x_par) * 2
+    e_cores = ((1 - core) * 4 + x_par * 2, (1 - core) * 4 + (1 - x_par) * 2)
+
+    def wz_copy(p, i, side):
+        dev = ((tm, partner_row), (outer_tm, partner_row))[i]
+        return rcopy(w_hbm.at[p, e_own + i], wbuf.at[side, p, e_own + i],
+                     wz_send.at[p, i], wz_recv.at[p, i], dev)
+
+    def wx_copy(p, i, e):
+        dev = ((x_up, row), (x_down, row))[i]
+        return rcopy(wbuf.at[oz, p, e + i], wbuf.at[oz, p, e + i],
+                     wx_send.at[p, i], wx_recv.at[p, i], dev)
+
+    def wc_copy(p, j, e):
+        pair = wbuf.at[oz, p, pl.ds(e, 2)]
+        return rcopy(pair, pair, wc_send.at[p, j], wc_recv.at[p, j], (other_core, row))
+
+    for p in range(3):
+        for i in range(2):
+            wz_copy(p, i, zl).start()
 
     load_stream.wait()
 
@@ -133,38 +149,53 @@
     same = (clip_r == clip_c) & (r_i % 4 == c_i % 4)
     mask[...] = jnp.where(same, 0.0, -1e30).astype(F32)
 
-    def project(yb, pz):
+    def project_part(yb, pz, part):
         kk = (pz + hz) % 2
         slot = kk * 2 + (1 - kk) * zl
-
+        qkv[yb, slot, part] = dot(xg[yb], wbuf[pz, part].reshape(3072, 256)).astype(BF)
+
+    def zcopy(yb, d, part, slot):
+        return rcopy(qkv.at[yb, 2, part], qkv.at[yb, slot, part], z_send.at[d, part],
+                     z_recv.at[d, part], (tm, partner_row))
+
+    def project(yb, d):
         @pl.loop(0, 3)
         def _(part):
-            acc = dot(xg[yb, :, 0:768], wbuf[pz, part, 0])
-            for q in range(1, 4):
-                acc = acc + dot(xg[yb, :, q * 768:(q + 1) * 768], wbuf[pz, part, q])
-            qkv[yb, slot, part] = acc.astype(BF)
-
-    def zcopy(yb, d):
-        return rcopy(qkv.at[yb, 2], qkv.at[yb, zl], z_send.at[d], z_recv.at[d], (tm, partner_row))
+            project_part(yb, 1 - hz, part)
+            zcopy(yb, d, part, zl).start()
+
+        @pl.loop(0, 3)
+        def _(part):
+            project_part(yb, hz, part)
 
     def tcopy(yb, d, zz, t, at):
         return rcopy(tsend.at[yb, zz, :, t], trecv.at[yb, zz, :, at], t_send.at[d, zz, t],
                      t_recv.at[d, zz, at], time_peer(t))
 
-    def stage_time(yb, d, zz):
-        @pl.loop(0, 3)
-        def _(part):
-            moved = dot(perm[...], qkv[yb, zz, part]).astype(BF)
-            tsend[yb, zz, part] = moved.reshape(16, 16, 256)
-            trecv[yb, zz, part, tm] = tsend[yb, zz, part, tm]
-
+    def stage_part(yb, zz, part):
+        moved = dot(perm[...], qkv[yb, zz, part]).astype(BF)
+        tsend[yb, zz, part] = moved.reshape(16, 16, 256)
+        trecv[yb, zz, part, tm] = tsend[yb, zz, part, tm]
+
+    def send_time(yb, d, zz):
         @pl.loop(1, 16)
         def _(k):
             tcopy(yb, d, zz, (tm + k) % 16, tm).start()
 
+    def stage_own(yb, d):
+        @pl.loop(0, 3)
+        def _(part):
+            stage_part(yb, zl, part)
+
+        send_time(yb, d, zl)
+
     def stage_partner(yb, d):
-        rcopy(qkv.at[yb, 2], qkv.at[yb, 1 - zl], z_send.at[d], z_recv.at[d], (tm, partner_row)).wait_recv()
-        stage_time(yb, d, 1 - zl)
+        @pl.loop(0, 3)
+        def _(part):
+            zcopy(yb, d, part, 1 - zl).wait_recv()
+            stage_part(yb, 1 - zl, part)
+
+        send_time(yb, d, 1 - zl)
 
     factor = LOG2E / math.sqrt(HD)
 
@@ -257,49 +288,43 @@
                     out_ref[f, :, cols] = acc[f] * mod_ref[2, pl.ds(clip, 1), cols]
 
     load_w.wait()
-    project(y, zl)
-
-    oz = 1 - zl
-    for i in range(2):
-        rcopy(w_hbm.at[:, qa + i], wbuf.at[oz, :, qa + i], w_send.at[i], w_recv.at[i],
-              (tm, partner_row)).wait_recv()
-        rcopy(wbuf.at[oz, :, qa + i], wbuf.at[oz, :, qa + i], w_send.at[2 + i], w_recv.at[2 + i],
-              (other_core, row)).start()
+    for p in range(3):
+        for i in range(2):
+            wz_copy(p, i, oz).wait_recv()
+            wx_copy(p, i, e_own).start()
+        wc_copy(p, 0, e_own).start()
+        project_part(y, zl, p)
+    for p in range(3):
+        for i in range(2):
+            wx_copy(p, i, e_x).wait_recv()
+        wc_copy(p, 1, e_x).start()
     ycopy(ym, lo, 0, up).wait_recv()
     ycopy(ym, lo, 4, up).start()
     ycopy(yp, hi, 2, down).wait_recv()
     ycopy(yp, hi, 5, down).start()
-    qb = (1 - core) * 2
-    for i in range(2):
-        rcopy(wbuf.at[oz, :, qb + i], wbuf.at[oz, :, qb + i], w_send.at[2 + i], w_recv.at[2 + i],
-              (other_core, row)).wait_recv()
-
-    project(y, oz)
-    zcopy(y, 0).start()
-    stage_time(y, 0, zl)
+    for p in range(3):
+        for j in range(2):
+            wc_copy(p, j, e_cores[j]).wait_recv()
+        project_part(y, oz, p)
+        zcopy(y, 0, p, zl).start()
+    stage_own(y, 0)
 
     ycopy(ym, hi, 1, up).wait_recv()
-    project(ym, 1 - hz)
-    zcopy(ym, 1).start()
-    project(ym, hz)
-    stage_time(ym, 1, zl)
+    project(ym, 1)
+    stage_own(ym, 1)
     stage_partner(y, 0)
 
     ycopy(yp, lo, 3, down).wait_recv()
-    project(yp, 1 - hz)
-    zcopy(yp, 2).start()
-    project(yp, hz)
-    stage_time(yp, 2, zl)
+    project(yp, 2)
+    stage_own(yp, 2)
     stage_partner(ym, 1)
     temporal(y, 0)
     stage_partner(yp, 2)
 
     ycopy(yq, lo, 4, up).wait_recv()
     ycopy(yq, hi, 5, down).wait_recv()
-    project(yq, 1 - hz)
-    zcopy(yq, 3).start()
-    project(yq, hz)
-    stage_time(yq, 3, zl)
+    project(yq, 3)
+    stage_own(yq, 3)
     temporal(ym, 1)
     stage_partner(yq, 3)
     temporal(yp, 2)
@@ -318,15 +343,16 @@
     project_out(ym)
     project_out(yq, last=True)
 
-    for c in w_out:
-        c.wait_send()
-    for i in range(2):
-        rcopy(wbuf.at[oz, :, qa + i], wbuf.at[oz, :, qa + i], w_send.at[2 + i], w_recv.at[2 + i],
-              (other_core, row)).wait_send()
+    for p in range(3):
+        for i in range(2):
+            wz_copy(p, i, zl).wait_send()
+            wx_copy(p, i, e_own).wait_send()
+            wc_copy(p, i, e_own).wait_send()
     for i, (block, half) in enumerate(((y, lo), (y, hi), (y, hi), (y, lo), (ym, lo), (yp, hi))):
         ycopy(block, half, i, up).wait_send()
     for d, yb in enumerate((y, ym, yp, yq)):
-        zcopy(yb, d).wait_send()
+        for part in range(3):
+            zcopy(yb, d, part, zl).wait_send()
 
         @pl.loop(0, 30)
         def _(i, d=d, yb=yb):
@@ -347,13 +373,13 @@
     dma = pltpu.SemaphoreType.DMA
     return pl.pallas_call(
         attention_kernel,
-        out_shape=jax.ShapeDtypeStruct((4, 64, 3072), F32),
+        out_shape=pltpu.VMEM((4, 64, 3072), F32),
         in_specs=[pl.BlockSpec(memory_space=pltpu.SMEM), hbm, vmem, hbm, hbm],
         out_specs=vmem,
         scratch_shapes=[
             pltpu.VMEM((4, 64, 3072), F32),
             pltpu.VMEM((4, 256, 3072), BF),
-            pltpu.VMEM((2, 3, 4, 768, 256), BF),
+            pltpu.VMEM((2, 3, 8, 384, 256), BF),
             pltpu.VMEM((8, 256, 3072), BF),
             pltpu.VMEM((4, 3, 3, 256, 256), BF),
             pltpu.VMEM((4, 2, 3, 16, 16, 256), BF),
@@ -368,8 +394,10 @@
             pltpu.VMEM((256, 256), F32),
             dma((3,)),
             dma((6,)), dma((6,)),
-            dma((4,)), dma((4,)),
-            dma((4,)), dma((4,)),
+            dma((3, 2)), dma((3, 2)),
+            dma((3, 2)), dma((3, 2)),
+            dma((3, 2)), dma((3, 2)),
+            dma((4, 3)), dma((4, 3)),
             dma((4, 2, 16)), dma((4, 2, 16)),
             dma((4, 16)), dma((4, 16)),
             dma((8,)), dma((8,)),
@@ -383,7 +411,7 @@
 
 def per_device(stream, clip_ids, modulation, qkv_weight, out_weight):
     mod = jnp.transpose(modulation, (1, 0, 2))
-    weight = jnp.transpose(qkv_weight, (1, 0, 2)).reshape(3, 4, 768, 256)
+    weight = jnp.transpose(qkv_weight, (1, 0, 2)).reshape(3, 8, 384, 256)
     return attention(clip_ids, stream, mod, weight, out_weight.reshape(8, 256, 3072))
 
 

time: 128 us -> 116 us (0.906); the launches traced: 126 us -> 116 us
  Pallas kernels: 122 us -> 114 us
  local copies, waits for them, and re-layouts: 3.89 us -> 1.67 us
    pallas_call x1, Pallas kernels: 122 us -> 114 us  [attention(): pl.pallas_call(attention_kernel, out_shape=pltpu.VMEM((4, 64, 3072), F32)...]
    unnamed x1, local copies, waits for them, and re-layouts: 3.89 us -> 1.67 us
where the time goes in v3:
time: 116 us
  Pallas kernels  114 us (98%)
  local copies, waits for them, and re-layouts  1.67 us (1%)
    pallas_call x1, Pallas kernels, attention(): pl.pallas_call(attention_kernel, out_shape=pltpu.VMEM((4, 64, 3072), F32)...  114 us

profile of v3, /device:TPU:32, one launch (start us, length us, event | category | flops | bytes accessed | tf_op | source)
XLA Modules:
  0.0 116.0 jit_solution(5678637468193538496)
XLA Ops:
  0.0 114.4 %attention.1 = f32[4,64,3072]{2,1,0:T(8,128)S(1)} custom-call(s32[64]{0:T(128)} %clip_ref.1, f32[4,64,3072]{2,1,0:T(8,128)} %stream_hbm.1, f32[3,8,3072]{2,1,0:T(8,128)} %bitcast.7, bf16[3,8,384,256]{3,2,1,0:T(8,128)(2,1)} %bitcast.6, bf16[8,256,3072]{2,1,0:T(8,128)(2,1)} %bitcast.5), custom_call_target="tpu_custom_call" | custom-call | tf_op jit(solution)/shard_map/attention/pallas_call | solution.py:374
  114.4 1.7 %copy.7 = f32[4,64,3072]{2,1,0:T(8,128)} copy(f32[4,64,3072]{2,1,0:T(8,128)S(1)} %attention.1) | data formatting | bytes 6291456

commit v4 on v3

--- a/solution.py
+++ b/solution.py
@@ -25,8 +25,8 @@
 
 def attention_kernel(
     clip_ref, stream_hbm, mod_ref, w_hbm, wo_hbm, out_ref,
-    stream_v, xg, wbuf, wo, qkv, tsend, trecv, osend, orecv, csend, comb, sp, perm, perm_t, mask,
-    load_sem, y_send, y_recv, wz_send, wz_recv, wx_send, wx_recv, wc_send, wc_recv, z_send, z_recv, t_send, t_recv,
+    stream_v, xg, wbuf, wo, qkv, tsend, trecv, osend, orecv, csend, comb, relay, sp, perm, perm_t, mask,
+    load_sem, y_send, y_recv, wz_send, wz_recv, wx_send, wx_recv, wc_send, wc_recv, z_send, z_recv, t_send, t_recv, b_send, b_recv, f_send,
     o_send, o_recv, c_send, c_recv,
 ):
     tm = lax.axis_index("tm")
@@ -72,6 +72,7 @@
 
     x_par = (tm // 4) % 2
     x_up, x_down = (tm + 4) % 16, (tm + 12) % 16
+    x_far = ((tm // 4 + 2) % 4) * 4
     oz = 1 - zl
     e_own = core * 4 + x_par * 2
     e_x = core * 4 + (1 - x_par) * 2
@@ -187,7 +188,25 @@
         def _(part):
             stage_part(yb, zl, part)
 
-        send_time(yb, d, zl)
+        @pl.loop(0, 11)
+        def _(k):
+            m = (5 + tm % 4 + k) % 12
+            tcopy(yb, d, zl, (x_far + 4 + m) % 16, tm).start()
+
+        bundle(yb, d).start()
+
+    def bundle(yb, d):
+        return rcopy(tsend.at[yb, zl, :, pl.ds(x_far, 4)], relay.at[d], b_send.at[d], b_recv.at[d],
+                     (x_down, row))
+
+    def fcopy(yb, d, j):
+        return rcopy(relay.at[d, :, j], trecv.at[yb, zl, :, x_up], f_send.at[d, j],
+                     t_recv.at[d, zl, x_up], time_peer((x_down // 4) * 4 + j))
+
+    def pass_on(yb, d):
+        bundle(yb, d).wait_recv()
+        for j in range(4):
+            fcopy(yb, d, j).start()
 
     def stage_partner(yb, d):
         @pl.loop(0, 3)
@@ -312,13 +331,16 @@
     ycopy(ym, hi, 1, up).wait_recv()
     project(ym, 1)
     stage_own(ym, 1)
+    pass_on(y, 0)
     stage_partner(y, 0)
 
     ycopy(yp, lo, 3, down).wait_recv()
     project(yp, 2)
     stage_own(yp, 2)
+    pass_on(ym, 1)
     stage_partner(ym, 1)
     temporal(y, 0)
+    pass_on(yp, 2)
     stage_partner(yp, 2)
 
     ycopy(yq, lo, 4, up).wait_recv()
@@ -326,6 +348,7 @@
     project(yq, 3)
     stage_own(yq, 3)
     temporal(ym, 1)
+    pass_on(yq, 3)
     stage_partner(yq, 3)
     temporal(yp, 2)
     spatial()
@@ -354,9 +377,18 @@
         for part in range(3):
             zcopy(yb, d, part, zl).wait_send()
 
-        @pl.loop(0, 30)
-        def _(i, d=d, yb=yb):
-            tcopy(yb, d, i // 15, (tm + 1 + i % 15) % 16, tm).wait_send()
+        @pl.loop(0, 11)
+        def _(k, d=d, yb=yb):
+            m = (5 + tm % 4 + k) % 12
+            tcopy(yb, d, zl, (x_far + 4 + m) % 16, tm).wait_send()
+
+        bundle(yb, d).wait_send()
+        for j in range(4):
+            fcopy(yb, d, j).wait_send()
+
+        @pl.loop(1, 16)
+        def _(k, d=d, yb=yb):
+            tcopy(yb, d, 1 - zl, (tm + k) % 16, tm).wait_send()
 
         @pl.loop(1, 16)
         def _(k, d=d, yb=yb):
@@ -388,6 +420,7 @@
             pltpu.VMEM((4, 2, 16, 16, 256), BF),
             pltpu.VMEM((8, 256, 256), BF),
             pltpu.VMEM((8, 256, 256), BF),
+            pltpu.VMEM((4, 3, 4, 16, 256), BF),
             pltpu.VMEM((4, 2, 256, 256), F32),
             pltpu.VMEM((256, 256), BF),
             pltpu.VMEM((256, 256), BF),
@@ -399,6 +432,7 @@
             dma((3, 2)), dma((3, 2)),
             dma((4, 3)), dma((4, 3)),
             dma((4, 2, 16)), dma((4, 2, 16)),
+            dma((4,)), dma((4,)), dma((4, 4)),
             dma((4, 16)), dma((4, 16)),
             dma((8,)), dma((8,)),
         ],

time: 116 us -> 125 us (1.078)
  Pallas kernels: 114 us -> 123 us
    pallas_call x1, Pallas kernels: 114 us -> 123 us  [attention(): pl.pallas_call(attention_kernel, out_shape=pltpu.VMEM((4, 64, 3072), F32)...]
where the time goes in v4:
time: 125 us
  Pallas kernels  123 us (98%)
  local copies, waits for them, and re-layouts  1.67 us (1%)
    pallas_call x1, Pallas kernels, attention(): pl.pallas_call(attention_kernel, out_shape=pltpu.VMEM((4, 64, 3072), F32)...  123 us

profile of v4, /device:TPU:32, one launch (start us, length us, event | category | flops | bytes accessed | tf_op | source)
XLA Modules:
  0.0 124.6 jit_solution(16162300156509457840)
XLA Ops:
  0.0 122.9 %attention.1 = f32[4,64,3072]{2,1,0:T(8,128)S(1)} custom-call(s32[64]{0:T(128)} %clip_ref.1, f32[4,64,3072]{2,1,0:T(8,128)} %stream_hbm.1, f32[3,8,3072]{2,1,0:T(8,128)} %bitcast.7, bf16[3,8,384,256]{3,2,1,0:T(8,128)(2,1)} %bitcast.6, bf16[8,256,3072]{2,1,0:T(8,128)(2,1)} %bitcast.5), custom_call_target="tpu_custom_call" | custom-call | tf_op jit(solution)/shard_map/attention/pallas_call | solution.py:406
  122.9 1.7 %copy.7 = f32[4,64,3072]{2,1,0:T(8,128)} copy(f32[4,64,3072]{2,1,0:T(8,128)S(1)} %attention.1) | data formatting | bytes 6291456

commit v5 on v3

v5 whole, which is shorter than its diff:
```python
import math

import jax
import jax.numpy as jnp
from jax import lax
from jax.experimental import pallas as pl
from jax.experimental.pallas import tpu as pltpu
from jax.sharding import PartitionSpec as P

HD = 128
MESH = pl.DeviceIdType.MESH
BF = jnp.bfloat16
F32 = jnp.float32
LOG2E = 1.4426950408889634


def dot(a, b):
    return jnp.dot(a, b, preferred_element_type=F32)


def dot_nt(a, b):
    return lax.dot_general(a, b, (((1,), (1,)), ((), ())), preferred_element_type=F32)


def attention_kernel(
    clip_ref, stream_hbm, mod_ref, w_hbm, wo_hbm, out_ref,
    stream_v, xg, wbuf, wo, qkv, tsend, trecv, osend, orecv, csend, comb, sp, perm, perm_t, mask,
    load_sem, y_send, y_recv, wz_send, wz_recv, wx_send, wx_recv, wc_send, wc_recv, z_send, z_recv,
    t_send, t_recv, o_send, o_recv, c_send, c_recv,
):
    batches = ((0, 2), (2, 2), (4, 2), (6, 1), (7, 1))
    tm = lax.axis_index("tm")
    row = lax.axis_index("row")
    zh = (tm // 2) % 2
    core = tm % 2
    y = row // 2
    zl = row % 2
    hz = (zl + zh) % 2
    oz = 1 - zl
    partner_row = y * 2 + oz
    outer_tm = tm + 2 - 4 * zh
    other_core = tm + 1 - 2 * core
    ym, yp, yq = (y + 3) % 4, (y + 1) % 4, (y + 2) % 4
    up, down = (tm, yp * 2 + zl), (tm, ym * 2 + zl)
    y_of = (y, y, ym, yp, ym, yp, yq, yq)
    half_of = (0, 1, 0, 0, 1, 1, 0, 1)

    def rcopy(src, dst, send, recv, dev):
        return pltpu.make_async_remote_copy(
            src_ref=src, dst_ref=dst, send_sem=send, recv_sem=recv,
            device_id=dev, device_id_type=MESH,
        )

    def await_bytes(ref, sem):
        pltpu.make_async_copy(ref, ref, sem).wait()

    def time_peer(t):
        return (t, y * 2 + (hz + (t // 2) % 2) % 2)

    load_stream = pltpu.make_async_copy(stream_hbm, stream_v, load_sem.at[0])
    load_stream.start()
    load_w = pltpu.make_async_copy(w_hbm, wbuf.at[zl], load_sem.at[1])
    load_w.start()
    load_wo = pltpu.make_async_copy(wo_hbm, wo, load_sem.at[2])
    load_wo.start()

    barrier = pltpu.get_barrier_semaphore()

    @pl.loop(1, 16)
    def _(k):
        pl.semaphore_signal(barrier, inc=1, device_id=time_peer((tm + k) % 16), device_id_type=MESH)

    @pl.loop(1, 8)
    def _(k):
        pl.semaphore_signal(barrier, inc=1, device_id=(tm, (row + k) % 8), device_id_type=MESH)

    pl.semaphore_wait(barrier, 22)

    x_par = (tm // 4) % 2
    x_up, x_down = (tm + 4) % 16, (tm + 12) % 16
    e_own = core * 4 + x_par * 2
    e_x = core * 4 + (1 - x_par) * 2
    e_cores = ((1 - core) * 4 + x_par * 2, (1 - core) * 4 + (1 - x_par) * 2)

    def wz_copy(p, i, side):
        dev = ((tm, partner_row), (outer_tm, partner_row))[i]
        return rcopy(w_hbm.at[p, e_own + i], wbuf.at[side, p, e_own + i],
                     wz_send.at[p, i], wz_recv.at[p, i], dev)

    def wx_copy(p, i, e):
        dev = ((x_up, row), (x_down, row))[i]
        return rcopy(wbuf.at[oz, p, e + i], wbuf.at[oz, p, e + i],
                     wx_send.at[p, i], wx_recv.at[p, i], dev)

    def wc_copy(p, j, e):
        pair = wbuf.at[oz, p, pl.ds(e, 2)]
        return rcopy(pair, pair, wc_send.at[p, j], wc_recv.at[p, j], (other_core, row))

    for p in range(3):
        for i in range(2):
            wz_copy(p, i, zl).start()

    load_stream.wait()

    def norm(unit):
        @pl.loop(0, 4)
        def _(f):
            clip = clip_ref[tm * 4 + f]
            shift = mod_ref[0, pl.ds(clip, 1), :]
            scale = 1.0 + mod_ref[1, pl.ds(clip, 1), :]
            v = stream_v[f, pl.ds(unit * 32, 32), :]
            centred = v - jnp.mean(v, axis=-1, keepdims=True)
            var = jnp.mean(centred * centred, axis=-1, keepdims=True)
            n = centred * lax.rsqrt(var + 1e-06) * scale + shift
            xg[unit, pl.ds(f * 32, 32), :] = n.astype(BF)

    def ycopy(i, src, dst, half, dev):
        if half is None:
            return rcopy(xg.at[src], xg.at[dst], y_send.at[i], y_recv.at[i], dev)
        rows = pl.ds(half * 64, 64)
        return rcopy(xg.at[src, rows], xg.at[dst, rows], y_send.at[i], y_recv.at[i], dev)

    y_copies = [
        ycopy(0, 0, 2, None, up), ycopy(1, 0, 3, None, down),
        ycopy(2, 1, 4, None, up), ycopy(3, 1, 5, None, down),
        ycopy(4, 2, 6, 0, up), ycopy(5, 3, 6, 1, down),
        ycopy(6, 4, 7, 0, up), ycopy(7, 5, 7, 1, down),
    ]
    for unit in range(2):
        norm(unit)
        y_copies[2 * unit].start()
        y_copies[2 * unit + 1].start()

    def unit_row(j):
        return (j // 128) * 128 + ((j // 4) % 4) * 32 + ((j // 16) % 8) * 4 + j % 4

    r_i = lax.broadcasted_iota(jnp.int32, (256, 256), 0)
    c_i = lax.broadcasted_iota(jnp.int32, (256, 256), 1)
    perm[...] = (unit_row(r_i) == c_i).astype(BF)
    perm_t[...] = (unit_row(c_i) == r_i).astype(BF)
    fr = r_i // 4
    fc = c_i // 4

    def clip_of(f, carry):
        a, b = carry
        c = clip_ref[f]
        return jnp.where(fr == f, c, a), jnp.where(fc == f, c, b)

    zero = jnp.zeros((256, 256), jnp.int32)
    clip_r, clip_c = lax.fori_loop(0, 64, clip_of, (zero, zero))
    same = (clip_r == clip_c) & (r_i % 4 == c_i % 4)
    mask[...] = jnp.where(same, 0.0, -1e30).astype(F32)

    def project_part(b, pz, part):
        k, n = batches[b]
        kk = (pz + hz) % 2
        slot = kk * 2 + (1 - kk) * zl
        x = xg[k:k + n].reshape(n * 128, 3072)
        out = dot(x, wbuf[pz, part].reshape(3072, 256)).astype(BF)
        qkv[slot, part, k:k + n] = out.reshape(n, 128, 256)

    def zcopy(b, part, slot):
        k, n = batches[b]
        units = pl.ds(k, n)
        return rcopy(qkv.at[2, part, units], qkv.at[slot, part, units], z_send.at[b, part],
                     z_recv.at[b, part], (tm, partner_row))

    def project(b):
        @pl.loop(0, 3)
        def _(part):
            project_part(b, 1 - hz, part)
            zcopy(b, part, zl).start()

        @pl.loop(0, 3)
        def _(part):
            project_part(b, hz, part)

    def stage_part(b, zz, part):
        k, n = batches[b]
        rows = qkv[zz, part, k:k + n].reshape(n * 128, 256)
        moved = dot(perm[:n * 128, :n * 128], rows).astype(BF).reshape(n, 8, 16, 256)
        tsend[k:k + n, part, pl.ds(zz * 8, 8)] = moved

    def send_time(b, zz):
        k, n = batches[b]
        units = pl.ds(k, n)

        @pl.loop(0, 8)
        def _(i):
            t = zz * 8 + (tm + i) % 8

            @pl.when(t != tm)
            def _():
                rcopy(tsend.at[units, :, t], trecv.at[units, :, tm], t_send.at[b], t_recv.at[b],
                      time_peer(t)).start()

            @pl.when(t == tm)
            def _():
                trecv[k:k + n, :, tm] = tsend[k:k + n, :, tm]

    def stage_own(b):
        @pl.loop(0, 3)
        def _(part):
            stage_part(b, zl, part)

        send_time(b, zl)

    def stage_partner(b):
        @pl.loop(0, 3)
        def _(part):
            zcopy(b, part, oz).wait_recv()
            stage_part(b, oz, part)

        send_time(b, oz)

    factor = LOG2E / math.sqrt(HD)

    def soften(s):
        p = jnp.exp2((s - jnp.max(s, axis=-1, keepdims=True)) * factor)
        return p, jnp.sum(p, axis=-1, keepdims=True)

    def temporal(b):
        k, n = batches[b]
        units = pl.ds(k, n)
        await_bytes(trecv.at[units, :, pl.ds(0, 15)], t_recv.at[b])
        for u in range(k, k + n):
            for h in range(2):
                cols = slice(h * HD, (h + 1) * HD)
                q, kk, v = (trecv[u, part, :, :, cols].reshape(256, HD) for part in range(3))
                p, total = soften(dot_nt(q, kk) + mask[...])
                o = dot(p.astype(BF), v) / total
                osend[u, :, :, cols] = o.astype(BF).reshape(16, 16, HD)
        orecv[k:k + n, tm] = osend[k:k + n, tm]

        @pl.loop(1, 16)
        def _(i):
            t = (tm + i) % 16
            rcopy(osend.at[units, t], orecv.at[units, tm], o_send.at[b], o_recv.at[b],
                  time_peer(t)).start()

    def wait_back(b):
        k, n = batches[b]
        await_bytes(orecv.at[pl.ds(k, n), pl.ds(0, 15)], o_recv.at[b])

    def spatial(k):
        @pl.loop(0, 4)
        def _(f):
            rows = pl.ds(pl.multiple_of(f * 32, 32), 32)
            for h in range(2):
                cols = slice(h * HD, (h + 1) * HD)
                q = qkv[0:2, 0, k:k + 2, rows, cols].reshape(128, HD)
                kk, v = (qkv[0:2, part, :, rows, cols].reshape(512, HD) for part in (1, 2))
                p, total = soften(dot_nt(q, kk))
                o = dot(p.astype(BF), v) / total
                sp[:, k:k + 2, rows, cols] = o.reshape(2, 2, 32, HD)

    def ccopy(u, r, at, kept):
        half = half_of[u]
        return rcopy(csend.at[u, r % 2], comb.at[kept, half], c_send.at[u, r % 2], c_recv.at[at, half],
                     (tm, r))

    def combine(u):
        for zz in range(2):
            back = dot(perm_t[:128, :128], orecv[u, zz * 8:(zz + 1) * 8].reshape(128, 256))
            csend[u, zz] = (sp[zz, u] + back).astype(BF)
        if u < 2:
            ccopy(u, partner_row, row, y * 2 + hz).start()
            comb[y * 2 + hz, u] = csend[u, zl]
        else:
            for zz in range(2):
                ccopy(u, y_of[u] * 2 + zz, row, y * 2 + hz).start()

    def project_out(ys, first=False, last=False):
        for i in range(2):
            r = ys * 2 + i
            for half in range(2):
                def wait(r=r, half=half):
                    dst = comb.at[ys * 2 + (r + zh) % 2, half]
                    rcopy(csend.at[0, 0], dst, c_send.at[0, 0], c_recv.at[r, half], (tm, r)).wait_recv()
                if first:
                    pl.when(i != zl)(wait)
                else:
                    wait()

        @pl.loop(0, 6)
        def _(n):
            cols = pl.ds(pl.multiple_of(n * 512, 512), 512)
            acc = dot(comb[2 * ys].reshape(256, 256), wo[2 * ys, :, cols])
            acc = acc + dot(comb[2 * ys + 1].reshape(256, 256), wo[2 * ys + 1, :, cols])
            for half in range(2):
                for f in range(4):
                    at = (half * 4 + f) * 32
                    rows = slice(half * 32, (half + 1) * 32)
                    piece = acc[at:at + 32]
                    if not first:
                        piece = piece + out_ref[f, rows, cols]
                    if last:
                        clip = clip_ref[tm * 4 + f]
                        piece = piece * mod_ref[2, pl.ds(clip, 1), cols]
                    out_ref[f, rows, cols] = piece

    load_w.wait()
    for p in range(3):
        for i in range(2):
            wz_copy(p, i, oz).wait_recv()
            wx_copy(p, i, e_own).start()
        wc_copy(p, 0, e_own).start()
        project_part(0, zl, p)
    for p in range(3):
        for i in range(2):
            wx_copy(p, i, e_x).wait_recv()
        wc_copy(p, 1, e_x).start()
    for p in range(3):
        for j in range(2):
            wc_copy(p, j, e_cores[j]).wait_recv()
        project_part(0, oz, p)
        zcopy(0, p, zl).start()
    for i in range(2):
        y_copies[i].wait_recv()
        y_copies[4 + i].start()
    stage_own(0)
    project(1)
    stage_own(1)
    stage_partner(0)

    for i in range(2):
        y_copies[2 + i].wait_recv()
        y_copies[6 + i].start()
    project(2)
    stage_own(2)
    stage_partner(1)
    temporal(0)

    y_copies[4].wait_recv()
    y_copies[5].wait_recv()
    project(3)
    stage_own(3)
    stage_partner(2)
    temporal(1)

    y_copies[6].wait_recv()
    y_copies[7].wait_recv()
    project(4)
    stage_own(4)
    stage_partner(3)
    temporal(2)
    stage_partner(4)
    temporal(3)

    spatial(2)
    wait_back(1)
    combine(2)
    combine(3)
    spatial(4)
    wait_back(2)
    combine(4)
    combine(5)
    temporal(4)
    spatial(6)
    wait_back(3)
    combine(6)
    spatial(0)
    wait_back(0)
    combine(0)
    combine(1)
    wait_back(4)
    combine(7)
    load_wo.wait()
    project_out(y, first=True)
    project_out(yp)
    project_out(ym)
    project_out(yq, last=True)

    for p in range(3):
        for i in range(2):
            wz_copy(p, i, zl).wait_send()
            wx_copy(p, i, e_own).wait_send()
            wc_copy(p, i, e_own).wait_send()
    for c in y_copies:
        c.wait_send()
    for b, (k, n) in enumerate(batches):
        for part in range(3):
            zcopy(b, part, zl).wait_send()
        await_bytes(tsend.at[pl.ds(k, n), :, pl.ds(0, 15)], t_send.at[b])
        await_bytes(osend.at[pl.ds(k, n), pl.ds(0, 15)], o_send.at[b])
    for u in range(8):
        if u < 2:
            ccopy(u, partner_row, row, y * 2 + hz).wait_send()
        else:
            for zz in range(2):
                ccopy(u, y_of[u] * 2 + zz, row, y * 2 + hz).wait_send()


def attention(clip_ids, stream, mod, weight, out_weight):
    vmem = pl.BlockSpec(memory_space=pltpu.VMEM)
    hbm = pl.BlockSpec(memory_space=pl.ANY)
    dma = pltpu.SemaphoreType.DMA
    return pl.pallas_call(
        attention_kernel,
        out_shape=pltpu.VMEM((4, 64, 3072), F32),
        in_specs=[pl.BlockSpec(memory_space=pltpu.SMEM), hbm, vmem, hbm, hbm],
        out_specs=vmem,
        scratch_shapes=[
            pltpu.VMEM((4, 64, 3072), F32),
            pltpu.VMEM((8, 128, 3072), BF),
            pltpu.VMEM((2, 3, 8, 384, 256), BF),
            pltpu.VMEM((8, 256, 3072), BF),
            pltpu.VMEM((3, 3, 8, 128, 256), BF),
            pltpu.VMEM((8, 3, 16, 16, 256), BF),
            pltpu.VMEM((8, 3, 16, 16, 256), BF),
            pltpu.VMEM((8, 16, 16, 256), BF),
            pltpu.VMEM((8, 16, 16, 256), BF),
            pltpu.VMEM((8, 2, 128, 256), BF),
            pltpu.VMEM((8, 2, 128, 256), BF),
            pltpu.VMEM((2, 8, 128, 256), F32),
            pltpu.VMEM((256, 256), BF),
            pltpu.VMEM((256, 256), BF),
            pltpu.VMEM((256, 256), F32),
            dma((3,)),
            dma((8,)), dma((8,)),
            dma((3, 2)), dma((3, 2)),
            dma((3, 2)), dma((3, 2)),
            dma((3, 2)), dma((3, 2)),
            dma((5, 3)), dma((5, 3)),
            dma((5,)), dma((5,)),
            dma((5,)), dma((5,)),
            dma((8, 2)), dma((8, 2)),
        ],
        compiler_params=pltpu.CompilerParams(
            collective_id=0, has_side_effects=True, vmem_limit_bytes=60 * 1024 * 1024
        ),
        name="attention",
    )(clip_ids, stream, mod, weight, out_weight)


def per_device(stream, clip_ids, modulation, qkv_weight, out_weight):
    mod = jnp.transpose(modulation, (1, 0, 2))
    weight = jnp.transpose(qkv_weight, (1, 0, 2)).reshape(3, 8, 384, 256)
    return attention(clip_ids, stream, mod, weight, out_weight.reshape(8, 256, 3072))


def solution(mesh):
    placed = (P("tm", "row", None), P(), P(), P(None, None, "row"), P())
    return jax.shard_map(
        per_device, mesh=mesh, in_specs=placed, out_specs=P("tm", "row", None), check_vma=False
    )
```

time: 116 us -> 115 us (level)
  the two profiles are of different devices: /device:TPU:32 before, /device:TPU:71 now
where the time goes in v5:
time: 115 us
  Pallas kernels  113 us (98%)
  local copies, waits for them, and re-layouts  1.67 us (1%)
    pallas_call x1, Pallas kernels, attention(): pl.pallas_call(attention_kernel, out_shape=pltpu.VMEM((4, 64, 3072), F32)...  113 us

profile of v5, /device:TPU:71, one launch (start us, length us, event | category | flops | bytes accessed | tf_op | source)
XLA Modules:
  0.0 114.9 jit_solution(14642656122833620659)
XLA Ops:
  0.0 113.2 %attention.1 = f32[4,64,3072]{2,1,0:T(8,128)S(1)} custom-call(s32[64]{0:T(128)} %clip_ref.1, f32[4,64,3072]{2,1,0:T(8,128)} %stream_hbm.1, f32[3,8,3072]{2,1,0:T(8,128)} %bitcast.7, bf16[3,8,384,256]{3,2,1,0:T(8,128)(2,1)} %bitcast.6, bf16[8,256,3072]{2,1,0:T(8,128)(2,1)} %bitcast.5), custom_call_target="tpu_custom_call" | custom-call | tf_op jit(solution)/shard_map/attention/pallas_call | solution.py:398
  113.2 1.7 %copy.7 = f32[4,64,3072]{2,1,0:T(8,128)} copy(f32[4,64,3072]{2,1,0:T(8,128)S(1)} %attention.1) | data formatting | bytes 6291456

commit v6 on v5

--- a/solution.py
+++ b/solution.py
@@ -54,29 +54,38 @@
     def await_bytes(ref, sem):
         pltpu.make_async_copy(ref, ref, sem).wait()
 
-    def time_peer(t):
-        return (t, y * 2 + (hz + (t // 2) % 2) % 2)
-
-    load_stream = pltpu.make_async_copy(stream_hbm, stream_v, load_sem.at[0])
-    load_stream.start()
-    load_w = pltpu.make_async_copy(w_hbm, wbuf.at[zl], load_sem.at[1])
-    load_w.start()
-    load_wo = pltpu.make_async_copy(wo_hbm, wo, load_sem.at[2])
-    load_wo.start()
+    x = tm // 4
+    xs = [((x + d) % 4) for d in range(4)]
+    zs = [zh, 1 - zh]
+    cs = [core, 1 - core]
+    rows_of = [y * 2 + (hz + zh) % 2, y * 2 + (hz + 1 - zh) % 2]
+    offsets = [(dx, dz, dc) for dx in (1, 3, 2, 0) for dz in range(2) for dc in range(2)][:-4]
+    offsets = offsets + [(0, 1, 0), (0, 1, 1), (0, 0, 1)]
+    me_at = core * 8 + x * 2 + zh
+
+    def peer(dx, dz, dc):
+        t = xs[dx] * 4 + zs[dz] * 2 + cs[dc]
+        return (t, rows_of[dz]), cs[dc] * 8 + xs[dx] * 2 + zs[dz]
+
+    load_stream = [
+        pltpu.make_async_copy(stream_hbm.at[:, pl.ds(32 * u, 32)], stream_v.at[:, pl.ds(32 * u, 32)],
+                              load_sem.at[u])
+        for u in range(2)
+    ]
+    load_w = pltpu.make_async_copy(w_hbm, wbuf.at[zl], load_sem.at[2])
+    load_wo = pltpu.make_async_copy(wo_hbm, wo, load_sem.at[3])
+    for c in load_stream:
+        c.start()
 
     barrier = pltpu.get_barrier_semaphore()
-
-    @pl.loop(1, 16)
-    def _(k):
-        pl.semaphore_signal(barrier, inc=1, device_id=time_peer((tm + k) % 16), device_id_type=MESH)
-
-    @pl.loop(1, 8)
-    def _(k):
-        pl.semaphore_signal(barrier, inc=1, device_id=(tm, (row + k) % 8), device_id_type=MESH)
-
+    for o in offsets:
+        pl.semaphore_signal(barrier, inc=1, device_id=peer(*o)[0], device_id_type=MESH)
+    row_peers = [(tm, r * 2 + (zl if i == 0 else oz)) for r in (y, ym, yp, yq) for i in range(2)][1:]
+    for dev in row_peers:
+        pl.semaphore_signal(barrier, inc=1, device_id=dev, device_id_type=MESH)
     pl.semaphore_wait(barrier, 22)
 
-    x_par = (tm // 4) % 2
+    x_par = x % 2
     x_up, x_down = (tm + 4) % 16, (tm + 12) % 16
     e_own = core * 4 + x_par * 2
     e_x = core * 4 + (1 - x_par) * 2
@@ -100,7 +109,6 @@
         for i in range(2):
             wz_copy(p, i, zl).start()
 
-    load_stream.wait()
 
     def norm(unit):
         @pl.loop(0, 4)
@@ -127,29 +135,28 @@
         ycopy(6, 4, 7, 0, up), ycopy(7, 5, 7, 1, down),
     ]
     for unit in range(2):
+        load_stream[unit].wait()
+        if unit == 0:
+            load_w.start()
         norm(unit)
         y_copies[2 * unit].start()
         y_copies[2 * unit + 1].start()
 
     def unit_row(j):
-        return (j // 128) * 128 + ((j // 4) % 4) * 32 + ((j // 16) % 8) * 4 + j % 4
+        return (j & 128) + ((j >> 2) & 3) * 32 + ((j >> 4) & 7) * 4 + (j & 3)
 
     r_i = lax.broadcasted_iota(jnp.int32, (256, 256), 0)
     c_i = lax.broadcasted_iota(jnp.int32, (256, 256), 1)
     perm[...] = (unit_row(r_i) == c_i).astype(BF)
     perm_t[...] = (unit_row(c_i) == r_i).astype(BF)
-    fr = r_i // 4
-    fc = c_i // 4
-
-    def clip_of(f, carry):
-        a, b = carry
-        c = clip_ref[f]
-        return jnp.where(fr == f, c, a), jnp.where(fc == f, c, b)
-
-    zero = jnp.zeros((256, 256), jnp.int32)
-    clip_r, clip_c = lax.fori_loop(0, 64, clip_of, (zero, zero))
-    same = (clip_r == clip_c) & (r_i % 4 == c_i % 4)
-    mask[...] = jnp.where(same, 0.0, -1e30).astype(F32)
+    lane = lax.broadcasted_iota(jnp.int32, (1, 256), 1)
+
+    def clip_of(f, found):
+        return jnp.where((lane >> 2) == f, clip_ref[f], found)
+
+    key = lax.fori_loop(0, 64, clip_of, jnp.zeros((1, 256), jnp.int32)) * 4 + (lane & 3)
+    key = jnp.broadcast_to(key.astype(F32), (256, 256))
+    mask[...] = jnp.where(key == key.T, 0.0, -1e30).astype(F32)
 
     def project_part(b, pz, part):
         k, n = batches[b]
@@ -184,19 +191,23 @@
     def send_time(b, zz):
         k, n = batches[b]
         units = pl.ds(k, n)
-
-        @pl.loop(0, 8)
-        def _(i):
-            t = zz * 8 + (tm + i) % 8
-
-            @pl.when(t != tm)
-            def _():
-                rcopy(tsend.at[units, :, t], trecv.at[units, :, tm], t_send.at[b], t_recv.at[b],
-                      time_peer(t)).start()
-
-            @pl.when(t == tm)
-            def _():
-                trecv[k:k + n, :, tm] = tsend[k:k + n, :, tm]
+        for dx in (1, 3, 2, 0):
+            for dz in (1, 0):
+                t = xs[dx] * 4 + zs[dz] * 2 + zz
+                at = zz * 8 + xs[dx] * 2 + zs[dz]
+
+                def send(t=t, at=at, dz=dz):
+                    rcopy(tsend.at[units, :, at], trecv.at[units, :, tm], t_send.at[b], t_recv.at[b],
+                          (t, rows_of[dz])).start()
+
+                def keep(at=at):
+                    trecv[k:k + n, :, tm] = tsend[k:k + n, :, at]
+
+                if (dx, dz) == (0, 0):
+                    pl.when(zz != core)(send)
+                    pl.when(zz == core)(keep)
+                else:
+                    send()
 
     def stage_own(b):
         @pl.loop(0, 3)
@@ -230,13 +241,10 @@
                 p, total = soften(dot_nt(q, kk) + mask[...])
                 o = dot(p.astype(BF), v) / total
                 osend[u, :, :, cols] = o.astype(BF).reshape(16, 16, HD)
-        orecv[k:k + n, tm] = osend[k:k + n, tm]
-
-        @pl.loop(1, 16)
-        def _(i):
-            t = (tm + i) % 16
-            rcopy(osend.at[units, t], orecv.at[units, tm], o_send.at[b], o_recv.at[b],
-                  time_peer(t)).start()
+        orecv[k:k + n, me_at] = osend[k:k + n, tm]
+        for o in offsets:
+            dev, _ = peer(*o)
+            rcopy(osend.at[units, dev[0]], orecv.at[units, me_at], o_send.at[b], o_recv.at[b], dev).start()
 
     def wait_back(b):
         k, n = batches[b]
@@ -270,33 +278,34 @@
             for zz in range(2):
                 ccopy(u, y_of[u] * 2 + zz, row, y * 2 + hz).start()
 
-    def project_out(ys, first=False, last=False):
-        for i in range(2):
-            r = ys * 2 + i
-            for half in range(2):
-                def wait(r=r, half=half):
-                    dst = comb.at[ys * 2 + (r + zh) % 2, half]
-                    rcopy(csend.at[0, 0], dst, c_send.at[0, 0], c_recv.at[r, half], (tm, r)).wait_recv()
-                if first:
-                    pl.when(i != zl)(wait)
-                else:
-                    wait()
+    def project_out(pair, first):
+        for ys in pair:
+            for i in range(2):
+                r = ys * 2 + i
+                for half in range(2):
+                    def wait(r=r, half=half, ys=ys):
+                        dst = comb.at[ys * 2 + (r + zh) % 2, half]
+                        rcopy(csend.at[0, 0], dst, c_send.at[0, 0], c_recv.at[r, half], (tm, r)).wait_recv()
+                    if ys is y:
+                        pl.when(i != zl)(wait)
+                    else:
+                        wait()
 
         @pl.loop(0, 6)
         def _(n):
             cols = pl.ds(pl.multiple_of(n * 512, 512), 512)
-            acc = dot(comb[2 * ys].reshape(256, 256), wo[2 * ys, :, cols])
-            acc = acc + dot(comb[2 * ys + 1].reshape(256, 256), wo[2 * ys + 1, :, cols])
+            heads = [2 * ys + i for ys in pair for i in range(2)]
+            left = jnp.concatenate([comb[h].reshape(256, 256) for h in heads], axis=1)
+            right = jnp.concatenate([wo[h, :, cols] for h in heads], axis=0)
+            acc = dot(left, right)
             for half in range(2):
                 for f in range(4):
                     at = (half * 4 + f) * 32
                     rows = slice(half * 32, (half + 1) * 32)
                     piece = acc[at:at + 32]
                     if not first:
-                        piece = piece + out_ref[f, rows, cols]
-                    if last:
                         clip = clip_ref[tm * 4 + f]
-                        piece = piece * mod_ref[2, pl.ds(clip, 1), cols]
+                        piece = (piece + out_ref[f, rows, cols]) * mod_ref[2, pl.ds(clip, 1), cols]
                     out_ref[f, rows, cols] = piece
 
     load_w.wait()
@@ -315,6 +324,7 @@
             wc_copy(p, j, e_cores[j]).wait_recv()
         project_part(0, oz, p)
         zcopy(0, p, zl).start()
+    load_wo.start()
     for i in range(2):
         y_copies[i].wait_recv()
         y_copies[4 + i].start()
@@ -337,12 +347,12 @@
     stage_own(3)
     stage_partner(2)
     temporal(1)
+    stage_partner(3)
 
     y_copies[6].wait_recv()
     y_copies[7].wait_recv()
     project(4)
     stage_own(4)
-    stage_partner(3)
     temporal(2)
     stage_partner(4)
     temporal(3)
@@ -363,13 +373,11 @@
     wait_back(0)
     combine(0)
     combine(1)
+    load_wo.wait()
+    project_out((yp, ym), first=True)
     wait_back(4)
     combine(7)
-    load_wo.wait()
-    project_out(y, first=True)
-    project_out(yp)
-    project_out(ym)
-    project_out(yq, last=True)
+    project_out((y, yq), first=False)
 
     for p in range(3):
         for i in range(2):
@@ -416,7 +424,7 @@
             pltpu.VMEM((256, 256), BF),
             pltpu.VMEM((256, 256), BF),
             pltpu.VMEM((256, 256), F32),
-            dma((3,)),
+            dma((4,)),
             dma((8,)), dma((8,)),
             dma((3, 2)), dma((3, 2)),
             dma((3, 2)), dma((3, 2)),

time: 115 us -> 102 us (0.89)
  the two profiles are of different devices: /device:TPU:71 before, /device:TPU:32 now
where the time goes in v6:
time: 102 us
  Pallas kernels  101 us (99%)
  local copies, waits for them, and re-layouts  1.67 us (2%)
    pallas_call x1, Pallas kernels, attention(): pl.pallas_call(attention_kernel, out_shape=pltpu.VMEM((4, 64, 3072), F32)...  101 us

profile of v6, /device:TPU:32, one launch (start us, length us, event | category | flops | bytes accessed | tf_op | source)
XLA Modules:
  0.0 102.3 jit_solution(150204205647337448)
XLA Ops:
  0.0 100.6 %attention.1 = f32[4,64,3072]{2,1,0:T(8,128)S(1)} custom-call(s32[64]{0:T(128)} %clip_ref.1, f32[4,64,3072]{2,1,0:T(8,128)} %stream_hbm.1, f32[3,8,3072]{2,1,0:T(8,128)} %bitcast.7, bf16[3,8,384,256]{3,2,1,0:T(8,128)(2,1)} %bitcast.6, bf16[8,256,3072]{2,1,0:T(8,128)(2,1)} %bitcast.5), custom_call_target="tpu_custom_call" | custom-call | tf_op jit(solution)/shard_map/attention/pallas_call | solution.py:406
  100.6 1.7 %copy.7 = f32[4,64,3072]{2,1,0:T(8,128)} copy(f32[4,64,3072]{2,1,0:T(8,128)S(1)} %attention.1) | data formatting | bytes 6291456

commit v7 on v6

--- a/solution.py
+++ b/solution.py
@@ -83,7 +83,6 @@
     row_peers = [(tm, r * 2 + (zl if i == 0 else oz)) for r in (y, ym, yp, yq) for i in range(2)][1:]
     for dev in row_peers:
         pl.semaphore_signal(barrier, inc=1, device_id=dev, device_id_type=MESH)
-    pl.semaphore_wait(barrier, 22)
 
     x_par = x % 2
     x_up, x_down = (tm + 4) % 16, (tm + 12) % 16
@@ -104,10 +103,6 @@
     def wc_copy(p, j, e):
         pair = wbuf.at[oz, p, pl.ds(e, 2)]
         return rcopy(pair, pair, wc_send.at[p, j], wc_recv.at[p, j], (other_core, row))
-
-    for p in range(3):
-        for i in range(2):
-            wz_copy(p, i, zl).start()
 
 
     def norm(unit):
@@ -136,9 +131,13 @@
     ]
     for unit in range(2):
         load_stream[unit].wait()
+        norm(unit)
         if unit == 0:
+            pl.semaphore_wait(barrier, 22)
             load_w.start()
-        norm(unit)
+            for p in range(3):
+                for i in range(2):
+                    wz_copy(p, i, zl).start()
         y_copies[2 * unit].start()
         y_copies[2 * unit + 1].start()
 
@@ -250,17 +249,20 @@
         k, n = batches[b]
         await_bytes(orecv.at[pl.ds(k, n), pl.ds(0, 15)], o_recv.at[b])
 
-    def spatial(k):
-        @pl.loop(0, 4)
-        def _(f):
-            rows = pl.ds(pl.multiple_of(f * 32, 32), 32)
-            for h in range(2):
-                cols = slice(h * HD, (h + 1) * HD)
-                q = qkv[0:2, 0, k:k + 2, rows, cols].reshape(128, HD)
-                kk, v = (qkv[0:2, part, :, rows, cols].reshape(512, HD) for part in (1, 2))
-                p, total = soften(dot_nt(q, kk))
-                o = dot(p.astype(BF), v) / total
-                sp[:, k:k + 2, rows, cols] = o.reshape(2, 2, 32, HD)
+    def spatial(ka, kb):
+        @pl.loop(0, 2)
+        def _(pair):
+            for f in range(2):
+                rows = pl.ds(pl.multiple_of(pair * 64 + f * 32, 32), 32)
+                for h in range(2):
+                    cols = slice(h * HD, (h + 1) * HD)
+                    q = jnp.concatenate(
+                        [qkv[0:2, 0, k:k + 2, rows, cols].reshape(128, HD) for k in (ka, kb)], axis=0)
+                    kk, v = (qkv[0:2, part, :, rows, cols].reshape(512, HD) for part in (1, 2))
+                    p, total = soften(dot_nt(q, kk))
+                    o = (dot(p.astype(BF), v) / total).reshape(2, 2, 2, 32, HD)
+                    sp[:, ka:ka + 2, rows, cols] = o[0]
+                    sp[:, kb:kb + 2, rows, cols] = o[1]
 
     def ccopy(u, r, at, kept):
         half = half_of[u]
@@ -278,7 +280,7 @@
             for zz in range(2):
                 ccopy(u, y_of[u] * 2 + zz, row, y * 2 + hz).start()
 
-    def project_out(pair, first):
+    def project_out(pair, first, last=True):
         for ys in pair:
             for i in range(2):
                 r = ys * 2 + i
@@ -304,8 +306,10 @@
                     rows = slice(half * 32, (half + 1) * 32)
                     piece = acc[at:at + 32]
                     if not first:
+                        piece = piece + out_ref[f, rows, cols]
+                    if not first and last:
                         clip = clip_ref[tm * 4 + f]
-                        piece = (piece + out_ref[f, rows, cols]) * mod_ref[2, pl.ds(clip, 1), cols]
+                        piece = piece * mod_ref[2, pl.ds(clip, 1), cols]
                     out_ref[f, rows, cols] = piece
 
     load_w.wait()
@@ -315,15 +319,20 @@
             wx_copy(p, i, e_own).start()
         wc_copy(p, 0, e_own).start()
         project_part(0, zl, p)
-    for p in range(3):
+    def pass_x(p):
         for i in range(2):
             wx_copy(p, i, e_x).wait_recv()
         wc_copy(p, 1, e_x).start()
+
+    pass_x(0)
+    pass_x(1)
     for p in range(3):
         for j in range(2):
             wc_copy(p, j, e_cores[j]).wait_recv()
         project_part(0, oz, p)
         zcopy(0, p, zl).start()
+        if p == 0:
+            pass_x(2)
     load_wo.start()
     for i in range(2):
         y_copies[i].wait_recv()
@@ -357,27 +366,26 @@
     stage_partner(4)
     temporal(3)
 
-    spatial(2)
+    spatial(2, 4)
     wait_back(1)
     combine(2)
     combine(3)
-    spatial(4)
     wait_back(2)
     combine(4)
     combine(5)
     temporal(4)
-    spatial(6)
+    spatial(6, 0)
     wait_back(3)
     combine(6)
-    spatial(0)
     wait_back(0)
     combine(0)
     combine(1)
+    wait_back(4)
+    combine(7)
     load_wo.wait()
     project_out((yp, ym), first=True)
-    wait_back(4)
-    combine(7)
-    project_out((y, yq), first=False)
+    project_out((y,), first=False, last=False)
+    project_out((yq,), first=False)
 
     for p in range(3):
         for i in range(2):

time: 102 us -> 99.5 us (0.975); the launches traced: 102 us -> 97.6 us
  Pallas kernels: 101 us -> 95.9 us
    pallas_call x1, Pallas kernels: 101 us -> 95.9 us  [attention(): pl.pallas_call(attention_kernel, out_shape=pltpu.VMEM((4, 64, 3072), F32)...]
where the time goes in v7:
time: 99.5 us; the launch traced here: 97.6 us
  Pallas kernels  95.9 us (96%)
  local copies, waits for them, and re-layouts  1.67 us (2%)
    pallas_call x1, Pallas kernels, attention(): pl.pallas_call(attention_kernel, out_shape=pltpu.VMEM((4, 64, 3072), F32)...  95.9 us

profile of v7, /device:TPU:32, one launch (start us, length us, event | category | flops | bytes accessed | tf_op | source)
XLA Modules:
  0.0 97.6 jit_solution(11523584879534851282)
XLA Ops:
  0.0 95.9 %attention.1 = f32[4,64,3072]{2,1,0:T(8,128)S(1)} custom-call(s32[64]{0:T(128)} %clip_ref.1, f32[4,64,3072]{2,1,0:T(8,128)} %stream_hbm.1, f32[3,8,3072]{2,1,0:T(8,128)} %bitcast.7, bf16[3,8,384,256]{3,2,1,0:T(8,128)(2,1)} %bitcast.6, bf16[8,256,3072]{2,1,0:T(8,128)(2,1)} %bitcast.5), custom_call_target="tpu_custom_call" | custom-call | tf_op jit(solution)/shard_map/attention/pallas_call | solution.py:414
  95.9 1.7 %copy.7 = f32[4,64,3072]{2,1,0:T(8,128)} copy(f32[4,64,3072]{2,1,0:T(8,128)S(1)} %attention.1) | data formatting | bytes 6291456

commit v8 on v7

--- a/solution.py
+++ b/solution.py
@@ -24,11 +24,12 @@
 
 def attention_kernel(
     clip_ref, stream_hbm, mod_ref, w_hbm, wo_hbm, out_ref,
-    stream_v, xg, wbuf, wo, qkv, tsend, trecv, osend, orecv, csend, comb, sp, perm, perm_t, mask,
+    stream_v, xg, wbuf, wo, qkv, qf, trecv, osend, orecv, csend, comb, sp, perm_t, mask,
     load_sem, y_send, y_recv, wz_send, wz_recv, wx_send, wx_recv, wc_send, wc_recv, z_send, z_recv,
     t_send, t_recv, o_send, o_recv, c_send, c_recv,
 ):
     batches = ((0, 2), (2, 2), (4, 2), (6, 1), (7, 1))
+    sets = ((0, 4), (4, 3), (7, 1))
     tm = lax.axis_index("tm")
     row = lax.axis_index("row")
     zh = (tm // 2) % 2
@@ -106,16 +107,23 @@
 
 
     def norm(unit):
+        low = lax.broadcasted_iota(jnp.int32, (8, 3072), 0) < 4
+
         @pl.loop(0, 4)
-        def _(f):
-            clip = clip_ref[tm * 4 + f]
-            shift = mod_ref[0, pl.ds(clip, 1), :]
-            scale = 1.0 + mod_ref[1, pl.ds(clip, 1), :]
-            v = stream_v[f, pl.ds(unit * 32, 32), :]
-            centred = v - jnp.mean(v, axis=-1, keepdims=True)
-            var = jnp.mean(centred * centred, axis=-1, keepdims=True)
-            n = centred * lax.rsqrt(var + 1e-06) * scale + shift
-            xg[unit, pl.ds(f * 32, 32), :] = n.astype(BF)
+        def _(j):
+            here, moved = [], []
+            for f in range(4):
+                clip = clip_ref[tm * 4 + f]
+                shift = mod_ref[0, pl.ds(clip, 1), :]
+                scale = 1.0 + mod_ref[1, pl.ds(clip, 1), :]
+                v = stream_v[f, pl.ds(pl.multiple_of(unit * 32 + j * 8, 8), 8), :]
+                centred = v - jnp.mean(v, axis=-1, keepdims=True)
+                var = jnp.mean(centred * centred, axis=-1, keepdims=True)
+                here.append(centred * lax.rsqrt(var + 1e-06) * scale + shift)
+                moved.append(pltpu.roll(here[f], 4, 0))
+            rows = [jnp.where(low, here[f], moved[f + 1]) for f in (0, 2)]
+            rows += [jnp.where(low, moved[f], here[f + 1]) for f in (0, 2)]
+            xg[unit, pl.ds(pl.multiple_of(j * 32, 32), 32), :] = jnp.concatenate(rows, axis=0).astype(BF)
 
     def ycopy(i, src, dst, half, dev):
         if half is None:
@@ -146,7 +154,6 @@
 
     r_i = lax.broadcasted_iota(jnp.int32, (256, 256), 0)
     c_i = lax.broadcasted_iota(jnp.int32, (256, 256), 1)
-    perm[...] = (unit_row(r_i) == c_i).astype(BF)
     perm_t[...] = (unit_row(c_i) == r_i).astype(BF)
     lane = lax.broadcasted_iota(jnp.int32, (1, 256), 1)
 
@@ -181,26 +188,20 @@
         def _(part):
             project_part(b, hz, part)
 
-    def stage_part(b, zz, part):
-        k, n = batches[b]
-        rows = qkv[zz, part, k:k + n].reshape(n * 128, 256)
-        moved = dot(perm[:n * 128, :n * 128], rows).astype(BF).reshape(n, 8, 16, 256)
-        tsend[k:k + n, part, pl.ds(zz * 8, 8)] = moved
-
-    def send_time(b, zz):
-        k, n = batches[b]
+    def send_time(s, zz):
+        k, n = sets[s]
         units = pl.ds(k, n)
         for dx in (1, 3, 2, 0):
             for dz in (1, 0):
                 t = xs[dx] * 4 + zs[dz] * 2 + zz
-                at = zz * 8 + xs[dx] * 2 + zs[dz]
-
-                def send(t=t, at=at, dz=dz):
-                    rcopy(tsend.at[units, :, at], trecv.at[units, :, tm], t_send.at[b], t_recv.at[b],
+                rows = pl.ds(pl.multiple_of((xs[dx] * 2 + zs[dz]) * 16, 16), 16)
+
+                def send(t=t, rows=rows, dz=dz):
+                    rcopy(qkv.at[zz, :, units, rows], trecv.at[:, units, tm], t_send.at[s], t_recv.at[s],
                           (t, rows_of[dz])).start()
 
-                def keep(at=at):
-                    trecv[k:k + n, :, tm] = tsend[k:k + n, :, at]
+                def keep(rows=rows):
+                    trecv[:, k:k + n, tm] = qkv[zz, :, k:k + n, rows]
 
                 if (dx, dz) == (0, 0):
                     pl.when(zz != core)(send)
@@ -208,20 +209,19 @@
                 else:
                     send()
 
-    def stage_own(b):
-        @pl.loop(0, 3)
-        def _(part):
-            stage_part(b, zl, part)
-
-        send_time(b, zl)
-
-    def stage_partner(b):
-        @pl.loop(0, 3)
-        def _(part):
+    def wait_partner(b):
+        for part in range(3):
             zcopy(b, part, oz).wait_recv()
-            stage_part(b, oz, part)
-
-        send_time(b, oz)
+
+    def by_frame(b):
+        k, n = batches[b]
+
+        @pl.loop(0, 6)
+        def _(i):
+            zz, part = i // 3, i % 3
+            rows = qkv[zz, part, k:k + n].reshape(n * 128, 256)
+            moved = dot(perm_t[:n * 128, :n * 128], rows).astype(BF)
+            qf[zz, part, k:k + n] = moved.reshape(n, 128, 256)
 
     factor = LOG2E / math.sqrt(HD)
 
@@ -229,25 +229,25 @@
         p = jnp.exp2((s - jnp.max(s, axis=-1, keepdims=True)) * factor)
         return p, jnp.sum(p, axis=-1, keepdims=True)
 
-    def temporal(b):
-        k, n = batches[b]
+    def temporal(s):
+        k, n = sets[s]
         units = pl.ds(k, n)
-        await_bytes(trecv.at[units, :, pl.ds(0, 15)], t_recv.at[b])
+        await_bytes(trecv.at[:, units, pl.ds(0, 15)], t_recv.at[s])
         for u in range(k, k + n):
             for h in range(2):
                 cols = slice(h * HD, (h + 1) * HD)
-                q, kk, v = (trecv[u, part, :, :, cols].reshape(256, HD) for part in range(3))
+                q, kk, v = (trecv[part, u, :, :, cols].reshape(256, HD) for part in range(3))
                 p, total = soften(dot_nt(q, kk) + mask[...])
                 o = dot(p.astype(BF), v) / total
                 osend[u, :, :, cols] = o.astype(BF).reshape(16, 16, HD)
         orecv[k:k + n, me_at] = osend[k:k + n, tm]
         for o in offsets:
             dev, _ = peer(*o)
-            rcopy(osend.at[units, dev[0]], orecv.at[units, me_at], o_send.at[b], o_recv.at[b], dev).start()
-
-    def wait_back(b):
-        k, n = batches[b]
-        await_bytes(orecv.at[pl.ds(k, n), pl.ds(0, 15)], o_recv.at[b])
+            rcopy(osend.at[units, dev[0]], orecv.at[units, me_at], o_send.at[s], o_recv.at[s], dev).start()
+
+    def wait_back(s):
+        k, n = sets[s]
+        await_bytes(orecv.at[pl.ds(k, n), pl.ds(0, 15)], o_recv.at[s])
 
     def spatial(ka, kb):
         @pl.loop(0, 2)
@@ -257,8 +257,8 @@
                 for h in range(2):
                     cols = slice(h * HD, (h + 1) * HD)
                     q = jnp.concatenate(
-                        [qkv[0:2, 0, k:k + 2, rows, cols].reshape(128, HD) for k in (ka, kb)], axis=0)
-                    kk, v = (qkv[0:2, part, :, rows, cols].reshape(512, HD) for part in (1, 2))
+                        [qf[:, 0, k:k + 2, rows, cols].reshape(128, HD) for k in (ka, kb)], axis=0)
+                    kk, v = (qf[:, part, :, rows, cols].reshape(512, HD) for part in (1, 2))
                     p, total = soften(dot_nt(q, kk))
                     o = (dot(p.astype(BF), v) / total).reshape(2, 2, 2, 32, HD)
                     sp[:, ka:ka + 2, rows, cols] = o[0]
@@ -337,50 +337,52 @@
     for i in range(2):
         y_copies[i].wait_recv()
         y_copies[4 + i].start()
-    stage_own(0)
     project(1)
-    stage_own(1)
-    stage_partner(0)
+    send_time(0, zl)
+    wait_partner(0)
+    wait_partner(1)
+    send_time(0, oz)
 
     for i in range(2):
         y_copies[2 + i].wait_recv()
         y_copies[6 + i].start()
     project(2)
-    stage_own(2)
-    stage_partner(1)
+    by_frame(0)
+    by_frame(1)
     temporal(0)
 
     y_copies[4].wait_recv()
     y_copies[5].wait_recv()
     project(3)
-    stage_own(3)
-    stage_partner(2)
-    temporal(1)
-    stage_partner(3)
+    send_time(1, zl)
+    wait_partner(2)
+    by_frame(2)
+    wait_partner(3)
+    send_time(1, oz)
+    by_frame(3)
 
     y_copies[6].wait_recv()
     y_copies[7].wait_recv()
     project(4)
-    stage_own(4)
-    temporal(2)
-    stage_partner(4)
-    temporal(3)
+    send_time(2, zl)
+    temporal(1)
+    wait_partner(4)
+    send_time(2, oz)
+    by_frame(4)
 
     spatial(2, 4)
-    wait_back(1)
+    wait_back(0)
     combine(2)
     combine(3)
-    wait_back(2)
+    wait_back(1)
     combine(4)
     combine(5)
-    temporal(4)
+    temporal(2)
     spatial(6, 0)
-    wait_back(3)
     combine(6)
-    wait_back(0)
     combine(0)
     combine(1)
-    wait_back(4)
+    wait_back(2)
     combine(7)
     load_wo.wait()
     project_out((yp, ym), first=True)
@@ -397,8 +399,9 @@
     for b, (k, n) in enumerate(batches):
         for part in range(3):
             zcopy(b, part, zl).wait_send()
-        await_bytes(tsend.at[pl.ds(k, n), :, pl.ds(0, 15)], t_send.at[b])
-        await_bytes(osend.at[pl.ds(k, n), pl.ds(0, 15)], o_send.at[b])
+    for s, (k, n) in enumerate(sets):
+        await_bytes(trecv.at[:, pl.ds(k, n), pl.ds(0, 15)], t_send.at[s])
+        await_bytes(osend.at[pl.ds(k, n), pl.ds(0, 15)], o_send.at[s])
     for u in range(8):
         if u < 2:
             ccopy(u, partner_row, row, y * 2 + hz).wait_send()
@@ -422,14 +425,13 @@
             pltpu.VMEM((2, 3, 8, 384, 256), BF),
             pltpu.VMEM((8, 256, 3072), BF),
             pltpu.VMEM((3, 3, 8, 128, 256), BF),
-            pltpu.VMEM((8, 3, 16, 16, 256), BF),
-            pltpu.VMEM((8, 3, 16, 16, 256), BF),
+            pltpu.VMEM((2, 3, 8, 128, 256), BF),
+            pltpu.VMEM((3, 8, 16, 16, 256), BF),
             pltpu.VMEM((8, 16, 16, 256), BF),
             pltpu.VMEM((8, 16, 16, 256), BF),
             pltpu.VMEM((8, 2, 128, 256), BF),
             pltpu.VMEM((8, 2, 128, 256), BF),
             pltpu.VMEM((2, 8, 128, 256), F32),
-            pltpu.VMEM((256, 256), BF),
             pltpu.VMEM((256, 256), BF),
             pltpu.VMEM((256, 256), F32),
             dma((4,)),
@@ -438,8 +440,8 @@
             dma((3, 2)), dma((3, 2)),
             dma((3, 2)), dma((3, 2)),
             dma((5, 3)), dma((5, 3)),
-            dma((5,)), dma((5,)),
-            dma((5,)), dma((5,)),
+            dma((3,)), dma((3,)),
+            dma((3,)), dma((3,)),
             dma((8, 2)), dma((8, 2)),
         ],
         compiler_params=pltpu.CompilerParams(

time: 99.5 us -> 107 us (1.075); the launches traced: 97.6 us -> 106 us
  Pallas kernels: 95.9 us -> 105 us
    pallas_call x1, Pallas kernels: 95.9 us -> 105 us  [attention(): pl.pallas_call(attention_kernel, out_shape=pltpu.VMEM((4, 64, 3072), F32)...]
where the time goes in v8:
time: 107 us; the launch traced here: 106 us
  Pallas kernels  105 us (98%)
  local copies, waits for them, and re-layouts  1.67 us (2%)
    pallas_call x1, Pallas kernels, attention(): pl.pallas_call(attention_kernel, out_shape=pltpu.VMEM((4, 64, 3072), F32)...  105 us

profile of v8, /device:TPU:32, one launch (start us, length us, event | category | flops | bytes accessed | tf_op | source)
XLA Modules:
  0.0 106.4 jit_solution(5232932890308066125)
XLA Ops:
  0.0 104.7 %attention.1 = f32[4,64,3072]{2,1,0:T(8,128)S(1)} custom-call(s32[64]{0:T(128)} %clip_ref.1, f32[4,64,3072]{2,1,0:T(8,128)} %stream_hbm.1, f32[3,8,3072]{2,1,0:T(8,128)} %bitcast.7, bf16[3,8,384,256]{3,2,1,0:T(8,128)(2,1)} %bitcast.6, bf16[8,256,3072]{2,1,0:T(8,128)(2,1)} %bitcast.5), custom_call_target="tpu_custom_call" | custom-call | tf_op jit(solution)/shard_map/attention/pallas_call | solution.py:417
  104.7 1.7 %copy.7 = f32[4,64,3072]{2,1,0:T(8,128)} copy(f32[4,64,3072]{2,1,0:T(8,128)S(1)} %attention.1) | data formatting | bytes 6291456

commit v9 on v7

--- a/solution.py
+++ b/solution.py
@@ -24,9 +24,9 @@
 
 def attention_kernel(
     clip_ref, stream_hbm, mod_ref, w_hbm, wo_hbm, out_ref,
-    stream_v, xg, wbuf, wo, qkv, tsend, trecv, osend, orecv, csend, comb, sp, perm, perm_t, mask,
+    stream_v, xg, wbuf, wo, qkv, tsend, trecv, osend, orecv, csend, comb, relay, sp, perm, perm_t, mask,
     load_sem, y_send, y_recv, wz_send, wz_recv, wx_send, wx_recv, wc_send, wc_recv, z_send, z_recv,
-    t_send, t_recv, o_send, o_recv, c_send, c_recv,
+    t_send, t_recv, b_send, b_recv, f_send, o_send, o_recv, c_send, c_recv,
 ):
     batches = ((0, 2), (2, 2), (4, 2), (6, 1), (7, 1))
     tm = lax.axis_index("tm")
@@ -190,7 +190,9 @@
     def send_time(b, zz):
         k, n = batches[b]
         units = pl.ds(k, n)
-        for dx in (1, 3, 2, 0):
+        if b < 3:
+            bundle(b, zz).start()
+        for dx in (1, 3, 0) if b < 3 else (1, 3, 2, 0):
             for dz in (1, 0):
                 t = xs[dx] * 4 + zs[dz] * 2 + zz
                 at = zz * 8 + xs[dx] * 2 + zs[dz]
@@ -207,6 +209,25 @@
                     pl.when(zz == core)(keep)
                 else:
                     send()
+
+    def bundle(b, zz):
+        k, n = batches[b]
+        units = pl.ds(k, n)
+        return rcopy(tsend.at[units, :, pl.ds(zz * 8 + xs[2] * 2, 2)], relay.at[units, :, zz],
+                     b_send.at[b, zz], b_recv.at[b, zz], (x_up, row))
+
+    def fcopy(b, zz, z):
+        k, n = batches[b]
+        units = pl.ds(k, n)
+        dev = (xs[1] * 4 + z * 2 + zz, y * 2 + (hz + z) % 2)
+        return rcopy(relay.at[units, :, zz, z], trecv.at[units, :, x_down], f_send.at[b, zz, z],
+                     t_recv.at[b], dev)
+
+    def pass_on(b):
+        for zz in range(2):
+            bundle(b, zz).wait_recv()
+            for z in range(2):
+                fcopy(b, zz, z).start()
 
     def stage_own(b):
         @pl.loop(0, 3)
@@ -346,6 +367,7 @@
         y_copies[2 + i].wait_recv()
         y_copies[6 + i].start()
     project(2)
+    pass_on(0)
     stage_own(2)
     stage_partner(1)
     temporal(0)
@@ -353,6 +375,7 @@
     y_copies[4].wait_recv()
     y_copies[5].wait_recv()
     project(3)
+    pass_on(1)
     stage_own(3)
     stage_partner(2)
     temporal(1)
@@ -362,9 +385,10 @@
     y_copies[7].wait_recv()
     project(4)
     stage_own(4)
-    temporal(2)
+    pass_on(2)
     stage_partner(4)
     temporal(3)
+    temporal(2)
 
     spatial(2, 4)
     wait_back(1)
@@ -397,7 +421,12 @@
     for b, (k, n) in enumerate(batches):
         for part in range(3):
             zcopy(b, part, zl).wait_send()
-        await_bytes(tsend.at[pl.ds(k, n), :, pl.ds(0, 15)], t_send.at[b])
+        await_bytes(tsend.at[pl.ds(k, n), :, pl.ds(0, 11 if b < 3 else 15)], t_send.at[b])
+        if b < 3:
+            for zz in range(2):
+                bundle(b, zz).wait_send()
+                for z in range(2):
+                    fcopy(b, zz, z).wait_send()
         await_bytes(osend.at[pl.ds(k, n), pl.ds(0, 15)], o_send.at[b])
     for u in range(8):
         if u < 2:
@@ -428,6 +457,7 @@
             pltpu.VMEM((8, 16, 16, 256), BF),
             pltpu.VMEM((8, 2, 128, 256), BF),
             pltpu.VMEM((8, 2, 128, 256), BF),
+            pltpu.VMEM((6, 3, 2, 2, 16, 256), BF),
             pltpu.VMEM((2, 8, 128, 256), F32),
             pltpu.VMEM((256, 256), BF),
             pltpu.VMEM((256, 256), BF),
@@ -439,6 +469,7 @@
             dma((3, 2)), dma((3, 2)),
             dma((5, 3)), dma((5, 3)),
             dma((5,)), dma((5,)),
+            dma((3, 2)), dma((3, 2)), dma((3, 2, 2)),
             dma((5,)), dma((5,)),
             dma((8, 2)), dma((8, 2)),
         ],

time: 99.5 us -> 113 us (1.14)
  Pallas kernels: 95.9 us -> 110 us
    pallas_call x1, Pallas kernels: 95.9 us -> 110 us  [attention(): pl.pallas_call(attention_kernel, out_shape=pltpu.VMEM((4, 64, 3072), F32)...]
where the time goes in v9:
time: 113 us; the launch traced here: 112 us
  Pallas kernels  110 us (97%)
  local copies, waits for them, and re-layouts  1.67 us (1%)
    pallas_call x1, Pallas kernels, attention(): pl.pallas_call(attention_kernel, out_shape=pltpu.VMEM((4, 64, 3072), F32)...  110 us

profile of v9, /device:TPU:32, one launch (start us, length us, event | category | flops | bytes accessed | tf_op | source)
XLA Modules:
  0.0 111.8 jit_solution(1682429412065169742)
XLA Ops:
  0.0 110.2 %attention.1 = f32[4,64,3072]{2,1,0:T(8,128)S(1)} custom-call(s32[64]{0:T(128)} %clip_ref.1, f32[4,64,3072]{2,1,0:T(8,128)} %stream_hbm.1, f32[3,8,3072]{2,1,0:T(8,128)} %bitcast.7, bf16[3,8,384,256]{3,2,1,0:T(8,128)(2,1)} %bitcast.6, bf16[8,256,3072]{2,1,0:T(8,128)(2,1)} %bitcast.5), custom_call_target="tpu_custom_call" | custom-call | tf_op jit(solution)/shard_map/attention/pallas_call | solution.py:443
  110.2 1.7 %copy.7 = f32[4,64,3072]{2,1,0:T(8,128)} copy(f32[4,64,3072]{2,1,0:T(8,128)S(1)} %attention.1) | data formatting | bytes 6291456

commit v10 on v7

--- a/solution.py
+++ b/solution.py
@@ -138,8 +138,9 @@
             for p in range(3):
                 for i in range(2):
                     wz_copy(p, i, zl).start()
-        y_copies[2 * unit].start()
-        y_copies[2 * unit + 1].start()
+        if unit == 0:
+            y_copies[0].start()
+            y_copies[1].start()
 
     def unit_row(j):
         return (j & 128) + ((j >> 2) & 3) * 32 + ((j >> 4) & 7) * 4 + (j & 3)
@@ -319,6 +320,9 @@
             wx_copy(p, i, e_own).start()
         wc_copy(p, 0, e_own).start()
         project_part(0, zl, p)
+    y_copies[2].start()
+    y_copies[3].start()
+
     def pass_x(p):
         for i in range(2):
             wx_copy(p, i, e_x).wait_recv()
@@ -348,33 +352,33 @@
     project(2)
     stage_own(2)
     stage_partner(1)
-    temporal(0)
 
     y_copies[4].wait_recv()
     y_copies[5].wait_recv()
     project(3)
     stage_own(3)
     stage_partner(2)
-    temporal(1)
-    stage_partner(3)
+    temporal(0)
 
     y_copies[6].wait_recv()
     y_copies[7].wait_recv()
     project(4)
     stage_own(4)
+    stage_partner(3)
+    temporal(1)
+    stage_partner(4)
+
+    spatial(2, 4)
     temporal(2)
-    stage_partner(4)
     temporal(3)
-
-    spatial(2, 4)
     wait_back(1)
     combine(2)
     combine(3)
+    temporal(4)
+    spatial(6, 0)
     wait_back(2)
     combine(4)
     combine(5)
-    temporal(4)
-    spatial(6, 0)
     wait_back(3)
     combine(6)
     wait_back(0)

time: 99.5 us -> 101 us (1.015)
  the two profiles are of different devices: /device:TPU:32 before, /device:TPU:56 now
where the time goes in v10:
time: 101 us
  Pallas kernels  99.5 us (99%)
  local copies, waits for them, and re-layouts  1.67 us (2%)
    pallas_call x1, Pallas kernels, attention(): pl.pallas_call(attention_kernel, out_shape=pltpu.VMEM((4, 64, 3072), F32)...  99.5 us

profile of v10, /device:TPU:56, one launch (start us, length us, event | category | flops | bytes accessed | tf_op | source)
XLA Modules:
  0.0 101.1 jit_solution(3089031046592042731)
XLA Ops:
  0.0 99.5 %attention.1 = f32[4,64,3072]{2,1,0:T(8,128)S(1)} custom-call(s32[64]{0:T(128)} %clip_ref.1, f32[4,64,3072]{2,1,0:T(8,128)} %stream_hbm.1, f32[3,8,3072]{2,1,0:T(8,128)} %bitcast.7, bf16[3,8,384,256]{3,2,1,0:T(8,128)(2,1)} %bitcast.6, bf16[8,256,3072]{2,1,0:T(8,128)(2,1)} %bitcast.5), custom_call_target="tpu_custom_call" | custom-call | tf_op jit(solution)/shard_map/attention/pallas_call | solution.py:418
  99.5 1.7 %copy.7 = f32[4,64,3072]{2,1,0:T(8,128)} copy(f32[4,64,3072]{2,1,0:T(8,128)S(1)} %attention.1) | data formatting | bytes 6291456

commit v11 on v7

--- a/solution.py
+++ b/solution.py
@@ -29,6 +29,7 @@
     t_send, t_recv, o_send, o_recv, c_send, c_recv,
 ):
     batches = ((0, 2), (2, 2), (4, 2), (6, 1), (7, 1))
+    sets = ((0, 2), (2, 2), (4, 3), (7, 1))
     tm = lax.axis_index("tm")
     row = lax.axis_index("row")
     zh = (tm // 2) % 2
@@ -171,11 +172,14 @@
         return rcopy(qkv.at[2, part, units], qkv.at[slot, part, units], z_send.at[b, part],
                      z_recv.at[b, part], (tm, partner_row))
 
-    def project(b):
+    def project_sent(b):
         @pl.loop(0, 3)
         def _(part):
             project_part(b, 1 - hz, part)
             zcopy(b, part, zl).start()
+
+    def project(b):
+        project_sent(b)
 
         @pl.loop(0, 3)
         def _(part):
@@ -229,25 +233,35 @@
         p = jnp.exp2((s - jnp.max(s, axis=-1, keepdims=True)) * factor)
         return p, jnp.sum(p, axis=-1, keepdims=True)
 
+    def wait_time(b):
+        k, n = batches[b]
+        await_bytes(trecv.at[pl.ds(k, n), :, pl.ds(0, 15)], t_recv.at[b])
+
+    def temporal_head(u, h):
+        cols = slice(h * HD, (h + 1) * HD)
+        q, kk, v = (trecv[u, part, :, :, cols].reshape(256, HD) for part in range(3))
+        p, total = soften(dot_nt(q, kk) + mask[...])
+        o = dot(p.astype(BF), v) / total
+        osend[u, :, :, cols] = o.astype(BF).reshape(16, 16, HD)
+
     def temporal(b):
         k, n = batches[b]
-        units = pl.ds(k, n)
-        await_bytes(trecv.at[units, :, pl.ds(0, 15)], t_recv.at[b])
+        wait_time(b)
         for u in range(k, k + n):
             for h in range(2):
-                cols = slice(h * HD, (h + 1) * HD)
-                q, kk, v = (trecv[u, part, :, :, cols].reshape(256, HD) for part in range(3))
-                p, total = soften(dot_nt(q, kk) + mask[...])
-                o = dot(p.astype(BF), v) / total
-                osend[u, :, :, cols] = o.astype(BF).reshape(16, 16, HD)
+                temporal_head(u, h)
+
+    def send_back(s):
+        k, n = sets[s]
+        units = pl.ds(k, n)
         orecv[k:k + n, me_at] = osend[k:k + n, tm]
         for o in offsets:
             dev, _ = peer(*o)
-            rcopy(osend.at[units, dev[0]], orecv.at[units, me_at], o_send.at[b], o_recv.at[b], dev).start()
-
-    def wait_back(b):
-        k, n = batches[b]
-        await_bytes(orecv.at[pl.ds(k, n), pl.ds(0, 15)], o_recv.at[b])
+            rcopy(osend.at[units, dev[0]], orecv.at[units, me_at], o_send.at[s], o_recv.at[s], dev).start()
+
+    def wait_back(s):
+        k, n = sets[s]
+        await_bytes(orecv.at[pl.ds(k, n), pl.ds(0, 15)], o_recv.at[s])
 
     def spatial(ka, kb):
         @pl.loop(0, 2)
@@ -269,16 +283,18 @@
         return rcopy(csend.at[u, r % 2], comb.at[kept, half], c_send.at[u, r % 2], c_recv.at[at, half],
                      (tm, r))
 
-    def combine(u):
-        for zz in range(2):
-            back = dot(perm_t[:128, :128], orecv[u, zz * 8:(zz + 1) * 8].reshape(128, 256))
-            csend[u, zz] = (sp[zz, u] + back).astype(BF)
-        if u < 2:
-            ccopy(u, partner_row, row, y * 2 + hz).start()
-            comb[y * 2 + hz, u] = csend[u, zl]
-        else:
+    def combine(*units):
+        for u in units:
             for zz in range(2):
-                ccopy(u, y_of[u] * 2 + zz, row, y * 2 + hz).start()
+                back = dot(perm_t[:128, :128], orecv[u, zz * 8:(zz + 1) * 8].reshape(128, 256))
+                csend[u, zz] = (sp[zz, u] + back).astype(BF)
+        for u in units:
+            if u < 2:
+                ccopy(u, partner_row, row, y * 2 + hz).start()
+                comb[y * 2 + hz, u] = csend[u, zl]
+            else:
+                for zz in range(2):
+                    ccopy(u, y_of[u] * 2 + zz, row, y * 2 + hz).start()
 
     def project_out(pair, first, last=True):
         for ys in pair:
@@ -293,9 +309,9 @@
                     else:
                         wait()
 
-        @pl.loop(0, 6)
+        @pl.loop(0, 3)
         def _(n):
-            cols = pl.ds(pl.multiple_of(n * 512, 512), 512)
+            cols = pl.ds(pl.multiple_of(n * 1024, 1024), 1024)
             heads = [2 * ys + i for ys in pair for i in range(2)]
             left = jnp.concatenate([comb[h].reshape(256, 256) for h in heads], axis=1)
             right = jnp.concatenate([wo[h, :, cols] for h in heads], axis=0)
@@ -349,6 +365,7 @@
     stage_own(2)
     stage_partner(1)
     temporal(0)
+    send_back(0)
 
     y_copies[4].wait_recv()
     y_copies[5].wait_recv()
@@ -356,31 +373,36 @@
     stage_own(3)
     stage_partner(2)
     temporal(1)
+    send_back(1)
     stage_partner(3)
 
     y_copies[6].wait_recv()
     y_copies[7].wait_recv()
-    project(4)
+    project_sent(4)
+    wait_time(2)
+    temporal_head(4, 0)
+    project_part(4, hz, 0)
+    temporal_head(4, 1)
+    project_part(4, hz, 1)
+    temporal_head(5, 0)
+    project_part(4, hz, 2)
+    temporal_head(5, 1)
     stage_own(4)
-    temporal(2)
+    temporal(3)
+    send_back(2)
     stage_partner(4)
-    temporal(3)
 
     spatial(2, 4)
     wait_back(1)
-    combine(2)
-    combine(3)
+    combine(2, 3)
+    temporal(4)
+    send_back(3)
     wait_back(2)
-    combine(4)
-    combine(5)
-    temporal(4)
+    combine(4, 5)
     spatial(6, 0)
+    wait_back(0)
+    combine(6, 0, 1)
     wait_back(3)
-    combine(6)
-    wait_back(0)
-    combine(0)
-    combine(1)
-    wait_back(4)
     combine(7)
     load_wo.wait()
     project_out((yp, ym), first=True)
@@ -398,7 +420,8 @@
         for part in range(3):
             zcopy(b, part, zl).wait_send()
         await_bytes(tsend.at[pl.ds(k, n), :, pl.ds(0, 15)], t_send.at[b])
-        await_bytes(osend.at[pl.ds(k, n), pl.ds(0, 15)], o_send.at[b])
+    for s, (k, n) in enumerate(sets):
+        await_bytes(osend.at[pl.ds(k, n), pl.ds(0, 15)], o_send.at[s])
     for u in range(8):
         if u < 2:
             ccopy(u, partner_row, row, y * 2 + hz).wait_send()
@@ -439,7 +462,7 @@
             dma((3, 2)), dma((3, 2)),
             dma((5, 3)), dma((5, 3)),
             dma((5,)), dma((5,)),
-            dma((5,)), dma((5,)),
+            dma((4,)), dma((4,)),
             dma((8, 2)), dma((8, 2)),
         ],
         compiler_params=pltpu.CompilerParams(

time: 99.5 us -> 102 us (1.025)
  the two profiles are of different devices: /device:TPU:32 before, /device:TPU:56 now
where the time goes in v11:
time: 102 us
  Pallas kernels  101 us (99%)
  local copies, waits for them, and re-layouts  1.67 us (2%)
    pallas_call x1, Pallas kernels, attention(): pl.pallas_call(attention_kernel, out_shape=pltpu.VMEM((4, 64, 3072), F32)...  101 us

profile of v11, /device:TPU:56, one launch (start us, length us, event | category | flops | bytes accessed | tf_op | source)
XLA Modules:
  0.0 102.2 jit_solution(11318287403157036226)
XLA Ops:
  0.0 100.5 %attention.1 = f32[4,64,3072]{2,1,0:T(8,128)S(1)} custom-call(s32[64]{0:T(128)} %clip_ref.1, f32[4,64,3072]{2,1,0:T(8,128)} %stream_hbm.1, f32[3,8,3072]{2,1,0:T(8,128)} %bitcast.7, bf16[3,8,384,256]{3,2,1,0:T(8,128)(2,1)} %bitcast.6, bf16[8,256,3072]{2,1,0:T(8,128)(2,1)} %bitcast.5), custom_call_target="tpu_custom_call" | custom-call | tf_op jit(solution)/shard_map/attention/pallas_call | solution.py:437
  100.6 1.7 %copy.7 = f32[4,64,3072]{2,1,0:T(8,128)} copy(f32[4,64,3072]{2,1,0:T(8,128)S(1)} %attention.1) | data formatting | bytes 6291456

commit v12 on v7

--- a/solution.py
+++ b/solution.py
@@ -28,7 +28,7 @@
     load_sem, y_send, y_recv, wz_send, wz_recv, wx_send, wx_recv, wc_send, wc_recv, z_send, z_recv,
     t_send, t_recv, o_send, o_recv, c_send, c_recv,
 ):
-    batches = ((0, 2), (2, 2), (4, 2), (6, 1), (7, 1))
+    batches = ((0, 2), (2, 2), (4, 2), (6, 2))
     tm = lax.axis_index("tm")
     row = lax.axis_index("row")
     zh = (tm // 2) % 2
@@ -270,9 +270,8 @@
                      (tm, r))
 
     def combine(u):
-        for zz in range(2):
-            back = dot(perm_t[:128, :128], orecv[u, zz * 8:(zz + 1) * 8].reshape(128, 256))
-            csend[u, zz] = (sp[zz, u] + back).astype(BF)
+        back = dot(perm_t[...], orecv[u].reshape(256, 256)).reshape(2, 128, 256)
+        csend[u] = (sp[:, u] + back).astype(BF)
         if u < 2:
             ccopy(u, partner_row, row, y * 2 + hz).start()
             comb[y * 2 + hz, u] = csend[u, zl]
@@ -349,22 +348,15 @@
     stage_own(2)
     stage_partner(1)
     temporal(0)
-
-    y_copies[4].wait_recv()
-    y_copies[5].wait_recv()
+    stage_partner(2)
+    temporal(1)
+
+    for i in range(4):
+        y_copies[4 + i].wait_recv()
     project(3)
     stage_own(3)
-    stage_partner(2)
-    temporal(1)
+    temporal(2)
     stage_partner(3)
-
-    y_copies[6].wait_recv()
-    y_copies[7].wait_recv()
-    project(4)
-    stage_own(4)
-    temporal(2)
-    stage_partner(4)
-    temporal(3)
 
     spatial(2, 4)
     wait_back(1)
@@ -373,14 +365,13 @@
     wait_back(2)
     combine(4)
     combine(5)
-    temporal(4)
+    temporal(3)
     spatial(6, 0)
-    wait_back(3)
-    combine(6)
     wait_back(0)
     combine(0)
     combine(1)
-    wait_back(4)
+    wait_back(3)
+    combine(6)
     combine(7)
     load_wo.wait()
     project_out((yp, ym), first=True)
@@ -437,9 +428,9 @@
             dma((3, 2)), dma((3, 2)),
             dma((3, 2)), dma((3, 2)),
             dma((3, 2)), dma((3, 2)),
-            dma((5, 3)), dma((5, 3)),
-            dma((5,)), dma((5,)),
-            dma((5,)), dma((5,)),
+            dma((4, 3)), dma((4, 3)),
+            dma((4,)), dma((4,)),
+            dma((4,)), dma((4,)),
             dma((8, 2)), dma((8, 2)),
         ],
         compiler_params=pltpu.CompilerParams(

time: 99.5 us -> 101 us (1.015); the launches traced: 97.6 us -> 101 us
  Pallas kernels: 95.9 us -> 99.5 us
    pallas_call x1, Pallas kernels: 95.9 us -> 99.5 us  [attention(): pl.pallas_call(attention_kernel, out_shape=pltpu.VMEM((4, 64, 3072), F32)...]
where the time goes in v12:
time: 101 us
  Pallas kernels  99.5 us (99%)
  local copies, waits for them, and re-layouts  1.67 us (2%)
    pallas_call x1, Pallas kernels, attention(): pl.pallas_call(attention_kernel, out_shape=pltpu.VMEM((4, 64, 3072), F32)...  99.5 us

profile of v12, /device:TPU:32, one launch (start us, length us, event | category | flops | bytes accessed | tf_op | source)
XLA Modules:
  0.0 101.1 jit_solution(9979941908479458676)
XLA Ops:
  0.0 99.5 %attention.1 = f32[4,64,3072]{2,1,0:T(8,128)S(1)} custom-call(s32[64]{0:T(128)} %clip_ref.1, f32[4,64,3072]{2,1,0:T(8,128)} %stream_hbm.1, f32[3,8,3072]{2,1,0:T(8,128)} %bitcast.7, bf16[3,8,384,256]{3,2,1,0:T(8,128)(2,1)} %bitcast.6, bf16[8,256,3072]{2,1,0:T(8,128)(2,1)} %bitcast.5), custom_call_target="tpu_custom_call" | custom-call | tf_op jit(solution)/shard_map/attention/pallas_call | solution.py:405
  99.5 1.7 %copy.7 = f32[4,64,3072]{2,1,0:T(8,128)} copy(f32[4,64,3072]{2,1,0:T(8,128)S(1)} %attention.1) | data formatting | bytes 6291456

commit v13 on v7

--- a/solution.py
+++ b/solution.py
@@ -185,7 +185,8 @@
         k, n = batches[b]
         rows = qkv[zz, part, k:k + n].reshape(n * 128, 256)
         moved = dot(perm[:n * 128, :n * 128], rows).astype(BF).reshape(n, 8, 16, 256)
-        tsend[k:k + n, part, pl.ds(zz * 8, 8)] = moved
+        for i in range(n):
+            tsend[pl.ds(zz * 8, 8), k + i, part] = moved[i]
 
     def send_time(b, zz):
         k, n = batches[b]
@@ -196,11 +197,11 @@
                 at = zz * 8 + xs[dx] * 2 + zs[dz]
 
                 def send(t=t, at=at, dz=dz):
-                    rcopy(tsend.at[units, :, at], trecv.at[units, :, tm], t_send.at[b], t_recv.at[b],
+                    rcopy(tsend.at[at, units], trecv.at[tm, units], t_send.at[b], t_recv.at[b],
                           (t, rows_of[dz])).start()
 
                 def keep(at=at):
-                    trecv[k:k + n, :, tm] = tsend[k:k + n, :, at]
+                    trecv[tm, k:k + n] = tsend[at, k:k + n]
 
                 if (dx, dz) == (0, 0):
                     pl.when(zz != core)(send)
@@ -232,22 +233,22 @@
     def temporal(b):
         k, n = batches[b]
         units = pl.ds(k, n)
-        await_bytes(trecv.at[units, :, pl.ds(0, 15)], t_recv.at[b])
+        await_bytes(trecv.at[pl.ds(0, 15), units], t_recv.at[b])
         for u in range(k, k + n):
             for h in range(2):
                 cols = slice(h * HD, (h + 1) * HD)
-                q, kk, v = (trecv[u, part, :, :, cols].reshape(256, HD) for part in range(3))
+                q, kk, v = (trecv[:, u, part, :, cols].reshape(256, HD) for part in range(3))
                 p, total = soften(dot_nt(q, kk) + mask[...])
                 o = dot(p.astype(BF), v) / total
-                osend[u, :, :, cols] = o.astype(BF).reshape(16, 16, HD)
-        orecv[k:k + n, me_at] = osend[k:k + n, tm]
+                osend[:, u, :, cols] = o.astype(BF).reshape(16, 16, HD)
+        orecv[me_at, k:k + n] = osend[tm, k:k + n]
         for o in offsets:
             dev, _ = peer(*o)
-            rcopy(osend.at[units, dev[0]], orecv.at[units, me_at], o_send.at[b], o_recv.at[b], dev).start()
+            rcopy(osend.at[dev[0], units], orecv.at[me_at, units], o_send.at[b], o_recv.at[b], dev).start()
 
     def wait_back(b):
         k, n = batches[b]
-        await_bytes(orecv.at[pl.ds(k, n), pl.ds(0, 15)], o_recv.at[b])
+        await_bytes(orecv.at[pl.ds(0, 15), pl.ds(k, n)], o_recv.at[b])
 
     def spatial(ka, kb):
         @pl.loop(0, 2)
@@ -271,7 +272,7 @@
 
     def combine(u):
         for zz in range(2):
-            back = dot(perm_t[:128, :128], orecv[u, zz * 8:(zz + 1) * 8].reshape(128, 256))
+            back = dot(perm_t[:128, :128], orecv[zz * 8:(zz + 1) * 8, u].reshape(128, 256))
             csend[u, zz] = (sp[zz, u] + back).astype(BF)
         if u < 2:
             ccopy(u, partner_row, row, y * 2 + hz).start()
@@ -397,8 +398,8 @@
     for b, (k, n) in enumerate(batches):
         for part in range(3):
             zcopy(b, part, zl).wait_send()
-        await_bytes(tsend.at[pl.ds(k, n), :, pl.ds(0, 15)], t_send.at[b])
-        await_bytes(osend.at[pl.ds(k, n), pl.ds(0, 15)], o_send.at[b])
+        await_bytes(tsend.at[pl.ds(0, 15), pl.ds(k, n)], t_send.at[b])
+        await_bytes(osend.at[pl.ds(0, 15), pl.ds(k, n)], o_send.at[b])
     for u in range(8):
         if u < 2:
             ccopy(u, partner_row, row, y * 2 + hz).wait_send()
@@ -422,10 +423,10 @@
             pltpu.VMEM((2, 3, 8, 384, 256), BF),
             pltpu.VMEM((8, 256, 3072), BF),
             pltpu.VMEM((3, 3, 8, 128, 256), BF),
-            pltpu.VMEM((8, 3, 16, 16, 256), BF),
-            pltpu.VMEM((8, 3, 16, 16, 256), BF),
-            pltpu.VMEM((8, 16, 16, 256), BF),
-            pltpu.VMEM((8, 16, 16, 256), BF),
+            pltpu.VMEM((16, 8, 3, 16, 256), BF),
+            pltpu.VMEM((16, 8, 3, 16, 256), BF),
+            pltpu.VMEM((16, 8, 16, 256), BF),
+            pltpu.VMEM((16, 8, 16, 256), BF),
             pltpu.VMEM((8, 2, 128, 256), BF),
             pltpu.VMEM((8, 2, 128, 256), BF),
             pltpu.VMEM((2, 8, 128, 256), F32),

time: 99.5 us -> 99.5 us (level)
  no operation moved by 1% of the time
where the time goes in v13:
time: 99.5 us; the launch traced here: 97.6 us
  Pallas kernels  95.9 us (96%)
  local copies, waits for them, and re-layouts  1.67 us (2%)
    pallas_call x1, Pallas kernels, attention(): pl.pallas_call(attention_kernel, out_shape=pltpu.VMEM((4, 64, 3072), F32)...  95.9 us

profile of v13, /device:TPU:32, one launch (start us, length us, event | category | flops | bytes accessed | tf_op | source)
XLA Modules:
  0.0 97.6 jit_solution(5291017733275804955)
XLA Ops:
  0.0 95.9 %attention.1 = f32[4,64,3072]{2,1,0:T(8,128)S(1)} custom-call(s32[64]{0:T(128)} %clip_ref.1, f32[4,64,3072]{2,1,0:T(8,128)} %stream_hbm.1, f32[3,8,3072]{2,1,0:T(8,128)} %bitcast.7, bf16[3,8,384,256]{3,2,1,0:T(8,128)(2,1)} %bitcast.6, bf16[8,256,3072]{2,1,0:T(8,128)(2,1)} %bitcast.5), custom_call_target="tpu_custom_call" | custom-call | tf_op jit(solution)/shard_map/attention/pallas_call | solution.py:415
  95.9 1.7 %copy.7 = f32[4,64,3072]{2,1,0:T(8,128)} copy(f32[4,64,3072]{2,1,0:T(8,128)S(1)} %attention.1) | data formatting | bytes 6291456

commit v14 on v13

--- a/solution.py
+++ b/solution.py
@@ -28,7 +28,7 @@
     load_sem, y_send, y_recv, wz_send, wz_recv, wx_send, wx_recv, wc_send, wc_recv, z_send, z_recv,
     t_send, t_recv, o_send, o_recv, c_send, c_recv,
 ):
-    batches = ((0, 2), (2, 2), (4, 2), (6, 1), (7, 1))
+    batches = ((0, 2), (2, 2), (4, 2), (6, 2))
     tm = lax.axis_index("tm")
     row = lax.axis_index("row")
     zh = (tm // 2) % 2
@@ -43,7 +43,7 @@
     ym, yp, yq = (y + 3) % 4, (y + 1) % 4, (y + 2) % 4
     up, down = (tm, yp * 2 + zl), (tm, ym * 2 + zl)
     y_of = (y, y, ym, yp, ym, yp, yq, yq)
-    half_of = (0, 1, 0, 0, 1, 1, 0, 1)
+    half_of = (0, 1, 0, 1, 1, 0, 0, 1)
 
     def rcopy(src, dst, send, recv, dev):
         return pltpu.make_async_remote_copy(
@@ -117,17 +117,13 @@
             n = centred * lax.rsqrt(var + 1e-06) * scale + shift
             xg[unit, pl.ds(f * 32, 32), :] = n.astype(BF)
 
-    def ycopy(i, src, dst, half, dev):
-        if half is None:
-            return rcopy(xg.at[src], xg.at[dst], y_send.at[i], y_recv.at[i], dev)
-        rows = pl.ds(half * 64, 64)
-        return rcopy(xg.at[src, rows], xg.at[dst, rows], y_send.at[i], y_recv.at[i], dev)
+    def ycopy(i, src, dst, dev):
+        return rcopy(xg.at[src], xg.at[dst], y_send.at[i], y_recv.at[i], dev)
 
     y_copies = [
-        ycopy(0, 0, 2, None, up), ycopy(1, 0, 3, None, down),
-        ycopy(2, 1, 4, None, up), ycopy(3, 1, 5, None, down),
-        ycopy(4, 2, 6, 0, up), ycopy(5, 3, 6, 1, down),
-        ycopy(6, 4, 7, 0, up), ycopy(7, 5, 7, 1, down),
+        ycopy(0, 0, 2, up), ycopy(1, 1, 3, down),
+        ycopy(2, 1, 4, up), ycopy(3, 0, 5, down),
+        ycopy(4, 2, 6, up), ycopy(5, 3, 7, down),
     ]
     for unit in range(2):
         load_stream[unit].wait()
@@ -138,8 +134,9 @@
             for p in range(3):
                 for i in range(2):
                     wz_copy(p, i, zl).start()
-        y_copies[2 * unit].start()
-        y_copies[2 * unit + 1].start()
+        y_copies[unit].start()
+    y_copies[2].start()
+    y_copies[3].start()
 
     def unit_row(j):
         return (j & 128) + ((j >> 2) & 3) * 32 + ((j >> 4) & 7) * 4 + (j & 3)
@@ -271,9 +268,8 @@
                      (tm, r))
 
     def combine(u):
-        for zz in range(2):
-            back = dot(perm_t[:128, :128], orecv[zz * 8:(zz + 1) * 8, u].reshape(128, 256))
-            csend[u, zz] = (sp[zz, u] + back).astype(BF)
+        back = dot(perm_t[...], orecv[:, u].reshape(256, 256)).reshape(2, 128, 256)
+        csend[u] = (sp[:, u] + back).astype(BF)
         if u < 2:
             ccopy(u, partner_row, row, y * 2 + hz).start()
             comb[y * 2 + hz, u] = csend[u, zl]
@@ -343,29 +339,21 @@
     stage_own(1)
     stage_partner(0)
 
-    for i in range(2):
-        y_copies[2 + i].wait_recv()
-        y_copies[6 + i].start()
+    y_copies[2].wait_recv()
+    y_copies[3].wait_recv()
     project(2)
     stage_own(2)
     stage_partner(1)
     temporal(0)
+    stage_partner(2)
+    temporal(1)
 
     y_copies[4].wait_recv()
     y_copies[5].wait_recv()
     project(3)
     stage_own(3)
-    stage_partner(2)
-    temporal(1)
+    temporal(2)
     stage_partner(3)
-
-    y_copies[6].wait_recv()
-    y_copies[7].wait_recv()
-    project(4)
-    stage_own(4)
-    temporal(2)
-    stage_partner(4)
-    temporal(3)
 
     spatial(2, 4)
     wait_back(1)
@@ -374,14 +362,13 @@
     wait_back(2)
     combine(4)
     combine(5)
-    temporal(4)
+    temporal(3)
     spatial(6, 0)
-    wait_back(3)
-    combine(6)
     wait_back(0)
     combine(0)
     combine(1)
-    wait_back(4)
+    wait_back(3)
+    combine(6)
     combine(7)
     load_wo.wait()
     project_out((yp, ym), first=True)
@@ -434,13 +421,13 @@
             pltpu.VMEM((256, 256), BF),
             pltpu.VMEM((256, 256), F32),
             dma((4,)),
-            dma((8,)), dma((8,)),
+            dma((6,)), dma((6,)),
             dma((3, 2)), dma((3, 2)),
             dma((3, 2)), dma((3, 2)),
             dma((3, 2)), dma((3, 2)),
-            dma((5, 3)), dma((5, 3)),
-            dma((5,)), dma((5,)),
-            dma((5,)), dma((5,)),
+            dma((4, 3)), dma((4, 3)),
+            dma((4,)), dma((4,)),
+            dma((4,)), dma((4,)),
             dma((8, 2)), dma((8, 2)),
         ],
         compiler_params=pltpu.CompilerParams(

time: 99.5 us -> 102 us (1.025); the launches traced: 97.6 us -> 102 us
  Pallas kernels: 95.9 us -> 100 us
    pallas_call x1, Pallas kernels: 95.9 us -> 100 us  [attention(): pl.pallas_call(attention_kernel, out_shape=pltpu.VMEM((4, 64, 3072), F32)...]
where the time goes in v14:
time: 102 us
  Pallas kernels  100 us (98%)
  local copies, waits for them, and re-layouts  1.67 us (2%)
    pallas_call x1, Pallas kernels, attention(): pl.pallas_call(attention_kernel, out_shape=pltpu.VMEM((4, 64, 3072), F32)...  100 us

profile of v14, /device:TPU:32, one launch (start us, length us, event | category | flops | bytes accessed | tf_op | source)
XLA Modules:
  0.0 102.2 jit_solution(17790031244450147831)
XLA Ops:
  0.0 100.5 %attention.1 = f32[4,64,3072]{2,1,0:T(8,128)S(1)} custom-call(s32[64]{0:T(128)} %clip_ref.1, f32[4,64,3072]{2,1,0:T(8,128)} %stream_hbm.1, f32[3,8,3072]{2,1,0:T(8,128)} %bitcast.7, bf16[3,8,384,256]{3,2,1,0:T(8,128)(2,1)} %bitcast.6, bf16[8,256,3072]{2,1,0:T(8,128)(2,1)} %bitcast.5), custom_call_target="tpu_custom_call" | custom-call | tf_op jit(solution)/shard_map/attention/pallas_call | solution.py:402
  100.5 1.7 %copy.7 = f32[4,64,3072]{2,1,0:T(8,128)} copy(f32[4,64,3072]{2,1,0:T(8,128)S(1)} %attention.1) | data formatting | bytes 6291456

commit v15 on v14

--- a/solution.py
+++ b/solution.py
@@ -24,7 +24,7 @@
 
 def attention_kernel(
     clip_ref, stream_hbm, mod_ref, w_hbm, wo_hbm, out_ref,
-    stream_v, xg, wbuf, wo, qkv, tsend, trecv, osend, orecv, csend, comb, sp, perm, perm_t, mask,
+    stream_v, xg, wbuf, wo, qkv, tsend, trecv, osend, orecv, csend, comb, sp, total, perm, perm_t, mask,
     load_sem, y_send, y_recv, wz_send, wz_recv, wx_send, wx_recv, wc_send, wc_recv, z_send, z_recv,
     t_send, t_recv, o_send, o_recv, c_send, c_recv,
 ):
@@ -117,13 +117,17 @@
             n = centred * lax.rsqrt(var + 1e-06) * scale + shift
             xg[unit, pl.ds(f * 32, 32), :] = n.astype(BF)
 
-    def ycopy(i, src, dst, dev):
-        return rcopy(xg.at[src], xg.at[dst], y_send.at[i], y_recv.at[i], dev)
+    def ycopy(i, src, dst, dev, half=None):
+        if half is None:
+            return rcopy(xg.at[src], xg.at[dst], y_send.at[i], y_recv.at[i], dev)
+        cols = pl.ds(half * 1536, 1536)
+        return rcopy(xg.at[src, :, cols], xg.at[dst, :, cols], y_send.at[i], y_recv.at[i], dev)
 
     y_copies = [
         ycopy(0, 0, 2, up), ycopy(1, 1, 3, down),
         ycopy(2, 1, 4, up), ycopy(3, 0, 5, down),
-        ycopy(4, 2, 6, up), ycopy(5, 3, 7, down),
+        ycopy(4, 2, 6, up, 0), ycopy(5, 3, 7, down, 0),
+        ycopy(6, 2, 6, up, 1), ycopy(7, 3, 7, down, 1),
     ]
     for unit in range(2):
         load_stream[unit].wait()
@@ -154,13 +158,26 @@
     key = jnp.broadcast_to(key.astype(F32), (256, 256))
     mask[...] = jnp.where(key == key.T, 0.0, -1e30).astype(F32)
 
+    def slot_of(pz):
+        kk = (pz + hz) % 2
+        return kk * 2 + (1 - kk) * zl
+
     def project_part(b, pz, part):
         k, n = batches[b]
-        kk = (pz + hz) % 2
-        slot = kk * 2 + (1 - kk) * zl
         x = xg[k:k + n].reshape(n * 128, 3072)
         out = dot(x, wbuf[pz, part].reshape(3072, 256)).astype(BF)
-        qkv[slot, part, k:k + n] = out.reshape(n, 128, 256)
+        qkv[slot_of(pz), part, k:k + n] = out.reshape(n, 128, 256)
+
+    def far_first():
+        @pl.loop(0, 6)
+        def _(i):
+            w = wbuf[i // 3, i % 3, 0:4].reshape(1536, 256)
+            total[i // 3, i % 3] = dot(xg[6:8, :, 0:1536].reshape(256, 1536), w)
+
+    def far_part(pz, part):
+        w = wbuf[pz, part, 4:8].reshape(1536, 256)
+        out = total[pz, part] + dot(xg[6:8, :, 1536:3072].reshape(256, 1536), w)
+        qkv[slot_of(pz), part, 6:8] = out.astype(BF).reshape(2, 128, 256)
 
     def zcopy(b, part, slot):
         k, n = batches[b]
@@ -171,12 +188,12 @@
     def project(b):
         @pl.loop(0, 3)
         def _(part):
-            project_part(b, 1 - hz, part)
+            far_part(1 - hz, part) if b == 3 else project_part(b, 1 - hz, part)
             zcopy(b, part, zl).start()
 
         @pl.loop(0, 3)
         def _(part):
-            project_part(b, hz, part)
+            far_part(hz, part) if b == 3 else project_part(b, hz, part)
 
     def stage_part(b, zz, part):
         k, n = batches[b]
@@ -223,9 +240,10 @@
 
     factor = LOG2E / math.sqrt(HD)
 
-    def soften(s):
-        p = jnp.exp2((s - jnp.max(s, axis=-1, keepdims=True)) * factor)
-        return p, jnp.sum(p, axis=-1, keepdims=True)
+    def attend(s, v):
+        p = jnp.exp2((s - jnp.max(s, axis=-1, keepdims=True)) * factor).astype(BF)
+        out = dot(p, jnp.concatenate([v, jnp.ones(v.shape, BF)], axis=1))
+        return out[:, :HD] / out[:, HD:]
 
     def temporal(b):
         k, n = batches[b]
@@ -235,8 +253,7 @@
             for h in range(2):
                 cols = slice(h * HD, (h + 1) * HD)
                 q, kk, v = (trecv[:, u, part, :, cols].reshape(256, HD) for part in range(3))
-                p, total = soften(dot_nt(q, kk) + mask[...])
-                o = dot(p.astype(BF), v) / total
+                o = attend(dot_nt(q, kk) + mask[...], v)
                 osend[:, u, :, cols] = o.astype(BF).reshape(16, 16, HD)
         orecv[me_at, k:k + n] = osend[tm, k:k + n]
         for o in offsets:
@@ -257,8 +274,7 @@
                     q = jnp.concatenate(
                         [qkv[0:2, 0, k:k + 2, rows, cols].reshape(128, HD) for k in (ka, kb)], axis=0)
                     kk, v = (qkv[0:2, part, :, rows, cols].reshape(512, HD) for part in (1, 2))
-                    p, total = soften(dot_nt(q, kk))
-                    o = (dot(p.astype(BF), v) / total).reshape(2, 2, 2, 32, HD)
+                    o = attend(dot_nt(q, kk), v).reshape(2, 2, 2, 32, HD)
                     sp[:, ka:ka + 2, rows, cols] = o[0]
                     sp[:, kb:kb + 2, rows, cols] = o[1]
 
@@ -336,6 +352,8 @@
         y_copies[4 + i].start()
     stage_own(0)
     project(1)
+    y_copies[6].start()
+    y_copies[7].start()
     stage_own(1)
     stage_partner(0)
 
@@ -346,10 +364,13 @@
     stage_partner(1)
     temporal(0)
     stage_partner(2)
-    temporal(1)
-
     y_copies[4].wait_recv()
     y_copies[5].wait_recv()
+    far_first()
+    temporal(1)
+
+    y_copies[6].wait_recv()
+    y_copies[7].wait_recv()
     project(3)
     stage_own(3)
     temporal(2)
@@ -417,11 +438,12 @@
             pltpu.VMEM((8, 2, 128, 256), BF),
             pltpu.VMEM((8, 2, 128, 256), BF),
             pltpu.VMEM((2, 8, 128, 256), F32),
+            pltpu.VMEM((2, 3, 256, 256), F32),
             pltpu.VMEM((256, 256), BF),
             pltpu.VMEM((256, 256), BF),
             pltpu.VMEM((256, 256), F32),
             dma((4,)),
-            dma((6,)), dma((6,)),
+            dma((8,)), dma((8,)),
             dma((3, 2)), dma((3, 2)),
             dma((3, 2)), dma((3, 2)),
             dma((3, 2)), dma((3, 2)),

time: 102 us -> 101 us (level)
  no operation moved by 1% of the time
where the time goes in v15:
time: 101 us
  Pallas kernels  99.6 us (99%)
  local copies, waits for them, and re-layouts  1.67 us (2%)
    pallas_call x1, Pallas kernels, attention(): pl.pallas_call(attention_kernel, out_shape=pltpu.VMEM((4, 64, 3072), F32)...  99.6 us

profile of v15, /device:TPU:32, one launch (start us, length us, event | category | flops | bytes accessed | tf_op | source)
XLA Modules:
  0.0 101.3 jit_solution(13551081068840767868)
XLA Ops:
  0.0 99.6 %attention.1 = f32[4,64,3072]{2,1,0:T(8,128)S(1)} custom-call(s32[64]{0:T(128)} %clip_ref.1, f32[4,64,3072]{2,1,0:T(8,128)} %stream_hbm.1, f32[3,8,3072]{2,1,0:T(8,128)} %bitcast.7, bf16[3,8,384,256]{3,2,1,0:T(8,128)(2,1)} %bitcast.6, bf16[8,256,3072]{2,1,0:T(8,128)(2,1)} %bitcast.5), custom_call_target="tpu_custom_call" | custom-call | tf_op jit(solution)/shard_map/attention/pallas_call | solution.py:423
  99.7 1.7 %copy.7 = f32[4,64,3072]{2,1,0:T(8,128)} copy(f32[4,64,3072]{2,1,0:T(8,128)S(1)} %attention.1) | data formatting | bytes 6291456

commit v16 on v13

--- a/solution.py
+++ b/solution.py
@@ -226,9 +226,10 @@
 
     factor = LOG2E / math.sqrt(HD)
 
-    def soften(s):
-        p = jnp.exp2((s - jnp.max(s, axis=-1, keepdims=True)) * factor)
-        return p, jnp.sum(p, axis=-1, keepdims=True)
+    def attend(s, v):
+        p = jnp.exp2((s - jnp.max(s, axis=-1, keepdims=True)) * factor).astype(BF)
+        out = dot(p, jnp.concatenate([v, jnp.ones(v.shape, BF)], axis=1))
+        return out[:, :HD] / out[:, HD:]
 
     def temporal(b):
         k, n = batches[b]
@@ -238,8 +239,7 @@
             for h in range(2):
                 cols = slice(h * HD, (h + 1) * HD)
                 q, kk, v = (trecv[:, u, part, :, cols].reshape(256, HD) for part in range(3))
-                p, total = soften(dot_nt(q, kk) + mask[...])
-                o = dot(p.astype(BF), v) / total
+                o = attend(dot_nt(q, kk) + mask[...], v)
                 osend[:, u, :, cols] = o.astype(BF).reshape(16, 16, HD)
         orecv[me_at, k:k + n] = osend[tm, k:k + n]
         for o in offsets:
@@ -250,36 +250,33 @@
         k, n = batches[b]
         await_bytes(orecv.at[pl.ds(0, 15), pl.ds(k, n)], o_recv.at[b])
 
-    def spatial(ka, kb):
+    def spatial(k):
         @pl.loop(0, 2)
         def _(pair):
             for f in range(2):
                 rows = pl.ds(pl.multiple_of(pair * 64 + f * 32, 32), 32)
                 for h in range(2):
                     cols = slice(h * HD, (h + 1) * HD)
-                    q = jnp.concatenate(
-                        [qkv[0:2, 0, k:k + 2, rows, cols].reshape(128, HD) for k in (ka, kb)], axis=0)
+                    q = qkv[0:2, 0, k:k + 2, rows, cols].reshape(128, HD)
                     kk, v = (qkv[0:2, part, :, rows, cols].reshape(512, HD) for part in (1, 2))
-                    p, total = soften(dot_nt(q, kk))
-                    o = (dot(p.astype(BF), v) / total).reshape(2, 2, 2, 32, HD)
-                    sp[:, ka:ka + 2, rows, cols] = o[0]
-                    sp[:, kb:kb + 2, rows, cols] = o[1]
+                    sp[:, k:k + 2, rows, cols] = attend(dot_nt(q, kk), v).reshape(2, 2, 32, HD)
 
     def ccopy(u, r, at, kept):
         half = half_of[u]
         return rcopy(csend.at[u, r % 2], comb.at[kept, half], c_send.at[u, r % 2], c_recv.at[at, half],
                      (tm, r))
 
-    def combine(u):
-        for zz in range(2):
-            back = dot(perm_t[:128, :128], orecv[zz * 8:(zz + 1) * 8, u].reshape(128, 256))
-            csend[u, zz] = (sp[zz, u] + back).astype(BF)
-        if u < 2:
-            ccopy(u, partner_row, row, y * 2 + hz).start()
-            comb[y * 2 + hz, u] = csend[u, zl]
-        else:
-            for zz in range(2):
-                ccopy(u, y_of[u] * 2 + zz, row, y * 2 + hz).start()
+    def combine(*units):
+        for u in units:
+            back = dot(perm_t[...], orecv[:, u].reshape(256, 256)).reshape(2, 128, 256)
+            csend[u] = (sp[:, u] + back).astype(BF)
+        for u in units:
+            if u < 2:
+                ccopy(u, partner_row, row, y * 2 + hz).start()
+                comb[y * 2 + hz, u] = csend[u, zl]
+            else:
+                for zz in range(2):
+                    ccopy(u, y_of[u] * 2 + zz, row, y * 2 + hz).start()
 
     def project_out(pair, first, last=True):
         for ys in pair:
@@ -364,23 +361,22 @@
     project(4)
     stage_own(4)
     temporal(2)
+    temporal(3)
     stage_partner(4)
-    temporal(3)
-
-    spatial(2, 4)
+
+    spatial(2)
     wait_back(1)
-    combine(2)
-    combine(3)
+    combine(2, 3)
+    spatial(4)
     wait_back(2)
-    combine(4)
-    combine(5)
+    combine(4, 5)
     temporal(4)
-    spatial(6, 0)
+    spatial(6)
     wait_back(3)
     combine(6)
+    spatial(0)
     wait_back(0)
-    combine(0)
-    combine(1)
+    combine(0, 1)
     wait_back(4)
     combine(7)
     load_wo.wait()

time: 99.5 us -> 99.1 us (level); the launches traced: 97.6 us -> 98.9 us
  Pallas kernels: 95.9 us -> 97.3 us
    pallas_call x1, Pallas kernels: 95.9 us -> 97.3 us  [attention(): pl.pallas_call(attention_kernel, out_shape=pltpu.VMEM((4, 64, 3072), F32)...]
where the time goes in v16:
time: 99.1 us; the launch traced here: 98.9 us
  Pallas kernels  97.3 us (98%)
  local copies, waits for them, and re-layouts  1.67 us (2%)
    pallas_call x1, Pallas kernels, attention(): pl.pallas_call(attention_kernel, out_shape=pltpu.VMEM((4, 64, 3072), F32)...  97.3 us

profile of v16, /device:TPU:32, one launch (start us, length us, event | category | flops | bytes accessed | tf_op | source)
XLA Modules:
  0.0 98.9 jit_solution(1410316713446203409)
XLA Ops:
  0.0 97.3 %attention.1 = f32[4,64,3072]{2,1,0:T(8,128)S(1)} custom-call(s32[64]{0:T(128)} %clip_ref.1, f32[4,64,3072]{2,1,0:T(8,128)} %stream_hbm.1, f32[3,8,3072]{2,1,0:T(8,128)} %bitcast.7, bf16[3,8,384,256]{3,2,1,0:T(8,128)(2,1)} %bitcast.6, bf16[8,256,3072]{2,1,0:T(8,128)(2,1)} %bitcast.5), custom_call_target="tpu_custom_call" | custom-call | tf_op jit(solution)/shard_map/attention/pallas_call | solution.py:411
  97.3 1.7 %copy.7 = f32[4,64,3072]{2,1,0:T(8,128)} copy(f32[4,64,3072]{2,1,0:T(8,128)S(1)} %attention.1) | data formatting | bytes 6291456

commit v17 on v16

--- a/solution.py
+++ b/solution.py
@@ -317,6 +317,13 @@
             wx_copy(p, i, e_own).start()
         wc_copy(p, 0, e_own).start()
         project_part(0, zl, p)
+    def hand_over(p):
+        zcopy(0, p, zl).start()
+
+    pl.when(zh == 0)(lambda: stage_own(0))
+    for p in range(3):
+        pl.when(zh == 1)(lambda p=p: hand_over(p))
+
     def pass_x(p):
         for i in range(2):
             wx_copy(p, i, e_x).wait_recv()
@@ -328,14 +335,14 @@
         for j in range(2):
             wc_copy(p, j, e_cores[j]).wait_recv()
         project_part(0, oz, p)
-        zcopy(0, p, zl).start()
+        pl.when(zh == 0)(lambda p=p: hand_over(p))
         if p == 0:
             pass_x(2)
     load_wo.start()
     for i in range(2):
         y_copies[i].wait_recv()
         y_copies[4 + i].start()
-    stage_own(0)
+    pl.when(zh == 1)(lambda: stage_own(0))
     project(1)
     stage_own(1)
     stage_partner(0)

time: 99.1 us -> 99.1 us (level)
  no operation moved by 1% of the time
where the time goes in v17:
time: 99.1 us; the launch traced here: 98.9 us
  Pallas kernels  97.3 us (98%)
  local copies, waits for them, and re-layouts  1.67 us (2%)
    pallas_call x1, Pallas kernels, attention(): pl.pallas_call(attention_kernel, out_shape=pltpu.VMEM((4, 64, 3072), F32)...  97.3 us

profile of v17, /device:TPU:32, one launch (start us, length us, event | category | flops | bytes accessed | tf_op | source)
XLA Modules:
  0.0 98.9 jit_solution(12633864713523139925)
XLA Ops:
  0.0 97.3 %attention.1 = f32[4,64,3072]{2,1,0:T(8,128)S(1)} custom-call(s32[64]{0:T(128)} %clip_ref.1, f32[4,64,3072]{2,1,0:T(8,128)} %stream_hbm.1, f32[3,8,3072]{2,1,0:T(8,128)} %bitcast.7, bf16[3,8,384,256]{3,2,1,0:T(8,128)(2,1)} %bitcast.6, bf16[8,256,3072]{2,1,0:T(8,128)(2,1)} %bitcast.5), custom_call_target="tpu_custom_call" | custom-call | tf_op jit(solution)/shard_map/attention/pallas_call | solution.py:418
  97.3 1.7 %copy.7 = f32[4,64,3072]{2,1,0:T(8,128)} copy(f32[4,64,3072]{2,1,0:T(8,128)S(1)} %attention.1) | data formatting | bytes 6291456

commit v18 on v16

--- a/solution.py
+++ b/solution.py
@@ -172,14 +172,19 @@
                      z_recv.at[b, part], (tm, partner_row))
 
     def project(b):
-        @pl.loop(0, 3)
-        def _(part):
+        def sent(part):
             project_part(b, 1 - hz, part)
             zcopy(b, part, zl).start()
 
-        @pl.loop(0, 3)
-        def _(part):
+        def kept(part):
             project_part(b, hz, part)
+
+        for step in (sent, kept):
+            if b == 4:
+                for part in range(3):
+                    step(part)
+            else:
+                pl.loop(0, 3)(step)
 
     def stage_part(b, zz, part):
         k, n = batches[b]
@@ -250,16 +255,19 @@
         k, n = batches[b]
         await_bytes(orecv.at[pl.ds(0, 15), pl.ds(k, n)], o_recv.at[b])
 
-    def spatial(k):
+    def spatial(ka, kb):
         @pl.loop(0, 2)
         def _(pair):
             for f in range(2):
                 rows = pl.ds(pl.multiple_of(pair * 64 + f * 32, 32), 32)
                 for h in range(2):
                     cols = slice(h * HD, (h + 1) * HD)
-                    q = qkv[0:2, 0, k:k + 2, rows, cols].reshape(128, HD)
+                    q = jnp.concatenate(
+                        [qkv[0:2, 0, k:k + 2, rows, cols].reshape(128, HD) for k in (ka, kb)], axis=0)
                     kk, v = (qkv[0:2, part, :, rows, cols].reshape(512, HD) for part in (1, 2))
-                    sp[:, k:k + 2, rows, cols] = attend(dot_nt(q, kk), v).reshape(2, 2, 32, HD)
+                    o = attend(dot_nt(q, kk), v).reshape(2, 2, 2, 32, HD)
+                    sp[:, ka:ka + 2, rows, cols] = o[0]
+                    sp[:, kb:kb + 2, rows, cols] = o[1]
 
     def ccopy(u, r, at, kept):
         half = half_of[u]
@@ -278,7 +286,7 @@
                 for zz in range(2):
                     ccopy(u, y_of[u] * 2 + zz, row, y * 2 + hz).start()
 
-    def project_out(pair, first, last=True):
+    def project_out(pair, first):
         for ys in pair:
             for i in range(2):
                 r = ys * 2 + i
@@ -291,10 +299,9 @@
                     else:
                         wait()
 
-        @pl.loop(0, 6)
-        def _(n):
-            cols = pl.ds(pl.multiple_of(n * 512, 512), 512)
-            heads = [2 * ys + i for ys in pair for i in range(2)]
+        heads = [2 * ys + i for ys in pair for i in range(2)]
+
+        def tile(cols):
             left = jnp.concatenate([comb[h].reshape(256, 256) for h in heads], axis=1)
             right = jnp.concatenate([wo[h, :, cols] for h in heads], axis=0)
             acc = dot(left, right)
@@ -304,11 +311,14 @@
                     rows = slice(half * 32, (half + 1) * 32)
                     piece = acc[at:at + 32]
                     if not first:
-                        piece = piece + out_ref[f, rows, cols]
-                    if not first and last:
                         clip = clip_ref[tm * 4 + f]
-                        piece = piece * mod_ref[2, pl.ds(clip, 1), cols]
+                        piece = (piece + out_ref[f, rows, cols]) * mod_ref[2, pl.ds(clip, 1), cols]
                     out_ref[f, rows, cols] = piece
+
+        @pl.loop(0, 3)
+        def _(n):
+            for i in range(2):
+                tile(pl.ds(pl.multiple_of(n * 1024 + i * 512, 512), 512))
 
     load_w.wait()
     for p in range(3):
@@ -364,25 +374,21 @@
     temporal(3)
     stage_partner(4)
 
-    spatial(2)
+    spatial(2, 4)
     wait_back(1)
     combine(2, 3)
-    spatial(4)
     wait_back(2)
     combine(4, 5)
     temporal(4)
-    spatial(6)
+    spatial(6, 0)
     wait_back(3)
-    combine(6)
-    spatial(0)
     wait_back(0)
-    combine(0, 1)
+    combine(6, 0, 1)
     wait_back(4)
     combine(7)
     load_wo.wait()
     project_out((yp, ym), first=True)
-    project_out((y,), first=False, last=False)
-    project_out((yq,), first=False)
+    project_out((y, yq), first=False)
 
     for p in range(3):
         for i in range(2):

time: 99.1 us -> 98.2 us (level)
  no operation moved by 1% of the time
where the time goes in v18:
time: 98.2 us; the launch traced here: 98.1 us
  Pallas kernels  96.4 us (98%)
  local copies, waits for them, and re-layouts  1.67 us (2%)
    pallas_call x1, Pallas kernels, attention(): pl.pallas_call(attention_kernel, out_shape=pltpu.VMEM((4, 64, 3072), F32)...  96.4 us

profile of v18, /device:TPU:32, one launch (start us, length us, event | category | flops | bytes accessed | tf_op | source)
XLA Modules:
  0.0 98.1 jit_solution(17513343530385963162)
XLA Ops:
  0.0 96.4 %attention.1 = f32[4,64,3072]{2,1,0:T(8,128)S(1)} custom-call(s32[64]{0:T(128)} %clip_ref.1, f32[4,64,3072]{2,1,0:T(8,128)} %stream_hbm.1, f32[3,8,3072]{2,1,0:T(8,128)} %bitcast.7, bf16[3,8,384,256]{3,2,1,0:T(8,128)(2,1)} %bitcast.6, bf16[8,256,3072]{2,1,0:T(8,128)(2,1)} %bitcast.5), custom_call_target="tpu_custom_call" | custom-call | tf_op jit(solution)/shard_map/attention/pallas_call | solution.py:417
  96.4 1.7 %copy.7 = f32[4,64,3072]{2,1,0:T(8,128)} copy(f32[4,64,3072]{2,1,0:T(8,128)S(1)} %attention.1) | data formatting | bytes 6291456

commit v19 on v18

--- a/solution.py
+++ b/solution.py
@@ -138,8 +138,9 @@
             for p in range(3):
                 for i in range(2):
                     wz_copy(p, i, zl).start()
-        y_copies[2 * unit].start()
-        y_copies[2 * unit + 1].start()
+        if unit == 0:
+            y_copies[0].start()
+            y_copies[1].start()
 
     def unit_row(j):
         return (j & 128) + ((j >> 2) & 3) * 32 + ((j >> 4) & 7) * 4 + (j & 3)
@@ -327,6 +328,9 @@
             wx_copy(p, i, e_own).start()
         wc_copy(p, 0, e_own).start()
         project_part(0, zl, p)
+    y_copies[2].start()
+    y_copies[3].start()
+
     def pass_x(p):
         for i in range(2):
             wx_copy(p, i, e_x).wait_recv()
@@ -344,7 +348,6 @@
     load_wo.start()
     for i in range(2):
         y_copies[i].wait_recv()
-        y_copies[4 + i].start()
     stage_own(0)
     project(1)
     stage_own(1)
@@ -352,8 +355,10 @@
 
     for i in range(2):
         y_copies[2 + i].wait_recv()
+        y_copies[4 + i].start()
+    project(2)
+    for i in range(2):
         y_copies[6 + i].start()
-    project(2)
     stage_own(2)
     stage_partner(1)
     temporal(0)

time: 98.2 us -> 98.2 us (level)
  no operation moved by 1% of the time
where the time goes in v19:
time: 98.2 us; the launch traced here: 98 us
  Pallas kernels  96.3 us (98%)
  local copies, waits for them, and re-layouts  1.67 us (2%)
    pallas_call x1, Pallas kernels, attention(): pl.pallas_call(attention_kernel, out_shape=pltpu.VMEM((4, 64, 3072), F32)...  96.3 us

profile of v19, /device:TPU:32, one launch (start us, length us, event | category | flops | bytes accessed | tf_op | source)
XLA Modules:
  0.0 98.0 jit_solution(17185100702624431130)
XLA Ops:
  0.0 96.3 %attention.1 = f32[4,64,3072]{2,1,0:T(8,128)S(1)} custom-call(s32[64]{0:T(128)} %clip_ref.1, f32[4,64,3072]{2,1,0:T(8,128)} %stream_hbm.1, f32[3,8,3072]{2,1,0:T(8,128)} %bitcast.7, bf16[3,8,384,256]{3,2,1,0:T(8,128)(2,1)} %bitcast.6, bf16[8,256,3072]{2,1,0:T(8,128)(2,1)} %bitcast.5), custom_call_target="tpu_custom_call" | custom-call | tf_op jit(solution)/shard_map/attention/pallas_call | solution.py:422
  96.3 1.7 %copy.7 = f32[4,64,3072]{2,1,0:T(8,128)} copy(f32[4,64,3072]{2,1,0:T(8,128)S(1)} %attention.1) | data formatting | bytes 6291456

commit v20 on v19

--- a/solution.py
+++ b/solution.py
@@ -173,19 +173,15 @@
                      z_recv.at[b, part], (tm, partner_row))
 
     def project(b):
-        def sent(part):
+        for part in range(3):
             project_part(b, 1 - hz, part)
-            zcopy(b, part, zl).start()
-
-        def kept(part):
+            if b == 4:
+                zcopy(b, part, zl).start()
+        if b < 4:
+            for part in range(3):
+                zcopy(b, part, zl).start()
+        for part in range(3):
             project_part(b, hz, part)
-
-        for step in (sent, kept):
-            if b == 4:
-                for part in range(3):
-                    step(part)
-            else:
-                pl.loop(0, 3)(step)
 
     def stage_part(b, zz, part):
         k, n = batches[b]
@@ -216,18 +212,15 @@
                     send()
 
     def stage_own(b):
-        @pl.loop(0, 3)
-        def _(part):
+        for part in range(3):
             stage_part(b, zl, part)
-
         send_time(b, zl)
 
     def stage_partner(b):
-        @pl.loop(0, 3)
-        def _(part):
+        for part in range(3):
             zcopy(b, part, oz).wait_recv()
+        for part in range(3):
             stage_part(b, oz, part)
-
         send_time(b, oz)
 
     factor = LOG2E / math.sqrt(HD)

time: 98.2 us -> 98 us (level)
  no operation moved by 1% of the time
where the time goes in v20:
time: 98 us; the launch traced here: 97.8 us
  Pallas kernels  96.1 us (98%)
  local copies, waits for them, and re-layouts  1.67 us (2%)
    pallas_call x1, Pallas kernels, attention(): pl.pallas_call(attention_kernel, out_shape=pltpu.VMEM((4, 64, 3072), F32)...  96.1 us

profile of v20, /device:TPU:32, one launch (start us, length us, event | category | flops | bytes accessed | tf_op | source)
XLA Modules:
  0.0 97.8 jit_solution(17212324596426076082)
XLA Ops:
  0.0 96.1 %attention.1 = f32[4,64,3072]{2,1,0:T(8,128)S(1)} custom-call(s32[64]{0:T(128)} %clip_ref.1, f32[4,64,3072]{2,1,0:T(8,128)} %stream_hbm.1, f32[3,8,3072]{2,1,0:T(8,128)} %bitcast.7, bf16[3,8,384,256]{3,2,1,0:T(8,128)(2,1)} %bitcast.6, bf16[8,256,3072]{2,1,0:T(8,128)(2,1)} %bitcast.5), custom_call_target="tpu_custom_call" | custom-call | tf_op jit(solution)/shard_map/attention/pallas_call | solution.py:415
  96.2 1.7 %copy.7 = f32[4,64,3072]{2,1,0:T(8,128)} copy(f32[4,64,3072]{2,1,0:T(8,128)S(1)} %attention.1) | data formatting | bytes 6291456

commit v21 on v19

--- a/solution.py
+++ b/solution.py
@@ -133,14 +133,14 @@
         load_stream[unit].wait()
         norm(unit)
         if unit == 0:
+            load_w.start()
+            load_wo.start()
             pl.semaphore_wait(barrier, 22)
-            load_w.start()
+            y_copies[0].start()
+            y_copies[1].start()
             for p in range(3):
                 for i in range(2):
                     wz_copy(p, i, zl).start()
-        if unit == 0:
-            y_copies[0].start()
-            y_copies[1].start()
 
     def unit_row(j):
         return (j & 128) + ((j >> 2) & 3) * 32 + ((j >> 4) & 7) * 4 + (j & 3)
@@ -345,7 +345,6 @@
         zcopy(0, p, zl).start()
         if p == 0:
             pass_x(2)
-    load_wo.start()
     for i in range(2):
         y_copies[i].wait_recv()
     stage_own(0)

time: 98.2 us -> 98.1 us (level)
  no operation moved by 1% of the time
where the time goes in v21:
time: 98.1 us; the launch traced here: 98 us
  Pallas kernels  96.3 us (98%)
  local copies, waits for them, and re-layouts  1.67 us (2%)
    pallas_call x1, Pallas kernels, attention(): pl.pallas_call(attention_kernel, out_shape=pltpu.VMEM((4, 64, 3072), F32)...  96.3 us

profile of v21, /device:TPU:32, one launch (start us, length us, event | category | flops | bytes accessed | tf_op | source)
XLA Modules:
  0.0 98.0 jit_solution(4937107316604483099)
XLA Ops:
  0.0 96.3 %attention.1 = f32[4,64,3072]{2,1,0:T(8,128)S(1)} custom-call(s32[64]{0:T(128)} %clip_ref.1, f32[4,64,3072]{2,1,0:T(8,128)} %stream_hbm.1, f32[3,8,3072]{2,1,0:T(8,128)} %bitcast.7, bf16[3,8,384,256]{3,2,1,0:T(8,128)(2,1)} %bitcast.6, bf16[8,256,3072]{2,1,0:T(8,128)(2,1)} %bitcast.5), custom_call_target="tpu_custom_call" | custom-call | tf_op jit(solution)/shard_map/attention/pallas_call | solution.py:421
  96.3 1.7 %copy.7 = f32[4,64,3072]{2,1,0:T(8,128)} copy(f32[4,64,3072]{2,1,0:T(8,128)S(1)} %attention.1) | data formatting | bytes 6291456

commit v22 on v19

--- a/solution.py
+++ b/solution.py
@@ -59,7 +59,7 @@
     zs = [zh, 1 - zh]
     cs = [core, 1 - core]
     rows_of = [y * 2 + (hz + zh) % 2, y * 2 + (hz + 1 - zh) % 2]
-    offsets = [(dx, dz, dc) for dx in (1, 3, 2, 0) for dz in range(2) for dc in range(2)][:-4]
+    offsets = [(dx, dz, dc) for dx in (2, 1, 3, 0) for dz in range(2) for dc in range(2)][:-4]
     offsets = offsets + [(0, 1, 0), (0, 1, 1), (0, 0, 1)]
     me_at = core * 8 + x * 2 + zh
 
@@ -197,7 +197,7 @@
     def send_time(b, zz):
         k, n = batches[b]
         units = pl.ds(k, n)
-        for dx in (1, 3, 2, 0):
+        for dx in (2, 1, 3, 0):
             for dz in (1, 0):
                 t = xs[dx] * 4 + zs[dz] * 2 + zz
                 at = zz * 8 + xs[dx] * 2 + zs[dz]

time: 98.2 us -> 97.7 us (level)
  no operation moved by 1% of the time
where the time goes in v22:
time: 97.7 us; the launch traced here: 97.5 us
  Pallas kernels  95.9 us (98%)
  local copies, waits for them, and re-layouts  1.67 us (2%)
    pallas_call x1, Pallas kernels, attention(): pl.pallas_call(attention_kernel, out_shape=pltpu.VMEM((4, 64, 3072), F32)...  95.9 us

profile of v22, /device:TPU:32, one launch (start us, length us, event | category | flops | bytes accessed | tf_op | source)
XLA Modules:
  0.0 97.5 jit_solution(4680216440897348700)
XLA Ops:
  0.0 95.9 %attention.1 = f32[4,64,3072]{2,1,0:T(8,128)S(1)} custom-call(s32[64]{0:T(128)} %clip_ref.1, f32[4,64,3072]{2,1,0:T(8,128)} %stream_hbm.1, f32[3,8,3072]{2,1,0:T(8,128)} %bitcast.7, bf16[3,8,384,256]{3,2,1,0:T(8,128)(2,1)} %bitcast.6, bf16[8,256,3072]{2,1,0:T(8,128)(2,1)} %bitcast.5), custom_call_target="tpu_custom_call" | custom-call | tf_op jit(solution)/shard_map/attention/pallas_call | solution.py:422
  95.9 1.7 %copy.7 = f32[4,64,3072]{2,1,0:T(8,128)} copy(f32[4,64,3072]{2,1,0:T(8,128)S(1)} %attention.1) | data formatting | bytes 6291456

commit v23 on v22

--- a/solution.py
+++ b/solution.py
@@ -376,8 +376,8 @@
     project(4)
     stage_own(4)
     temporal(2)
+    stage_partner(4)
     temporal(3)
-    stage_partner(4)
 
     spatial(2, 4)
     wait_back(1)

time: 97.7 us -> 97.1 us (level)
  no operation moved by 1% of the time
where the time goes in v23:
time: 97.1 us; the launch traced here: 96.9 us
  Pallas kernels  95.2 us (98%)
  local copies, waits for them, and re-layouts  1.67 us (2%)
    pallas_call x1, Pallas kernels, attention(): pl.pallas_call(attention_kernel, out_shape=pltpu.VMEM((4, 64, 3072), F32)...  95.2 us

profile of v23, /device:TPU:32, one launch (start us, length us, event | category | flops | bytes accessed | tf_op | source)
XLA Modules:
  0.0 96.9 jit_solution(7728315576142045291)
XLA Ops:
  0.0 95.2 %attention.1 = f32[4,64,3072]{2,1,0:T(8,128)S(1)} custom-call(s32[64]{0:T(128)} %clip_ref.1, f32[4,64,3072]{2,1,0:T(8,128)} %stream_hbm.1, f32[3,8,3072]{2,1,0:T(8,128)} %bitcast.7, bf16[3,8,384,256]{3,2,1,0:T(8,128)(2,1)} %bitcast.6, bf16[8,256,3072]{2,1,0:T(8,128)(2,1)} %bitcast.5), custom_call_target="tpu_custom_call" | custom-call | tf_op jit(solution)/shard_map/attention/pallas_call | solution.py:422
  95.2 1.7 %copy.7 = f32[4,64,3072]{2,1,0:T(8,128)} copy(f32[4,64,3072]{2,1,0:T(8,128)S(1)} %attention.1) | data formatting | bytes 6291456
